TPU v7x, 256 devices: a whole 4x4x8 slice. The times are simulated.
256 devices in a mesh: space: 16 (over x_hi, y, core), band: 16 (over x_lo, z).
Axes of the slice: x: 4 (x_hi: 2, x_lo: 2; x = x_hi * 2 + x_lo), y: 4, z: 8, core: 2. Of those that a mesh axis runs over, the one named last changes fastest.
Arguments:
- orbitals: float32 [384, 64, 4608], P('band', 'space'), may hold values from -6 to 6
- potential: float32 [64, 4608], P('space'), may hold values from -2 to 0
- rotation: bfloat16 [384, 384], replicated, may hold values from -0.3125 to 0.3125
Outputs:
- rotated: float32 [384, 64, 4608], P('band', 'space')
All inputs are finite; a program needn't handle non-finite values.
Results may differ from a plain program's by a relative error of at most 0.0029.
Values may be sent and summed in bfloat16 or wider, within the bound.
No kernel may reach another device: no remote copies, remote signals or barrier semaphores. Data moves between devices by JAX's collectives and lax.ppermute only.
A program may use at most 128 MiB of HBM per device.

v0:
```python
import jax
import jax.numpy as jnp
from jax import lax
from jax.sharding import PartitionSpec as P

NZ = 96
DEGREE = 4


center_value = 4.75
half_width = 3.75


def with_halo(cells, sides, width):
    for axis, dim in sides:
        count = lax.axis_size(axis)
        ends = count - 1
        head = lax.slice_in_dim(cells, 0, width, axis=dim)
        tail = lax.slice_in_dim(cells, cells.shape[dim] - width, cells.shape[dim], axis=dim)
        cells = jnp.concatenate(
            [
                lax.ppermute(tail, axis, [(i, (i + 1) % count) for i in range(ends)]),
                cells,
                lax.ppermute(head, axis, [((i + 1) % count, i) for i in range(ends)]),
            ],
            axis=dim,
        )
    return cells


def apply_hamiltonian(padded, potential):
    center = padded[:, 2:-2]
    planes = center.shape[1]
    columns = center.shape[2]
    laplace = -7.5 * center
    laplace = laplace + 4.0 / 3.0 * (padded[:, 1 : planes + 1] + padded[:, 3 : planes + 3])
    laplace = laplace - 1.0 / 12.0 * (padded[:, 0:planes] + padded[:, 4 : planes + 4])
    shifted_y = jnp.pad(center, ((0, 0), (0, 0), (2 * NZ, 2 * NZ)))
    laplace = laplace + 4.0 / 3.0 * (
        shifted_y[:, :, NZ : NZ + columns] + shifted_y[:, :, 3 * NZ : 3 * NZ + columns]
    )
    laplace = laplace - 1.0 / 12.0 * (
        shifted_y[:, :, 0:columns] + shifted_y[:, :, 4 * NZ : 4 * NZ + columns]
    )
    z_index = jnp.arange(columns) % NZ
    shifted_z = jnp.pad(center, ((0, 0), (0, 0), (2, 2)))
    minus_one = shifted_z[:, :, 1 : columns + 1] * jnp.where(z_index >= 1, 1.0, 0.0)
    plus_one = shifted_z[:, :, 3 : columns + 3] * jnp.where(z_index <= NZ - 2, 1.0, 0.0)
    minus_two = shifted_z[:, :, 0:columns] * jnp.where(z_index >= 2, 1.0, 0.0)
    plus_two = shifted_z[:, :, 4 : columns + 4] * jnp.where(z_index <= NZ - 3, 1.0, 0.0)
    laplace = laplace + 4.0 / 3.0 * (minus_one + plus_one) - 1.0 / 12.0 * (minus_two + plus_two)
    return -0.5 * laplace + potential * center


def step_once(current, potential):
    padded = with_halo(current, (("space", 1),), 2)
    return apply_hamiltonian(padded, potential) - center_value * current


def body(orbitals, potential, rotation):
    previous = orbitals
    current = step_once(orbitals, potential) / half_width
    for degree in range(DEGREE - 1):
        following = 2.0 / half_width * step_once(current, potential) - previous
        previous = current
        current = following
    filtered = current.astype(jnp.bfloat16)
    local_count = filtered.shape[0]
    planes = filtered.shape[1]
    columns = filtered.shape[2]
    own_columns = lax.dynamic_slice_in_dim(
        rotation, lax.axis_index("band") * local_count, local_count, 1
    )
    block_rows = lax.all_gather(filtered, "band", axis=0, tiled=True)
    count = block_rows.shape[0]
    flat_rows = block_rows.reshape(count, planes * columns)
    summed = jnp.dot(own_columns.T, flat_rows, preferred_element_type=jnp.float32)
    rotated = summed.reshape(local_count, planes, columns)
    return rotated


def solution(mesh):
    return jax.shard_map(
        body,
        mesh=mesh,
        in_specs=(P("band", "space", None), P("space", None), P()),
        out_specs=P("band", "space", None),
        check_vma=False,
    )
```

profile of v0, /device:TPU:25, one launch (start us, length us, event | category | flops | bytes accessed | tf_op | source)
XLA Modules:
  0.0 312.7 jit_solution(1034431220351966779)
XLA Ops:
  6.5 0.0 copy-start
  6.5 0.0 all-gather.2.cloned.1.call-start
  6.5 2.1 copy.8
  8.6 0.1 fusion.115
  8.8 0.0 copy-start.1
  8.8 5.0 %collective-permute-start = (f32[24,2,4608]{2,0,1:T(8,128)S(1)}, f32[24,2,4608]{2,0,1:T(8,128)S(1)}, u32[]{:S(2)}, u32[]{:S(2)}) collective-permute-start(f32[24,2,4608]{2,0,1:T(8,128)S(1)} %get-tuple-element.15), channel_id=1, source_target_pairs={{0,16},{16,32},{32,48},{48,64},{64,80},{80,96},{96,112},{112,128},... | collective-permute-start | bytes 2654216 | tf_op jit(solution)/shard_map/ppermute | solution.py:22
  13.8 1.9 collective-permute-start.1
  15.8 8.0 %collective-permute-done = f32[24,2,4608]{2,0,1:T(8,128)S(1)} collective-permute-done((f32[24,2,4608]{2,0,1:T(8,128)S(1)}, f32[24,2,4608]{2,0,1:T(8,128)S(1)}, u32[]{:S(2)}, u32[]{:S(2)}) %collective-permute-start) | collective-permute-done | bytes 884768 | tf_op jit(solution)/shard_map/ppermute | solution.py:22
  23.7 0.1 constant_dynamic-update-slice_fusion.1
  23.8 0.0 copy-done.1
  23.8 0.6 constant_dynamic-update-slice_fusion
  24.4 0.0 copy-start.2
  24.4 7.3 %collective-permute-done.1 = f32[24,2,4608]{2,0,1:T(8,128)S(1)} collective-permute-done((f32[24,2,4608]{2,0,1:T(8,128)S(1)}, f32[24,2,4608]{2,0,1:T(8,128)S(1)}, u32[]{:S(2)}, u32[]{:S(2)}) %collective-permute-start.1) | collective-permute-done | bytes 884768 | tf_op jit(solution)/shard_map/ppermute | solution.py:24
  31.8 0.1 constant_dynamic-update-slice_fusion.2
  31.8 0.0 copy-done.2
  31.8 4.3 %broadcast_multiply_fusion = (f32[24,4,4608]{2,0,1:T(8,128)S(1)}, f32[24,4,4608]{2,0,1:T(8,128)S(1)}) fusion(f32[24,4,4608]{2,0,1:T(8,128)S(1)} %copy.8, f32[4,4608]{1,0:T(4,128)S(1)} %copy-done.2, f32[4608]{0:T(1024)S(1)} %get-tuple-element.20, f32[4608]{0:T(1024)S(1)} %get-tuple-element.19, f32[4608]{0:T(1024)S(1)} %get-tuple-element.18, ...), kind=kLoop, calls=%fused_computation.141 | loop fusion | flops 12828672 | bytes 12533760 | tf_op jit(solution)/shard_map/div | solution.py:62
  36.1 0.1 fusion.114
  36.2 1.9 collective-permute-start.2
  38.2 2.4 collective-permute-start.3
  40.6 7.5 %collective-permute-done.2 = f32[24,2,4608]{2,0,1:T(8,128)S(1)} collective-permute-done((f32[24,2,4608]{2,0,1:T(8,128)S(1)}, f32[24,2,4608]{2,0,1:T(8,128)S(1)}, u32[]{:S(2)}, u32[]{:S(2)}) %collective-permute-start.2) | collective-permute-done | bytes 884768 | tf_op jit(solution)/shard_map/ppermute | solution.py:22
  48.1 8.0 %collective-permute-done.3 = f32[24,2,4608]{2,0,1:T(8,128)S(1)} collective-permute-done((f32[24,2,4608]{2,0,1:T(8,128)S(1)}, f32[24,2,4608]{2,0,1:T(8,128)S(1)}, u32[]{:S(2)}, u32[]{:S(2)}) %collective-permute-start.3) | collective-permute-done | bytes 884768 | tf_op jit(solution)/shard_map/ppermute | solution.py:24
  56.1 4.5 %fusion.23 = f32[24,4,4608]{2,0,1:T(8,128)S(1)} fusion(f32[24,4,4608]{2,0,1:T(8,128)S(1)} %get-tuple-element.5, f32[24,2,4608]{2,0,1:T(8,128)S(1)} %collective-permute-done.3, f32[24,2,4608]{2,0,1:T(8,128)S(1)} %collective-permute-done.2, f32[24,4,4608]{2,0,1:T(8,128)S(1)} %get-tuple-element.6, f32[4,4608]{1,0:T(4,128)S(1)} %broadcast_multiply_fusion.1, ...), kind=kLoop, calls=%fused_computation.51 | loop fusion | flops 15040512 | bytes 8994816 | tf_op jit(solution)/shard_map/sub | solution.py:64
  60.6 0.1 fusion.113
  60.8 1.9 collective-permute-start.4
  62.7 2.4 collective-permute-start.5
  65.1 7.6 %collective-permute-done.4 = f32[24,2,4608]{2,0,1:T(8,128)S(1)} collective-permute-done((f32[24,2,4608]{2,0,1:T(8,128)S(1)}, f32[24,2,4608]{2,0,1:T(8,128)S(1)}, u32[]{:S(2)}, u32[]{:S(2)}) %collective-permute-start.4) | collective-permute-done | bytes 884768 | tf_op jit(solution)/shard_map/ppermute | solution.py:22
  72.7 8.0 %collective-permute-done.5 = f32[24,2,4608]{2,0,1:T(8,128)S(1)} collective-permute-done((f32[24,2,4608]{2,0,1:T(8,128)S(1)}, f32[24,2,4608]{2,0,1:T(8,128)S(1)}, u32[]{:S(2)}, u32[]{:S(2)}) %collective-permute-start.5) | collective-permute-done | bytes 884768 | tf_op jit(solution)/shard_map/ppermute | solution.py:24
  80.7 4.3 %fusion.36 = f32[24,4,4608]{2,0,1:T(8,128)S(1)} fusion(f32[24,4,4608]{2,0,1:T(8,128)S(1)} %fusion.23, f32[24,2,4608]{2,0,1:T(8,128)S(1)} %collective-permute-done.5, f32[24,2,4608]{2,0,1:T(8,128)S(1)} %collective-permute-done.4, f32[24,4,4608]{2,0,1:T(8,128)S(1)} %get-tuple-element.6, f32[4,4608]{1,0:T(4,128)S(1)} %copy-done.2, ...), kind=kLoop, calls=%fused_computation.64 | loop fusion | flops 15482880 | bytes 7225344 | tf_op jit(solution)/shard_map/sub | solution.py:64
  85.0 0.1 fusion.112
  85.1 1.9 collective-permute-start.6
  87.0 2.6 collective-permute-start.7
  89.6 7.4 %collective-permute-done.6 = f32[24,2,4608]{2,0,1:T(8,128)S(1)} collective-permute-done((f32[24,2,4608]{2,0,1:T(8,128)S(1)}, f32[24,2,4608]{2,0,1:T(8,128)S(1)}, u32[]{:S(2)}, u32[]{:S(2)}) %collective-permute-start.6) | collective-permute-done | bytes 884768 | tf_op jit(solution)/shard_map/ppermute | solution.py:22
  97.0 8.0 %collective-permute-done.7 = f32[24,2,4608]{2,0,1:T(8,128)S(1)} collective-permute-done((f32[24,2,4608]{2,0,1:T(8,128)S(1)}, f32[24,2,4608]{2,0,1:T(8,128)S(1)}, u32[]{:S(2)}, u32[]{:S(2)}) %collective-permute-start.7) | collective-permute-done | bytes 884768 | tf_op jit(solution)/shard_map/ppermute | solution.py:24
  105.0 4.3 %fusion.96 = bf16[24,4,4608]{2,0,1:T(8,128)(2,1)S(1)} fusion(f32[24,4,4608]{2,0,1:T(8,128)S(1)} %fusion.23, f32[24,4,4608]{2,0,1:T(8,128)S(1)} %fusion.36, f32[24,2,4608]{2,0,1:T(8,128)S(1)} %collective-permute-done.7, f32[24,2,4608]{2,0,1:T(8,128)S(1)} %collective-permute-done.6, f32[4,4608]{1,0:T(4,128)S(1)} %copy-done.2, f32[4608]{0:T(1024)S(1)} %get-tuple-element.20, ...), kind=kLoop, calls=%fused_computation.140 | loop fusion | flops 15482880 | bytes 6340608 | tf_op jit(solution)/shard_map/convert_element_type | solution.py:67
  109.3 1.4 copy.18
  110.7 0.0 all-gather.2.cloned.1.call-update
  110.7 158.6 %all-gather.2.cloned.1.call-done = bf16[384,4,4608]{2,1,0:T(4,128)(2,1)} async-done(((bf16[24,4,4608]{2,1,0:T(4,128)(2,1)}), bf16[384,4,4608]{2,1,0:T(4,128)(2,1)}) %all-gather.2.cloned.1.call-update) | async-done | bytes 14155792 | tf_op jit(solution)/shard_map/all_gather | solution.py:74
  269.4 24.0 %copy.21 = bf16[384,4,4608]{0,2,1:T(8,128)(2,1)} copy(bf16[384,4,4608]{2,1,0:T(4,128)(2,1)} %all-gather.2.cloned.1.call-done) | data formatting | bytes 28311552 | tf_op jit(solution)/shard_map/reshape | solution.py:76
  293.4 0.0 copy-done
  293.4 10.1 %fusion = f32[24,4,4608]{2,0,1:T(8,128)S(1)} fusion(bf16[384,4,4608]{0,2,1:T(8,128)(2,1)} %copy.21, bf16[384,384]{1,0:T(8,128)(2,1)S(1)} %copy-done, s32[]{:T(128)S(6)} %select_n.124), kind=kOutput, calls=%fused_computation | convolution fusion | flops 339738624 | bytes 16023556 | tf_op jit(solution)/shard_map/dot_general | solution.py:77
  303.5 2.4 copy.20
  (3 shorter events, 0.1 us)
Async XLA Ops:
  6.5 286.8 %copy-start = (bf16[384,384]{1,0:T(8,128)(2,1)S(1)}, bf16[384,384]{1,0:T(8,128)(2,1)}, u32[]{:S(2)}) copy-start(bf16[384,384]{1,0:T(8,128)(2,1)} %param.5) | copy-start | bytes 884740
  6.5 262.8 %all-gather.2.cloned.1.call-start = ((), (), s32[]{:S(2)}) async-start(), calls=%async_computation | async-start | bytes 15040512 | tf_op jit(solution)/shard_map/all_gather | solution.py:74
  8.8 15.1 %copy-start.1 = (f32[24,4,4608]{2,1,0:T(4,128)S(1)}, f32[24,4,4608]{2,1,0:T(4,128)}, u32[]{:S(2)}) copy-start(f32[24,4,4608]{2,1,0:T(4,128)} %param.3) | copy-start | bytes 5308420
  8.8 15.0 %collective-permute-start = (f32[24,2,4608]{2,0,1:T(8,128)S(1)}, f32[24,2,4608]{2,0,1:T(8,128)S(1)}, u32[]{:S(2)}, u32[]{:S(2)}) collective-permute-start(f32[24,2,4608]{2,0,1:T(8,128)S(1)} %get-tuple-element.15), channel_id=1, source_target_pairs={{0,16},{16,32},{32,48},{48,64},{64,80},{80,96},{96,112},{112,128},... | collective-permute-start | bytes 2654216 | tf_op jit(solution)/shard_map/ppermute | solution.py:22
  13.8 18.0 %collective-permute-start.1 = (f32[24,2,4608]{2,0,1:T(8,128)S(1)}, f32[24,2,4608]{2,0,1:T(8,128)S(1)}, u32[]{:S(2)}, u32[]{:S(2)}) collective-permute-start(f32[24,2,4608]{2,0,1:T(8,128)S(1)} %get-tuple-element.16), channel_id=1, source_target_pairs={{16,0},{32,16},{48,32},{64,48},{80,64},{96,80},{112,96},{128,112},... | collective-permute-start | bytes 2654216 | tf_op jit(solution)/shard_map/ppermute | solution.py:24
  24.4 7.4 %copy-start.2 = (f32[4,4608]{1,0:T(4,128)S(1)}, f32[4,4608]{1,0:T(4,128)}, u32[]{:S(2)}) copy-start(f32[4,4608]{1,0:T(4,128)} %param.4) | copy-start | bytes 221188
  36.2 11.9 %collective-permute-start.2 = (f32[24,2,4608]{2,0,1:T(8,128)S(1)}, f32[24,2,4608]{2,0,1:T(8,128)S(1)}, u32[]{:S(2)}, u32[]{:S(2)}) collective-permute-start(f32[24,2,4608]{2,0,1:T(8,128)S(1)} %get-tuple-element.11), channel_id=1, source_target_pairs={{0,16},{16,32},{32,48},{48,64},{64,80},{80,96},{96,112},{112,128},... | collective-permute-start | bytes 2654216 | tf_op jit(solution)/shard_map/ppermute | solution.py:22
  38.2 18.0 %collective-permute-start.3 = (f32[24,2,4608]{2,0,1:T(8,128)S(1)}, f32[24,2,4608]{2,0,1:T(8,128)S(1)}, u32[]{:S(2)}, u32[]{:S(2)}) collective-permute-start(f32[24,2,4608]{2,0,1:T(8,128)S(1)} %get-tuple-element.12), channel_id=1, source_target_pairs={{16,0},{32,16},{48,32},{64,48},{80,64},{96,80},{112,96},{128,112},... | collective-permute-start | bytes 2654216 | tf_op jit(solution)/shard_map/ppermute | solution.py:24
  60.8 11.9 %collective-permute-start.4 = (f32[24,2,4608]{2,0,1:T(8,128)S(1)}, f32[24,2,4608]{2,0,1:T(8,128)S(1)}, u32[]{:S(2)}, u32[]{:S(2)}) collective-permute-start(f32[24,2,4608]{2,0,1:T(8,128)S(1)} %get-tuple-element.9), channel_id=1, source_target_pairs={{0,16},{16,32},{32,48},{48,64},{64,80},{80,96},{96,112},{112,128},... | collective-permute-start | bytes 2654216 | tf_op jit(solution)/shard_map/ppermute | solution.py:22
  62.7 18.0 %collective-permute-start.5 = (f32[24,2,4608]{2,0,1:T(8,128)S(1)}, f32[24,2,4608]{2,0,1:T(8,128)S(1)}, u32[]{:S(2)}, u32[]{:S(2)}) collective-permute-start(f32[24,2,4608]{2,0,1:T(8,128)S(1)} %get-tuple-element.10), channel_id=1, source_target_pairs={{16,0},{32,16},{48,32},{64,48},{80,64},{96,80},{112,96},{128,112},... | collective-permute-start | bytes 2654216 | tf_op jit(solution)/shard_map/ppermute | solution.py:24
  85.1 11.9 %collective-permute-start.6 = (f32[24,2,4608]{2,0,1:T(8,128)S(1)}, f32[24,2,4608]{2,0,1:T(8,128)S(1)}, u32[]{:S(2)}, u32[]{:S(2)}) collective-permute-start(f32[24,2,4608]{2,0,1:T(8,128)S(1)} %get-tuple-element.7), channel_id=1, source_target_pairs={{0,16},{16,32},{32,48},{48,64},{64,80},{80,96},{96,112},{112,128},... | collective-permute-start | bytes 2654216 | tf_op jit(solution)/shard_map/ppermute | solution.py:22
  87.0 18.0 %collective-permute-start.7 = (f32[24,2,4608]{2,0,1:T(8,128)S(1)}, f32[24,2,4608]{2,0,1:T(8,128)S(1)}, u32[]{:S(2)}, u32[]{:S(2)}) collective-permute-start(f32[24,2,4608]{2,0,1:T(8,128)S(1)} %get-tuple-element.8), channel_id=1, source_target_pairs={{16,0},{32,16},{48,32},{64,48},{80,64},{96,80},{112,96},{128,112},... | collective-permute-start | bytes 2654216 | tf_op jit(solution)/shard_map/ppermute | solution.py:24
Sparse Core Ops, SparseCore 0:
  110.8 158.4 all-gather.1
where the time goes:
time: 315 us; the launch traced here: 313 us
  waiting for transfers between devices  220 us (70%)
  local copies, waits for them, and re-layouts  31 us (10%)
  starting transfers between devices  20.1 us (6%)
  other arithmetic  17.4 us (6%)
  between operations  13.6 us (4%)
  matrix products  10.1 us (3%)
    all_gather x1, waiting for transfers between devices, body(): block_rows = lax.all_gather(filtered, 'band', axis=0, tiled=True)  159 us
    ppermute x4, waiting for transfers between devices, with_halo(): lax.ppermute(head, axis, [((i + 1) % count, i) for i in range(ends)])  31.4 us
    ppermute x4, waiting for transfers between devices, with_halo(): lax.ppermute(tail, axis, [(i, (i + 1) % count) for i in range(ends)])  30.4 us
    reshape x1, local copies, waits for them, and re-layouts, body(): flat_rows = block_rows.reshape(count, planes * columns)  24 us
    ppermute x4, starting transfers between devices, with_halo(): lax.ppermute(tail, axis, [(i, (i + 1) % count) for i in range(ends)])  10.8 us
    dot_general x1, matrix products, body(): jnp.dot(own_columns.T, flat_rows, preferred_element_type=jnp.float32)  10.1 us
    ppermute x4, starting transfers between devices, with_halo(): lax.ppermute(head, axis, [((i + 1) % count, i) for i in range(ends)])  9.32 us
    sub x2, other arithmetic, body(): following = 2.0 / half_width * step_once(current, potential) - previous  8.79 us
  transfers between devices with their start and end apart: 9, of which 9 were waited for; matrix products, arithmetic and copies ran while one was open for 0% of the time, Pallas kernels for 0%

commit v1 on v0

--- a/solution.py
+++ b/solution.py
@@ -65,18 +65,19 @@
         previous = current
         current = following
     filtered = current.astype(jnp.bfloat16)
-    local_count = filtered.shape[0]
-    planes = filtered.shape[1]
-    columns = filtered.shape[2]
-    own_columns = lax.dynamic_slice_in_dim(
-        rotation, lax.axis_index("band") * local_count, local_count, 1
-    )
-    block_rows = lax.all_gather(filtered, "band", axis=0, tiled=True)
-    count = block_rows.shape[0]
-    flat_rows = block_rows.reshape(count, planes * columns)
-    summed = jnp.dot(own_columns.T, flat_rows, preferred_element_type=jnp.float32)
-    rotated = summed.reshape(local_count, planes, columns)
-    return rotated
+    own, planes, columns = filtered.shape
+    members = lax.axis_size("band")
+    parts = members // planes
+    width = columns // parts
+    by_cells = filtered.reshape(own, planes, parts, width).transpose(1, 2, 0, 3)
+    by_cells = by_cells.reshape(members, own, width)
+    every = lax.all_to_all(by_cells, "band", 0, 0)
+    every = every.reshape(members * own, width)
+    summed = jnp.dot(rotation.T, every, preferred_element_type=jnp.float32)
+    summed = summed.astype(jnp.bfloat16).reshape(members, own, width)
+    back = lax.all_to_all(summed, "band", 0, 0)
+    back = back.reshape(planes, parts, own, width).transpose(2, 0, 1, 3)
+    return back.reshape(own, planes, columns).astype(jnp.float32)
 
 
 def solution(mesh):

time: 315 us -> 161 us (0.51)
  waiting for transfers between devices: 220 us -> 62 us
  blocking collectives: 0 us -> 53.9 us
  local copies, waits for them, and re-layouts: 31 us -> 5.9 us
  between operations: 13.6 us -> 0.22 us
  matrix products: 10.1 us -> 0.7 us
    all_gather x1 -> x0, waiting for transfers between devices: 159 us -> none  [body(): block_rows = lax.all_gather(filtered, 'band', axis=0, tiled=True)]
    all_to_all x0 -> x2, blocking collectives: none -> 53.9 us  [the longest x1 27.6 us: body(): every = lax.all_to_all(by_cells, 'band', 0, 0)]
    reshape x1, local copies, waits for them, and re-layouts: 24 us -> 0.07 us  [body(): by_cells = filtered.reshape(own, planes, parts, width).transpose(1, 2, 0, 3)]
    dot_general x1, matrix products: 10.1 us -> 0.7 us  [body(): summed = jnp.dot(rotation.T, every, preferred_element_type=jnp.float32)]
  transfers between devices with their start and end apart: 9 -> 8, of which waited for: 9 -> 8; matrix products, arithmetic and copies ran while one was open for 0% -> 0% of each run, Pallas kernels for 0% -> 0%
where the time goes in v1:
time: 161 us; the launch traced here: 160 us
  waiting for transfers between devices  62 us (39%)
  blocking collectives  53.9 us (33%)
  starting transfers between devices  19.9 us (12%)
  other arithmetic  17.4 us (11%)
  local copies, waits for them, and re-layouts  5.9 us (4%)
    ppermute x4, waiting for transfers between devices, with_halo(): lax.ppermute(head, axis, [((i + 1) % count, i) for i in range(ends)])  31.4 us
    ppermute x4, waiting for transfers between devices, with_halo(): lax.ppermute(tail, axis, [(i, (i + 1) % count) for i in range(ends)])  30.6 us
    all_to_all x1, blocking collectives, body(): every = lax.all_to_all(by_cells, 'band', 0, 0)  27.6 us
    all_to_all x1, blocking collectives, body(): back = lax.all_to_all(summed, 'band', 0, 0)  26.3 us
    ppermute x4, starting transfers between devices, with_halo(): lax.ppermute(tail, axis, [(i, (i + 1) % count) for i in range(ends)])  10.8 us
    ppermute x4, starting transfers between devices, with_halo(): lax.ppermute(head, axis, [((i + 1) % count, i) for i in range(ends)])  9.14 us
    sub x2, other arithmetic, body(): following = 2.0 / half_width * step_once(current, potential) - previous  8.79 us
    convert_element_type x1, other arithmetic, body(): filtered = current.astype(jnp.bfloat16)  4.31 us
  transfers between devices with their start and end apart: 8, of which 8 were waited for; matrix products, arithmetic and copies ran while one was open for 0% of the time, Pallas kernels for 0%

profile of v1, /device:TPU:25, one launch (start us, length us, event | category | flops | bytes accessed | tf_op | source)
XLA Modules:
  0.0 160.1 jit_solution(4843172341223422504)
XLA Ops:
  0.0 0.0 copy-start
  0.0 2.1 %copy.7 = f32[24,4,4608]{2,0,1:T(8,128)S(1)} copy(f32[24,4,4608]{2,1,0:T(4,128)} %param.3) | data formatting | bytes 3538944 | tf_op args[0]
  2.1 0.1 fusion.110
  2.2 0.0 copy-start.1
  2.2 5.0 %collective-permute-start = (f32[24,2,4608]{2,0,1:T(8,128)S(1)}, f32[24,2,4608]{2,0,1:T(8,128)S(1)}, u32[]{:S(2)}, u32[]{:S(2)}) collective-permute-start(f32[24,2,4608]{2,0,1:T(8,128)S(1)} %get-tuple-element.15), channel_id=1, source_target_pairs={{0,16},{16,32},{32,48},{48,64},{64,80},{80,96},{96,112},{112,128},... | collective-permute-start | bytes 2654216 | tf_op jit(solution)/shard_map/ppermute | solution.py:22
  7.2 1.9 %collective-permute-start.1 = (f32[24,2,4608]{2,0,1:T(8,128)S(1)}, f32[24,2,4608]{2,0,1:T(8,128)S(1)}, u32[]{:S(2)}, u32[]{:S(2)}) collective-permute-start(f32[24,2,4608]{2,0,1:T(8,128)S(1)} %get-tuple-element.16), channel_id=1, source_target_pairs={{16,0},{32,16},{48,32},{64,48},{80,64},{96,80},{112,96},{128,112},... | collective-permute-start | bytes 2654216 | tf_op jit(solution)/shard_map/ppermute | solution.py:24
  9.2 8.0 %collective-permute-done = f32[24,2,4608]{2,0,1:T(8,128)S(1)} collective-permute-done((f32[24,2,4608]{2,0,1:T(8,128)S(1)}, f32[24,2,4608]{2,0,1:T(8,128)S(1)}, u32[]{:S(2)}, u32[]{:S(2)}) %collective-permute-start) | collective-permute-done | bytes 884768 | tf_op jit(solution)/shard_map/ppermute | solution.py:22
  17.2 0.1 constant_dynamic-update-slice_fusion.1
  17.3 0.0 copy-done.1
  17.3 0.6 constant_dynamic-update-slice_fusion
  17.9 0.0 copy-start.2
  17.9 7.3 %collective-permute-done.1 = f32[24,2,4608]{2,0,1:T(8,128)S(1)} collective-permute-done((f32[24,2,4608]{2,0,1:T(8,128)S(1)}, f32[24,2,4608]{2,0,1:T(8,128)S(1)}, u32[]{:S(2)}, u32[]{:S(2)}) %collective-permute-start.1) | collective-permute-done | bytes 884768 | tf_op jit(solution)/shard_map/ppermute | solution.py:24
  25.2 0.1 constant_dynamic-update-slice_fusion.2
  25.3 0.0 copy-done.2
  25.3 4.3 %broadcast_multiply_fusion = (f32[24,4,4608]{2,0,1:T(8,128)S(1)}, f32[24,4,4608]{2,0,1:T(8,128)S(1)}) fusion(f32[24,4,4608]{2,0,1:T(8,128)S(1)} %copy.7, f32[4,4608]{1,0:T(4,128)S(1)} %copy-done.2, f32[4608]{0:T(1024)S(1)} %get-tuple-element.20, f32[4608]{0:T(1024)S(1)} %get-tuple-element.19, f32[4608]{0:T(1024)S(1)} %get-tuple-element.18, ...), kind=kLoop, calls=%fused_computation.142 | loop fusion | flops 12828672 | bytes 12533760 | tf_op jit(solution)/shard_map/div | solution.py:62
  29.6 0.1 fusion.109
  29.7 1.9 %collective-permute-start.2 = (f32[24,2,4608]{2,0,1:T(8,128)S(1)}, f32[24,2,4608]{2,0,1:T(8,128)S(1)}, u32[]{:S(2)}, u32[]{:S(2)}) collective-permute-start(f32[24,2,4608]{2,0,1:T(8,128)S(1)} %get-tuple-element.11), channel_id=1, source_target_pairs={{0,16},{16,32},{32,48},{48,64},{64,80},{80,96},{96,112},{112,128},... | collective-permute-start | bytes 2654216 | tf_op jit(solution)/shard_map/ppermute | solution.py:22
  31.6 2.4 %collective-permute-start.3 = (f32[24,2,4608]{2,0,1:T(8,128)S(1)}, f32[24,2,4608]{2,0,1:T(8,128)S(1)}, u32[]{:S(2)}, u32[]{:S(2)}) collective-permute-start(f32[24,2,4608]{2,0,1:T(8,128)S(1)} %get-tuple-element.12), channel_id=1, source_target_pairs={{16,0},{32,16},{48,32},{64,48},{80,64},{96,80},{112,96},{128,112},... | collective-permute-start | bytes 2654216 | tf_op jit(solution)/shard_map/ppermute | solution.py:24
  34.1 7.5 %collective-permute-done.2 = f32[24,2,4608]{2,0,1:T(8,128)S(1)} collective-permute-done((f32[24,2,4608]{2,0,1:T(8,128)S(1)}, f32[24,2,4608]{2,0,1:T(8,128)S(1)}, u32[]{:S(2)}, u32[]{:S(2)}) %collective-permute-start.2) | collective-permute-done | bytes 884768 | tf_op jit(solution)/shard_map/ppermute | solution.py:22
  41.6 8.0 %collective-permute-done.3 = f32[24,2,4608]{2,0,1:T(8,128)S(1)} collective-permute-done((f32[24,2,4608]{2,0,1:T(8,128)S(1)}, f32[24,2,4608]{2,0,1:T(8,128)S(1)}, u32[]{:S(2)}, u32[]{:S(2)}) %collective-permute-start.3) | collective-permute-done | bytes 884768 | tf_op jit(solution)/shard_map/ppermute | solution.py:24
  49.6 4.5 %fusion.21 = f32[24,4,4608]{2,0,1:T(8,128)S(1)} fusion(f32[24,4,4608]{2,0,1:T(8,128)S(1)} %get-tuple-element.5, f32[24,2,4608]{2,0,1:T(8,128)S(1)} %collective-permute-done.3, f32[24,2,4608]{2,0,1:T(8,128)S(1)} %collective-permute-done.2, f32[24,4,4608]{2,0,1:T(8,128)S(1)} %get-tuple-element.6, f32[4,4608]{1,0:T(4,128)S(1)} %broadcast_multiply_fusion.1, ...), kind=kLoop, calls=%fused_computation.50 | loop fusion | flops 15040512 | bytes 8994816 | tf_op jit(solution)/shard_map/sub | solution.py:64
  54.1 0.1 fusion.108
  54.2 1.9 %collective-permute-start.4 = (f32[24,2,4608]{2,0,1:T(8,128)S(1)}, f32[24,2,4608]{2,0,1:T(8,128)S(1)}, u32[]{:S(2)}, u32[]{:S(2)}) collective-permute-start(f32[24,2,4608]{2,0,1:T(8,128)S(1)} %get-tuple-element.9), channel_id=1, source_target_pairs={{0,16},{16,32},{32,48},{48,64},{64,80},{80,96},{96,112},{112,128},... | collective-permute-start | bytes 2654216 | tf_op jit(solution)/shard_map/ppermute | solution.py:22
  56.2 2.4 %collective-permute-start.5 = (f32[24,2,4608]{2,0,1:T(8,128)S(1)}, f32[24,2,4608]{2,0,1:T(8,128)S(1)}, u32[]{:S(2)}, u32[]{:S(2)}) collective-permute-start(f32[24,2,4608]{2,0,1:T(8,128)S(1)} %get-tuple-element.10), channel_id=1, source_target_pairs={{16,0},{32,16},{48,32},{64,48},{80,64},{96,80},{112,96},{128,112},... | collective-permute-start | bytes 2654216 | tf_op jit(solution)/shard_map/ppermute | solution.py:24
  58.6 7.6 %collective-permute-done.4 = f32[24,2,4608]{2,0,1:T(8,128)S(1)} collective-permute-done((f32[24,2,4608]{2,0,1:T(8,128)S(1)}, f32[24,2,4608]{2,0,1:T(8,128)S(1)}, u32[]{:S(2)}, u32[]{:S(2)}) %collective-permute-start.4) | collective-permute-done | bytes 884768 | tf_op jit(solution)/shard_map/ppermute | solution.py:22
  66.1 8.0 %collective-permute-done.5 = f32[24,2,4608]{2,0,1:T(8,128)S(1)} collective-permute-done((f32[24,2,4608]{2,0,1:T(8,128)S(1)}, f32[24,2,4608]{2,0,1:T(8,128)S(1)}, u32[]{:S(2)}, u32[]{:S(2)}) %collective-permute-start.5) | collective-permute-done | bytes 884768 | tf_op jit(solution)/shard_map/ppermute | solution.py:24
  74.1 4.3 %fusion.34 = f32[24,4,4608]{2,0,1:T(8,128)S(1)} fusion(f32[24,4,4608]{2,0,1:T(8,128)S(1)} %fusion.21, f32[24,2,4608]{2,0,1:T(8,128)S(1)} %collective-permute-done.5, f32[24,2,4608]{2,0,1:T(8,128)S(1)} %collective-permute-done.4, f32[24,4,4608]{2,0,1:T(8,128)S(1)} %get-tuple-element.6, f32[4,4608]{1,0:T(4,128)S(1)} %copy-done.2, ...), kind=kLoop, calls=%fused_computation.63 | loop fusion | flops 15482880 | bytes 7225344 | tf_op jit(solution)/shard_map/sub | solution.py:64
  78.4 0.1 fusion.107
  78.6 1.9 %collective-permute-start.6 = (f32[24,2,4608]{2,0,1:T(8,128)S(1)}, f32[24,2,4608]{2,0,1:T(8,128)S(1)}, u32[]{:S(2)}, u32[]{:S(2)}) collective-permute-start(f32[24,2,4608]{2,0,1:T(8,128)S(1)} %get-tuple-element.7), channel_id=1, source_target_pairs={{0,16},{16,32},{32,48},{48,64},{64,80},{80,96},{96,112},{112,128},... | collective-permute-start | bytes 2654216 | tf_op jit(solution)/shard_map/ppermute | solution.py:22
  80.5 2.4 %collective-permute-start.7 = (f32[24,2,4608]{2,0,1:T(8,128)S(1)}, f32[24,2,4608]{2,0,1:T(8,128)S(1)}, u32[]{:S(2)}, u32[]{:S(2)}) collective-permute-start(f32[24,2,4608]{2,0,1:T(8,128)S(1)} %get-tuple-element.8), channel_id=1, source_target_pairs={{16,0},{32,16},{48,32},{64,48},{80,64},{96,80},{112,96},{128,112},... | collective-permute-start | bytes 2654216 | tf_op jit(solution)/shard_map/ppermute | solution.py:24
  82.9 7.6 %collective-permute-done.6 = f32[24,2,4608]{2,0,1:T(8,128)S(1)} collective-permute-done((f32[24,2,4608]{2,0,1:T(8,128)S(1)}, f32[24,2,4608]{2,0,1:T(8,128)S(1)}, u32[]{:S(2)}, u32[]{:S(2)}) %collective-permute-start.6) | collective-permute-done | bytes 884768 | tf_op jit(solution)/shard_map/ppermute | solution.py:22
  90.5 8.0 %collective-permute-done.7 = f32[24,2,4608]{2,0,1:T(8,128)S(1)} collective-permute-done((f32[24,2,4608]{2,0,1:T(8,128)S(1)}, f32[24,2,4608]{2,0,1:T(8,128)S(1)}, u32[]{:S(2)}, u32[]{:S(2)}) %collective-permute-start.7) | collective-permute-done | bytes 884768 | tf_op jit(solution)/shard_map/ppermute | solution.py:24
  98.5 4.3 %fusion.94 = bf16[24,4,4608]{2,0,1:T(8,128)(2,1)S(1)} fusion(f32[24,4,4608]{2,0,1:T(8,128)S(1)} %fusion.21, f32[24,4,4608]{2,0,1:T(8,128)S(1)} %fusion.34, f32[24,2,4608]{2,0,1:T(8,128)S(1)} %collective-permute-done.7, f32[24,2,4608]{2,0,1:T(8,128)S(1)} %collective-permute-done.6, f32[4,4608]{1,0:T(4,128)S(1)} %copy-done.2, f32[4608]{0:T(1024)S(1)} %get-tuple-element.20, ...), kind=kLoop, calls=%fused_computation.140 | loop fusion | flops 15482880 | bytes 6340608 | tf_op jit(solution)/shard_map/convert_element_type | solution.py:67
  102.8 0.1 copy.26
  102.9 27.6 %all_to_all.10 = bf16[16,24,1152]{2,1,0:T(8,128)(2,1)S(1)} all-to-all(bf16[16,24,1152]{2,1,0:T(8,128)(2,1)S(1)} %bitcast.20), channel_id=1, replica_groups=mesh['space'=16,'band'=16] {'band'}, dimensions={0} | all-to-all | bytes 1769472 | tf_op jit(solution)/shard_map/all_to_all | solution.py:74
  130.5 0.0 copy-done
  130.5 0.7 convolution_convert_fusion
  131.2 26.3 %all_to_all.11 = bf16[16,24,1152]{2,1,0:T(8,128)(2,1)S(1)} all-to-all(bf16[16,24,1152]{2,1,0:T(8,128)(2,1)S(1)} %bitcast.22), channel_id=1, replica_groups=mesh['space'=16,'band'=16] {'band'}, dimensions={0} | all-to-all | bytes 1769472 | tf_op jit(solution)/shard_map/all_to_all | solution.py:78
  157.5 0.3 copy.25
  157.8 2.2 %reshape.46 = f32[24,4,4608]{2,1,0:T(4,128)} reshape(f32[24,4,4,1152]{3,2,1,0:T(4,128)S(1)} %bitcast.18) | data formatting | bytes 3538944 | tf_op jit(solution)/shard_map/convert_element_type | solution.py:80
  (3 shorter events, 0.1 us)
Async XLA Ops:
  0.0 130.5 %copy-start = (bf16[384,384]{1,0:T(8,128)(2,1)S(1)}, bf16[384,384]{1,0:T(8,128)(2,1)}, u32[]{:S(2)}) copy-start(bf16[384,384]{1,0:T(8,128)(2,1)} %param.5) | copy-start | bytes 884740
  2.2 15.1 %copy-start.1 = (f32[24,4,4608]{2,1,0:T(4,128)S(1)}, f32[24,4,4608]{2,1,0:T(4,128)}, u32[]{:S(2)}) copy-start(f32[24,4,4608]{2,1,0:T(4,128)} %param.3) | copy-start | bytes 5308420
  2.2 15.0 %collective-permute-start = (f32[24,2,4608]{2,0,1:T(8,128)S(1)}, f32[24,2,4608]{2,0,1:T(8,128)S(1)}, u32[]{:S(2)}, u32[]{:S(2)}) collective-permute-start(f32[24,2,4608]{2,0,1:T(8,128)S(1)} %get-tuple-element.15), channel_id=1, source_target_pairs={{0,16},{16,32},{32,48},{48,64},{64,80},{80,96},{96,112},{112,128},... | collective-permute-start | bytes 2654216 | tf_op jit(solution)/shard_map/ppermute | solution.py:22
  7.2 18.0 %collective-permute-start.1 = (f32[24,2,4608]{2,0,1:T(8,128)S(1)}, f32[24,2,4608]{2,0,1:T(8,128)S(1)}, u32[]{:S(2)}, u32[]{:S(2)}) collective-permute-start(f32[24,2,4608]{2,0,1:T(8,128)S(1)} %get-tuple-element.16), channel_id=1, source_target_pairs={{16,0},{32,16},{48,32},{64,48},{80,64},{96,80},{112,96},{128,112},... | collective-permute-start | bytes 2654216 | tf_op jit(solution)/shard_map/ppermute | solution.py:24
  17.9 7.4 %copy-start.2 = (f32[4,4608]{1,0:T(4,128)S(1)}, f32[4,4608]{1,0:T(4,128)}, u32[]{:S(2)}) copy-start(f32[4,4608]{1,0:T(4,128)} %param.4) | copy-start | bytes 221188
  29.7 11.9 %collective-permute-start.2 = (f32[24,2,4608]{2,0,1:T(8,128)S(1)}, f32[24,2,4608]{2,0,1:T(8,128)S(1)}, u32[]{:S(2)}, u32[]{:S(2)}) collective-permute-start(f32[24,2,4608]{2,0,1:T(8,128)S(1)} %get-tuple-element.11), channel_id=1, source_target_pairs={{0,16},{16,32},{32,48},{48,64},{64,80},{80,96},{96,112},{112,128},... | collective-permute-start | bytes 2654216 | tf_op jit(solution)/shard_map/ppermute | solution.py:22
  31.6 18.0 %collective-permute-start.3 = (f32[24,2,4608]{2,0,1:T(8,128)S(1)}, f32[24,2,4608]{2,0,1:T(8,128)S(1)}, u32[]{:S(2)}, u32[]{:S(2)}) collective-permute-start(f32[24,2,4608]{2,0,1:T(8,128)S(1)} %get-tuple-element.12), channel_id=1, source_target_pairs={{16,0},{32,16},{48,32},{64,48},{80,64},{96,80},{112,96},{128,112},... | collective-permute-start | bytes 2654216 | tf_op jit(solution)/shard_map/ppermute | solution.py:24
  54.2 11.9 %collective-permute-start.4 = (f32[24,2,4608]{2,0,1:T(8,128)S(1)}, f32[24,2,4608]{2,0,1:T(8,128)S(1)}, u32[]{:S(2)}, u32[]{:S(2)}) collective-permute-start(f32[24,2,4608]{2,0,1:T(8,128)S(1)} %get-tuple-element.9), channel_id=1, source_target_pairs={{0,16},{16,32},{32,48},{48,64},{64,80},{80,96},{96,112},{112,128},... | collective-permute-start | bytes 2654216 | tf_op jit(solution)/shard_map/ppermute | solution.py:22
  56.2 18.0 %collective-permute-start.5 = (f32[24,2,4608]{2,0,1:T(8,128)S(1)}, f32[24,2,4608]{2,0,1:T(8,128)S(1)}, u32[]{:S(2)}, u32[]{:S(2)}) collective-permute-start(f32[24,2,4608]{2,0,1:T(8,128)S(1)} %get-tuple-element.10), channel_id=1, source_target_pairs={{16,0},{32,16},{48,32},{64,48},{80,64},{96,80},{112,96},{128,112},... | collective-permute-start | bytes 2654216 | tf_op jit(solution)/shard_map/ppermute | solution.py:24
  78.6 11.9 %collective-permute-start.6 = (f32[24,2,4608]{2,0,1:T(8,128)S(1)}, f32[24,2,4608]{2,0,1:T(8,128)S(1)}, u32[]{:S(2)}, u32[]{:S(2)}) collective-permute-start(f32[24,2,4608]{2,0,1:T(8,128)S(1)} %get-tuple-element.7), channel_id=1, source_target_pairs={{0,16},{16,32},{32,48},{48,64},{64,80},{80,96},{96,112},{112,128},... | collective-permute-start | bytes 2654216 | tf_op jit(solution)/shard_map/ppermute | solution.py:22
  80.5 18.0 %collective-permute-start.7 = (f32[24,2,4608]{2,0,1:T(8,128)S(1)}, f32[24,2,4608]{2,0,1:T(8,128)S(1)}, u32[]{:S(2)}, u32[]{:S(2)}) collective-permute-start(f32[24,2,4608]{2,0,1:T(8,128)S(1)} %get-tuple-element.8), channel_id=1, source_target_pairs={{16,0},{32,16},{48,32},{64,48},{80,64},{96,80},{112,96},{128,112},... | collective-permute-start | bytes 2654216 | tf_op jit(solution)/shard_map/ppermute | solution.py:24

commit v2 on v1

v2 whole, which is shorter than its diff:
```python
import functools

import jax
import jax.numpy as jnp
import numpy as np
from jax import lax
from jax.experimental import pallas as pl
from jax.experimental.pallas import tpu as pltpu
from jax.sharding import PartitionSpec as P

NY = 48
NZ = 96
LANE = 128
ROWS = 8
GROUPS = 4
RUNS = NY // GROUPS
ZI = 3
ZB = NZ // ZI
PIECES = RUNS * ZI

CENTER = 4.75
HALF_WIDTH = 3.75
NEAR = -2.0 / 3.0 / HALF_WIDTH
FAR = 1.0 / 24.0 / HALF_WIDTH

CHUNKS = (24,)


def lanes_of(rows):
    return lax.broadcasted_iota(jnp.int32, (rows, LANE), 1)


def piece(j):
    return pl.ds(j * LANE, LANE)


def pick(values, lanes):
    return jnp.take_along_axis(values, lanes, axis=1)


def to_runs_kernel(cells, out):
    planes, rows, _ = out.shape
    lane = lanes_of(rows)
    group = lane // ZB

    def one_plane(p, _):
        for b in range(RUNS):
            for zi in range(ZI):
                total = None
                for a in range(GROUPS):
                    start = (RUNS * a + b) * NZ
                    j, offset = start // LANE, start % LANE
                    source = lane % ZB * ZI + (offset + zi)
                    part = pick(cells[p, :, piece(j)], source % LANE)
                    if offset + NZ > LANE:
                        part = jnp.where(source < LANE, part, pick(cells[p, :, piece(j + 1)], source % LANE))
                    total = part if total is None else jnp.where(group == a, part, total)
                out[p, :, piece(ZI * b + zi)] = total
        return 0

    lax.fori_loop(0, planes, one_plane, 0)


def to_runs(cells):
    planes, count, columns = cells.shape
    rows = min(count, ROWS)
    spec = pl.BlockSpec((planes, rows, columns), lambda i: (0, i, 0))
    return pl.pallas_call(
        to_runs_kernel,
        grid=(count // rows,),
        in_specs=[spec],
        out_specs=spec,
        out_shape=jax.ShapeDtypeStruct(cells.shape, cells.dtype),
        compiler_params=pltpu.CompilerParams(vmem_limit_bytes=32 * 1024 * 1024),
        cost_estimate=pl.CostEstimate(flops=40000 * count * columns, bytes_accessed=cells.size * 8, transcendentals=0),
    )(cells)


def stencil_row(src, plane, masks, emit):
    a_last, a_first, zb_last, zb_first = masks
    centers, turned = {}, {}

    def center(b, zi):
        if (b, zi) not in centers:
            centers[b, zi] = src[plane + 2, :, piece(ZI * b + zi)]
        return centers[b, zi]

    def turn(b, zi, by, mask):
        if (b, zi, by) not in turned:
            turned[b, zi, by] = jnp.where(mask, 0.0, pltpu.roll(center(b, zi), by, 1))
        return turned[b, zi, by]

    def at_y(b, zi):
        if b < 0:
            return turn(b + RUNS, zi, ZB, a_first)
        if b >= RUNS:
            return turn(b - RUNS, zi, LANE - ZB, a_last)
        return center(b, zi)

    def at_z(b, zi):
        if zi < 0:
            return turn(b, zi + ZI, 1, zb_first)
        if zi >= ZI:
            return turn(b, zi - ZI, LANE - 1, zb_last)
        return center(b, zi)

    def at_x(j, k):
        return src[plane + 2 + k, :, piece(j)]

    for b in range(RUNS):
        for zi in range(ZI):
            j = ZI * b + zi
            near, far = [
                (at_x(j, -k) + at_x(j, k)) + (at_y(b - k, zi) + at_y(b + k, zi)) + (at_z(b, zi - k) + at_z(b, zi + k))
                for k in (1, 2)
            ]
            emit(j, center(b, zi), near, far)


def split_groups(four, odd, upper):
    half = {}
    for i in (0, 2):
        half[i] = jnp.where(odd, pltpu.roll(four[i + 1], ZB, 1), four[i])
        half[i + 1] = jnp.where(odd, four[i + 1], pltpu.roll(four[i], LANE - ZB, 1))
    done = {}
    for i in (0, 1):
        done[i] = jnp.where(upper, pltpu.roll(half[i + 2], 2 * ZB, 1), half[i])
        done[i + 2] = jnp.where(upper, half[i + 2], pltpu.roll(half[i], 2 * ZB, 1))
    return done


def two_steps_kernel(last, inside, lo, own, hi, potential, *rest):
    if last:
        first, out, field, inner, diag = rest
    else:
        out, field, inner, diag = rest
    planes, rows, columns = own.shape

    @pl.when(pl.program_id(0) == 0)
    def _():
        for p in range(planes + 4):
            scaled = (potential[p : p + 1, :] + (HALF_WIDTH - CENTER)) / HALF_WIDTH
            diag[p] = jnp.broadcast_to(scaled, (rows, columns))

    field[0:planes] = lo[...]
    field[planes : 2 * planes] = own[...]
    field[2 * planes : 3 * planes] = hi[...]

    lane = lanes_of(rows)
    masks = (lane >= LANE - ZB, lane < ZB, lane % ZB == ZB - 1, lane % ZB == 0)
    odd = lane // ZB % 2 == 1
    upper = lane >= 2 * ZB

    def first_stage(p, _):
        here = jnp.where(p < 2, inside[0], jnp.where(p >= planes + 2, inside[1], 1.0))
        near_by = here * NEAR
        far_by = here * FAR

        def emit(j, center, near, far):
            inner[p, :, piece(j)] = diag[p, :, piece(j)] * center + near_by * near + far_by * far

        stencil_row(field, p + planes - 4, masks, emit)
        return 0

    lax.fori_loop(0, planes + 4, first_stage, 0)

    def second_stage(p, _):
        held = []

        def emit(j, center, near, far):
            total = diag[p + 2, :, piece(j)] * center + NEAR * near + FAR * far
            total = 2.0 * total - field[p + planes, :, piece(j)]
            if not last:
                out[p, :, piece(j)] = total
                return
            held.append(2.0 * total - first[p, :, piece(j)])
            if len(held) == GROUPS:
                done = split_groups(held, odd, upper)
                for a in range(GROUPS):
                    out[GROUPS * p + a, :, piece(j // GROUPS)] = done[a]
                held.clear()

        stencil_row(inner, p, masks, emit)
        return 0

    lax.fori_loop(0, planes, second_stage, 0)


def two_steps(inside, lo, own, hi, potential, first=None):
    planes, count, columns = own.shape
    last = first is not None
    spec = pl.BlockSpec((planes, ROWS, columns), lambda i: (0, i, 0))
    out_shape, out_spec = (planes, count, columns), spec
    if last:
        width = columns // GROUPS
        out_shape = (planes * GROUPS, count, width)
        out_spec = pl.BlockSpec((planes * GROUPS, ROWS, width), lambda i: (0, i, 0))
    return pl.pallas_call(
        functools.partial(two_steps_kernel, last),
        grid=(count // ROWS,),
        in_specs=[
            pl.BlockSpec(memory_space=pltpu.SMEM),
            spec,
            spec,
            spec,
            pl.BlockSpec(potential.shape, lambda i: (0, 0)),
        ]
        + [spec] * last,
        out_specs=out_spec,
        out_shape=jax.ShapeDtypeStruct(out_shape, jnp.float32),
        scratch_shapes=[
            pltpu.VMEM((planes * 3, ROWS, columns), jnp.float32),
            pltpu.VMEM((planes + 4, ROWS, columns), jnp.float32),
            pltpu.VMEM((planes + 4, ROWS, columns), jnp.float32),
        ],
        compiler_params=pltpu.CompilerParams(vmem_limit_bytes=32 * 1024 * 1024),
        cost_estimate=pl.CostEstimate(flops=80000 * count * columns, bytes_accessed=own.size * 16, transcendentals=0),
    )(inside, lo, own, hi, potential, *([first] if last else []))


def z_order():
    one = np.zeros((NZ, NZ), np.float32)
    for z in range(NZ):
        one[z % ZI * ZB + z // ZI, z] = 1.0
    return jnp.asarray(np.kron(np.eye(GROUPS, dtype=np.float32), one), jnp.bfloat16)


def body(orbitals, potential, rotation):
    count, planes, columns = orbitals.shape
    domains = lax.axis_size("space")
    members = lax.axis_size("band")
    up = [(i, i + 1) for i in range(domains - 1)]
    down = [(i + 1, i) for i in range(domains - 1)]

    def around(cells):
        return lax.ppermute(cells, "space", up), lax.ppermute(cells, "space", down)

    at = lax.axis_index("space")
    inside = jnp.stack([at > 0, at < domains - 1]).astype(jnp.float32)

    starts = [sum(CHUNKS[:i]) for i in range(len(CHUNKS))]
    pieces = [lax.slice_in_dim(orbitals, s, s + n, axis=0) for s, n in zip(starts, CHUNKS)]
    zeroth = [to_runs(x.transpose(1, 0, 2)) for x in pieces]
    zeroth_around = [around(x) for x in zeroth]

    own_potential = to_runs(potential[None])[0]
    potential_below = lax.ppermute(own_potential[planes - 2 :], "space", up)
    potential_above = lax.ppermute(own_potential[:2], "space", down)
    field = jnp.concatenate([potential_below, own_potential, potential_above], axis=0)

    gathered = []
    second = [two_steps(inside, lo, x, hi, field) for x, (lo, hi) in zip(zeroth, zeroth_around)]
    second_around = [around(x) for x in second]
    for x, y, (lo, hi) in zip(zeroth, second, second_around):
        filtered = two_steps(inside, lo, y, hi, field, first=x).astype(jnp.bfloat16)
        gathered.append(lax.all_to_all(filtered, "band", 0, 0))

    by_member = rotation.reshape(members, count, members * count)
    width = columns // GROUPS
    summed = 0.0
    for s, n, part in zip(starts, CHUNKS, gathered):
        weights = by_member[:, s : s + n].reshape(members * n, members * count)
        summed = summed + jnp.dot(weights.T, part.reshape(members * n, width), preferred_element_type=jnp.float32)
    summed = summed.astype(jnp.bfloat16)
    order = z_order()
    summed = jnp.dot(
        summed.reshape(-1, order.shape[0]), order, preferred_element_type=jnp.float32
    ).astype(jnp.bfloat16)
    back = lax.all_to_all(summed.reshape(members, count, width), "band", 0, 0)
    back = back.reshape(planes, GROUPS, count, width).transpose(2, 0, 1, 3)
    return back.reshape(count, planes, columns).astype(jnp.float32)


def solution(mesh):
    return jax.shard_map(
        body,
        mesh=mesh,
        in_specs=(P("band", "space", None), P("space", None), P()),
        out_specs=P("band", "space", None),
        check_vma=False,
    )
```

time: 161 us -> 142 us (0.88)
  waiting for transfers between devices: 62 us -> 34.4 us
  Pallas kernels: 0 us -> 21.3 us
  other arithmetic: 17.4 us -> 0.22 us
  starting transfers between devices: 19.9 us -> 23.4 us
    ppermute x8 -> x6, waiting for transfers between devices: 62 us -> 34.4 us  [the longest x2 18.3 us: around(): lax.ppermute(cells, 'space', down)]
    pallas_call x0 -> x4, Pallas kernels: none -> 21.3 us  [the longest x2 15.4 us: two_steps(): pl.pallas_call(functools.partial(two_steps_kernel, last), grid=(count //...]
    sub x2 -> x0, other arithmetic: 8.79 us -> none  [body(): following = 2.0 / half_width * step_once(current, potential) - previous]
    div x1 -> x0, other arithmetic: 4.27 us -> none  [body(): current = step_once(orbitals, potential) / half_width]
    convert_element_type x1 -> x2, other arithmetic: 4.31 us -> 0.17 us  [the longest x1 0.09 us: body(): filtered = two_steps(inside, lo, y, hi, field, first=x).astype(jnp.bfloat16)]
    ppermute x8 -> x6, starting transfers between devices: 19.9 us -> 23.4 us  [the longest x2 14.6 us: around(): lax.ppermute(cells, 'space', up)]
    convert_element_type x2 -> x3, local copies, waits for them, and re-layouts: 2.56 us -> 3.44 us  [the longest x2 2.56 us: body(): return back.reshape(count, planes, columns).astype(jnp.float32)]
  transfers between devices with their start and end apart: 8 -> 6, of which waited for: 8 -> 3; matrix products, arithmetic and copies ran while one was open for 0% -> 0% of each run, Pallas kernels for 0% -> 0%
where the time goes in v2:
time: 142 us; the launch traced here: 141 us
  blocking collectives  53.8 us (38%)
  waiting for transfers between devices  34.4 us (24%)
  starting transfers between devices  23.4 us (16%)
  Pallas kernels  21.3 us (15%)
  local copies, waits for them, and re-layouts  6.4 us (5%)
  matrix products  1.44 us (1%)
    all_to_all x1, blocking collectives, body(): gathered.append(lax.all_to_all(filtered, 'band', 0, 0))  27.4 us
    all_to_all x1, blocking collectives, body(): back = lax.all_to_all(summed.reshape(members, count, width), 'band', 0, 0)  26.3 us
    ppermute x2, waiting for transfers between devices, around(): lax.ppermute(cells, 'space', down)  18.3 us
    pallas_call x2, Pallas kernels, two_steps(): pl.pallas_call(functools.partial(two_steps_kernel, last), grid=(count //...  15.4 us
    ppermute x1, waiting for transfers between devices, body(): potential_below = lax.ppermute(own_potential[planes - 2:], 'space', up)  14.9 us
    ppermute x2, starting transfers between devices, around(): lax.ppermute(cells, 'space', up)  14.6 us
    pallas_call x2, Pallas kernels, to_runs(): pl.pallas_call(to_runs_kernel, grid=(count // rows,), in_specs=[spec], ou...  5.89 us
    ppermute x2, starting transfers between devices, around(): lax.ppermute(cells, 'space', down)  4.51 us
  transfers between devices with their start and end apart: 6, of which 3 were waited for; matrix products, arithmetic and copies ran while one was open for 0% of the time, Pallas kernels for 0%

profile of v2, /device:TPU:25, one launch (start us, length us, event | category | flops | bytes accessed | tf_op | source)
XLA Modules:
  0.0 141.2 jit_solution(2152564247912144950)
XLA Ops:
  0.0 0.0 copy-start
  0.0 2.1 %copy.13 = f32[24,4,4608]{2,0,1:T(8,128)S(1)} copy(f32[24,4,4608]{2,1,0:T(4,128)} %param.4) | data formatting | bytes 3538944 | tf_op args[0]
  2.1 0.0 copy-start.1
  2.1 5.5 %shard_map.46.own.rest_0_ = f32[4,24,4608]{2,1,0:T(8,128)S(1)} custom-call(f32[4,24,4608]{2,1,0:T(8,128)S(1)} %bitcast.23), custom_call_target="tpu_custom_call" | custom-call | flops 4423680000 | bytes 3538944 | tf_op jit(solution)/shard_map/pallas_call | solution.py:68
  7.6 2.6 %collective-permute-start.1 = (f32[4,24,4608]{2,1,0:T(8,128)S(1)}, f32[4,24,4608]{2,1,0:T(8,128)}, u32[]{:S(2)}, u32[]{:S(2)}) collective-permute-start(f32[4,24,4608]{2,1,0:T(8,128)S(1)} %shard_map.46.own.rest_0_), channel_id=1, source_target_pairs={{16,0},{32,16},{48,32},{64,48},{80,64},{96,80},{112,96},{128,112},... | collective-permute-start | bytes 5308424 | tf_op jit(solution)/shard_map/ppermute | solution.py:236
  10.2 6.6 %collective-permute-start = (f32[4,24,4608]{2,1,0:T(8,128)S(1)}, f32[4,24,4608]{2,1,0:T(8,128)}, u32[]{:S(2)}, u32[]{:S(2)}) collective-permute-start(f32[4,24,4608]{2,1,0:T(8,128)S(1)} %shard_map.46.own.rest_0_), channel_id=1, source_target_pairs={{0,16},{16,32},{32,48},{48,64},{64,80},{80,96},{96,112},{112,128},... | collective-permute-start | bytes 5308424 | tf_op jit(solution)/shard_map/ppermute | solution.py:236
  16.8 0.0 copy-done.1
  16.8 0.4 shard_map.47
  17.3 1.9 %collective-permute-start.2 = (f32[2,4608]{1,0:T(2,128)S(1)}, f32[2,4608]{1,0:T(2,128)S(1)}, u32[]{:S(2)}, u32[]{:S(2)}) collective-permute-start(f32[2,4608]{1,0:T(2,128)S(1)} %get-tuple-element.5), channel_id=1, source_target_pairs={{0,16},{16,32},{32,48},{48,64},{64,80},{80,96},{96,112},{112,128},... | collective-permute-start | bytes 110600 | tf_op jit(solution)/shard_map/ppermute | solution.py:247
  19.2 2.4 %collective-permute-start.3 = (f32[2,4608]{1,0:T(2,128)S(1)}, f32[2,4608]{1,0:T(2,128)S(1)}, u32[]{:S(2)}, u32[]{:S(2)}) collective-permute-start(f32[2,4608]{1,0:T(2,128)S(1)} %get-tuple-element.6), channel_id=1, source_target_pairs={{16,0},{32,16},{48,32},{64,48},{80,64},{96,80},{112,96},{128,112},... | collective-permute-start | bytes 110600 | tf_op jit(solution)/shard_map/ppermute | solution.py:248
  21.6 0.1 add_convert_fusion.inside
  21.7 14.9 %collective-permute-done.2 = f32[2,4608]{1,0:T(2,128)S(1)} collective-permute-done((f32[2,4608]{1,0:T(2,128)S(1)}, f32[2,4608]{1,0:T(2,128)S(1)}, u32[]{:S(2)}, u32[]{:S(2)}) %collective-permute-start.2) | collective-permute-done | bytes 36896 | tf_op jit(solution)/shard_map/ppermute | solution.py:247
  36.6 0.0 collective-permute-done.3
  36.6 0.1 pad_maximum_fusion.potential
  36.7 0.0 collective-permute-done.1.hi
  36.7 0.0 collective-permute-done.lo
  36.7 6.9 %shard_map.48.own = f32[4,24,4608]{2,1,0:T(8,128)S(1)} custom-call(f32[2]{0:T(128)S(1)} %add_convert_fusion.inside, f32[4,24,4608]{2,1,0:T(8,128)} %collective-permute-done.lo, f32[4,24,4608]{2,1,0:T(8,128)S(1)} %shard_map.46.own.rest_0_, f32[4,24,4608]{2,1,0:T(8,128)} %collective-permute-done.1.hi, f32[8,4608]{1,0:T(8,128)S(1)} %pad_maximum_fusion.potential), custom_call_target="tpu_custom_call" | custom-call | flops 8847360000 | bytes 7077888 | tf_op jit(solution)/shard_map/pallas_call | solution.py:198
  43.6 1.9 %collective-permute-start.5 = (f32[4,24,4608]{2,1,0:T(8,128)S(1)}, f32[4,24,4608]{2,1,0:T(8,128)S(1)}, u32[]{:S(2)}, u32[]{:S(2)}) collective-permute-start(f32[4,24,4608]{2,1,0:T(8,128)S(1)} %shard_map.48.own), channel_id=1, source_target_pairs={{16,0},{32,16},{48,32},{64,48},{80,64},{96,80},{112,96},{128,112},... | collective-permute-start | bytes 5308424 | tf_op jit(solution)/shard_map/ppermute | solution.py:236
  45.6 8.0 %collective-permute-start.4 = (f32[4,24,4608]{2,1,0:T(8,128)S(1)}, f32[4,24,4608]{2,1,0:T(8,128)S(1)}, u32[]{:S(2)}, u32[]{:S(2)}) collective-permute-start(f32[4,24,4608]{2,1,0:T(8,128)S(1)} %shard_map.48.own), channel_id=1, source_target_pairs={{0,16},{16,32},{32,48},{48,64},{64,80},{80,96},{96,112},{112,128},... | collective-permute-start | bytes 5308424 | tf_op jit(solution)/shard_map/ppermute | solution.py:236
  53.6 18.3 %collective-permute-done.5.hi = f32[4,24,4608]{2,1,0:T(8,128)S(1)} collective-permute-done((f32[4,24,4608]{2,1,0:T(8,128)S(1)}, f32[4,24,4608]{2,1,0:T(8,128)S(1)}, u32[]{:S(2)}, u32[]{:S(2)}) %collective-permute-start.5) | collective-permute-done | bytes 1769504 | tf_op jit(solution)/shard_map/ppermute | solution.py:236
  71.8 1.2 collective-permute-done.4.lo
  73.0 8.5 %shard_map.49 = f32[16,24,1152]{2,1,0:T(8,128)S(1)} custom-call(f32[2]{0:T(128)S(1)} %add_convert_fusion.inside, f32[4,24,4608]{2,1,0:T(8,128)S(1)} %collective-permute-done.4.lo, f32[4,24,4608]{2,1,0:T(8,128)S(1)} %shard_map.48.own, f32[4,24,4608]{2,1,0:T(8,128)S(1)} %collective-permute-done.5.hi, f32[8,4608]{1,0:T(8,128)S(1)} %pad_maximum_fusion.potential, ...), custom_call_target="tpu_custom_call" | custom-call | flops 8847360000 | bytes 7077888 | tf_op jit(solution)/shard_map/pallas_call | solution.py:198
  81.5 0.1 convert_element_type.28
  81.6 27.4 %all_to_all.10 = bf16[16,24,1152]{2,1,0:T(8,128)(2,1)S(1)} all-to-all(bf16[16,24,1152]{2,1,0:T(8,128)(2,1)S(1)} %convert_element_type.28), channel_id=1, replica_groups=mesh['space'=16,'band'=16] {'band'}, dimensions={0} | all-to-all | bytes 1769472 | tf_op jit(solution)/shard_map/all_to_all | solution.py:256
  109.1 0.0 copy-done
  109.1 0.8 fusion
  109.8 0.0 copy-start.2
  109.8 0.9 copy.8
  110.7 0.4 reshape.18
  111.1 0.0 copy-done.2
  111.2 0.7 convolution_convert_fusion
  111.9 0.4 reshape.19
  112.3 26.3 %all_to_all.11 = bf16[16,24,1152]{2,1,0:T(8,128)(2,1)S(1)} all-to-all(bf16[16,24,1152]{2,1,0:T(8,128)(2,1)S(1)} %reshape.19), channel_id=1, replica_groups=mesh['space'=16,'band'=16] {'band'}, dimensions={0} | all-to-all | bytes 1769472 | tf_op jit(solution)/shard_map/all_to_all | solution.py:269
  138.6 0.3 copy.12
  139.0 2.2 %reshape.20 = f32[24,4,4608]{2,1,0:T(4,128)} reshape(f32[24,4,4,1152]{3,2,1,0:T(4,128)S(1)} %bitcast.26) | data formatting | bytes 3538944 | tf_op jit(solution)/shard_map/convert_element_type | solution.py:271
  (1 shorter events, 0.0 us)
Async XLA Ops:
  0.0 109.1 %copy-start = (bf16[384,384]{1,0:T(8,128)(2,1)S(1)}, bf16[384,384]{1,0:T(8,128)(2,1)}, u32[]{:S(2)}) copy-start(bf16[384,384]{1,0:T(8,128)(2,1)} %param.6) | copy-start | bytes 884740
  2.1 14.7 %copy-start.1 = (f32[4,4608]{1,0:T(4,128)S(1)}, f32[4,4608]{1,0:T(4,128)}, u32[]{:S(2)}) copy-start(f32[4,4608]{1,0:T(4,128)} %param.5) | copy-start | bytes 221188
  7.6 29.1 %collective-permute-start.1 = (f32[4,24,4608]{2,1,0:T(8,128)S(1)}, f32[4,24,4608]{2,1,0:T(8,128)}, u32[]{:S(2)}, u32[]{:S(2)}) collective-permute-start(f32[4,24,4608]{2,1,0:T(8,128)S(1)} %shard_map.46.own.rest_0_), channel_id=1, source_target_pairs={{16,0},{32,16},{48,32},{64,48},{80,64},{96,80},{112,96},{128,112},... | collective-permute-start | bytes 5308424 | tf_op jit(solution)/shard_map/ppermute | solution.py:236
  10.2 26.5 %collective-permute-start = (f32[4,24,4608]{2,1,0:T(8,128)S(1)}, f32[4,24,4608]{2,1,0:T(8,128)}, u32[]{:S(2)}, u32[]{:S(2)}) collective-permute-start(f32[4,24,4608]{2,1,0:T(8,128)S(1)} %shard_map.46.own.rest_0_), channel_id=1, source_target_pairs={{0,16},{16,32},{32,48},{48,64},{64,80},{80,96},{96,112},{112,128},... | collective-permute-start | bytes 5308424 | tf_op jit(solution)/shard_map/ppermute | solution.py:236
  17.3 19.4 %collective-permute-start.2 = (f32[2,4608]{1,0:T(2,128)S(1)}, f32[2,4608]{1,0:T(2,128)S(1)}, u32[]{:S(2)}, u32[]{:S(2)}) collective-permute-start(f32[2,4608]{1,0:T(2,128)S(1)} %get-tuple-element.5), channel_id=1, source_target_pairs={{0,16},{16,32},{32,48},{48,64},{64,80},{80,96},{96,112},{112,128},... | collective-permute-start | bytes 110600 | tf_op jit(solution)/shard_map/ppermute | solution.py:247
  19.2 17.4 %collective-permute-start.3 = (f32[2,4608]{1,0:T(2,128)S(1)}, f32[2,4608]{1,0:T(2,128)S(1)}, u32[]{:S(2)}, u32[]{:S(2)}) collective-permute-start(f32[2,4608]{1,0:T(2,128)S(1)} %get-tuple-element.6), channel_id=1, source_target_pairs={{16,0},{32,16},{48,32},{64,48},{80,64},{96,80},{112,96},{128,112},... | collective-permute-start | bytes 110600 | tf_op jit(solution)/shard_map/ppermute | solution.py:248
  43.6 28.2 %collective-permute-start.5 = (f32[4,24,4608]{2,1,0:T(8,128)S(1)}, f32[4,24,4608]{2,1,0:T(8,128)S(1)}, u32[]{:S(2)}, u32[]{:S(2)}) collective-permute-start(f32[4,24,4608]{2,1,0:T(8,128)S(1)} %shard_map.48.own), channel_id=1, source_target_pairs={{16,0},{32,16},{48,32},{64,48},{80,64},{96,80},{112,96},{128,112},... | collective-permute-start | bytes 5308424 | tf_op jit(solution)/shard_map/ppermute | solution.py:236
  45.6 27.5 %collective-permute-start.4 = (f32[4,24,4608]{2,1,0:T(8,128)S(1)}, f32[4,24,4608]{2,1,0:T(8,128)S(1)}, u32[]{:S(2)}, u32[]{:S(2)}) collective-permute-start(f32[4,24,4608]{2,1,0:T(8,128)S(1)} %shard_map.48.own), channel_id=1, source_target_pairs={{0,16},{16,32},{32,48},{48,64},{64,80},{80,96},{96,112},{112,128},... | collective-permute-start | bytes 5308424 | tf_op jit(solution)/shard_map/ppermute | solution.py:236
  109.8 1.3 copy-start.2

commit v3 on v2

v3 whole, which is shorter than its diff:
```python
import functools

import jax
import jax.numpy as jnp
import numpy as np
from jax import lax
from jax.experimental import pallas as pl
from jax.experimental.pallas import tpu as pltpu
from jax.sharding import PartitionSpec as P

NY = 48
NZ = 96
LANE = 128
ROWS = 8
GROUPS = 4
RUNS = NY // GROUPS
ZI = 3
ZB = NZ // ZI
PIECES = RUNS * ZI
ROW_BLOCK = GROUPS * NZ

CENTER = 4.75
HALF_WIDTH = 3.75
NEAR = -2.0 / 3.0 / HALF_WIDTH
FAR = 1.0 / 24.0 / HALF_WIDTH


def lanes_of(rows):
    return lax.broadcasted_iota(jnp.int32, (rows, LANE), 1)


def piece(j):
    return pl.ds(j * LANE, LANE)


def split_groups(four, odd, upper):
    half = {}
    for i in (0, 2):
        half[i] = jnp.where(odd, pltpu.roll(four[i + 1], ZB, 1), four[i])
        half[i + 1] = jnp.where(odd, four[i + 1], pltpu.roll(four[i], LANE - ZB, 1))
    done = {}
    for i in (0, 1):
        done[i] = jnp.where(upper, pltpu.roll(half[i + 2], 2 * ZB, 1), half[i])
        done[i + 2] = jnp.where(upper, half[i + 2], pltpu.roll(half[i], 2 * ZB, 1))
    return done


def rounded(x):
    return x.astype(jnp.bfloat16).astype(jnp.float32)


def pack_halo(planes_at, j, to_above, to_below):
    for to, order in ((to_above, (3, 2, 1, 0)), (to_below, (0, 1, 2, 3))):
        near, next_near, far, farthest = [planes_at(p) for p in order]
        for i, x in enumerate((near, next_near)):
            both = jnp.concatenate([x, x - rounded(x)], axis=0)
            to[0, pl.ds(2 * ROWS * i, 2 * ROWS), piece(j)] = both.astype(jnp.bfloat16)
        both = jnp.concatenate([far, farthest], axis=0)
        to[0, pl.ds(4 * ROWS, 2 * ROWS), piece(j)] = both.astype(jnp.bfloat16)


def unpack_halo(halo, field, order):
    near, next_near, far, farthest = order
    columns = field.shape[2]
    for at in range(0, columns, ROW_BLOCK):
        lanes = pl.ds(at, ROW_BLOCK)
        for i, p in enumerate((near, next_near)):
            both = halo[0, pl.ds(2 * ROWS * i, 2 * ROWS), lanes].astype(jnp.float32)
            field[p, :, lanes] = both[:ROWS] + both[ROWS:]
        both = halo[0, pl.ds(4 * ROWS, 2 * ROWS), lanes].astype(jnp.float32)
        field[far, :, lanes] = both[:ROWS]
        field[farthest, :, lanes] = both[ROWS:]


def halo_shape(count, columns):
    return jax.ShapeDtypeStruct((count // ROWS, 6 * ROWS, columns), jnp.bfloat16)


def halo_spec(columns):
    return pl.BlockSpec((1, 6 * ROWS, columns), lambda i: (i, 0, 0))


def to_runs_kernel(cells, order, out, to_above, to_below, terms, turned):
    planes, rows, columns = out.shape
    blocks = columns // ROW_BLOCK
    for k in range(blocks):
        for pair in range(planes // 2):
            x = cells[2 * pair : 2 * pair + 2, :, pl.ds(k * ROW_BLOCK, ROW_BLOCK)].reshape(2 * rows, ROW_BLOCK)
            at = pl.ds((k * (planes // 2) + pair) * 2 * rows, 2 * rows)
            first = rounded(x)
            second = rounded(x - first)
            terms[0, at] = first.astype(jnp.bfloat16)
            terms[1, at] = second.astype(jnp.bfloat16)
            terms[2, at] = (x - first - second).astype(jnp.bfloat16)
    parts = [jnp.dot(terms[i], order[...], preferred_element_type=jnp.float32) for i in range(3)]
    turned[...] = parts[0] + (parts[1] + parts[2])

    group = lanes_of(rows) // ZB
    odd = group % 2 == 1
    upper = group >= 2
    per_group = blocks // GROUPS
    for m in range(PIECES // GROUPS):
        done = []
        for p in range(planes):
            four = [
                turned[pl.ds((a * per_group + m // ZI) * planes * rows + p * rows, rows), piece(m % ZI)]
                for a in range(GROUPS)
            ]
            done.append(split_groups(four, odd, upper))
        for i in range(GROUPS):
            j = GROUPS * m + i
            for p in range(planes):
                out[p, :, piece(j)] = done[p][i]
            pack_halo(lambda p: done[p][i], j, to_above, to_below)


def to_runs(cells):
    planes, count, columns = cells.shape
    order = z_order().T
    spec = pl.BlockSpec((planes, ROWS, columns), lambda i: (0, i, 0))
    halo = halo_spec(columns)
    total = planes * ROWS * columns // ROW_BLOCK
    return pl.pallas_call(
        to_runs_kernel,
        grid=(count // ROWS,),
        in_specs=[spec, pl.BlockSpec(order.shape, lambda i: (0, 0))],
        out_specs=[spec, halo, halo],
        out_shape=[jax.ShapeDtypeStruct(cells.shape, cells.dtype)] + [halo_shape(count, columns)] * 2,
        scratch_shapes=[
            pltpu.VMEM((3, total, ROW_BLOCK), jnp.bfloat16),
            pltpu.VMEM((total, ROW_BLOCK), jnp.float32),
        ],
        compiler_params=pltpu.CompilerParams(vmem_limit_bytes=32 * 1024 * 1024),
        cost_estimate=pl.CostEstimate(flops=40000 * count * columns, bytes_accessed=cells.size * 8, transcendentals=0),
    )(cells, order)


def stencil_row(src, plane, masks, emit):
    a_last, a_first, zb_last, zb_first = masks
    centers, turned = {}, {}

    def center(b, zi):
        if (b, zi) not in centers:
            centers[b, zi] = src[plane + 2, :, piece(ZI * b + zi)]
        return centers[b, zi]

    def turn(b, zi, by, mask):
        if (b, zi, by) not in turned:
            turned[b, zi, by] = jnp.where(mask, 0.0, pltpu.roll(center(b, zi), by, 1))
        return turned[b, zi, by]

    def at_y(b, zi):
        if b < 0:
            return turn(b + RUNS, zi, ZB, a_first)
        if b >= RUNS:
            return turn(b - RUNS, zi, LANE - ZB, a_last)
        return center(b, zi)

    def at_z(b, zi):
        if zi < 0:
            return turn(b, zi + ZI, 1, zb_first)
        if zi >= ZI:
            return turn(b, zi - ZI, LANE - 1, zb_last)
        return center(b, zi)

    def at_x(j, k):
        return src[plane + 2 + k, :, piece(j)]

    for b in range(RUNS):
        for zi in range(ZI):
            j = ZI * b + zi
            near, far = [
                (at_x(j, -k) + at_x(j, k)) + (at_y(b - k, zi) + at_y(b + k, zi)) + (at_z(b, zi - k) + at_z(b, zi + k))
                for k in (1, 2)
            ]
            emit(j, center(b, zi), near, far)


def two_steps_kernel(last, inside, below, own, above, potential, *rest):
    if last:
        first, out, field, inner, diag = rest
    else:
        out, to_above, to_below, field, inner, diag = rest
    planes, rows, columns = own.shape

    @pl.when(pl.program_id(0) == 0)
    def _():
        for p in range(planes + 4):
            scaled = (potential[p : p + 1, :] + (HALF_WIDTH - CENTER)) / HALF_WIDTH
            diag[p] = jnp.broadcast_to(scaled, (rows, columns))

    unpack_halo(below, field, (3, 2, 1, 0))
    field[planes : 2 * planes] = own[...]
    unpack_halo(above, field, (8, 9, 10, 11))

    lane = lanes_of(rows)
    masks = (lane >= LANE - ZB, lane < ZB, lane % ZB == ZB - 1, lane % ZB == 0)
    odd = lane // ZB % 2 == 1
    upper = lane >= 2 * ZB

    def first_stage(p, _):
        here = jnp.where(p < 2, inside[0], jnp.where(p >= planes + 2, inside[1], 1.0))
        near_by = here * NEAR
        far_by = here * FAR

        def emit(j, center, near, far):
            inner[p, :, piece(j)] = diag[p, :, piece(j)] * center + near_by * near + far_by * far

        stencil_row(field, p + planes - 4, masks, emit)
        return 0

    lax.fori_loop(0, planes + 4, first_stage, 0)

    def second_stage(p, _):
        held = []

        def emit(j, center, near, far):
            total = diag[p + 2, :, piece(j)] * center + NEAR * near + FAR * far
            total = 2.0 * total - field[p + planes, :, piece(j)]
            if not last:
                out[p, :, piece(j)] = total
                return
            held.append(2.0 * total - first[p, :, piece(j)])
            if len(held) == GROUPS:
                done = split_groups(held, odd, upper)
                for a in range(GROUPS):
                    out[GROUPS * p + a, :, piece(j // GROUPS)] = done[a]
                held.clear()

        stencil_row(inner, p, masks, emit)
        return 0

    lax.fori_loop(0, planes, second_stage, 0)
    if not last:
        for j in range(PIECES):
            pack_halo(lambda p: out[p, :, piece(j)], j, to_above, to_below)


def two_steps(inside, below, own, above, potential, first=None):
    planes, count, columns = own.shape
    last = first is not None
    spec = pl.BlockSpec((planes, ROWS, columns), lambda i: (0, i, 0))
    halo = halo_spec(columns)
    out_shape = [jax.ShapeDtypeStruct(own.shape, own.dtype)] + [halo_shape(count, columns)] * 2
    out_spec = [spec, halo, halo]
    if last:
        width = columns // GROUPS
        out_shape = jax.ShapeDtypeStruct((planes * GROUPS, count, width), jnp.float32)
        out_spec = pl.BlockSpec((planes * GROUPS, ROWS, width), lambda i: (0, i, 0))
    return pl.pallas_call(
        functools.partial(two_steps_kernel, last),
        grid=(count // ROWS,),
        in_specs=[
            pl.BlockSpec(memory_space=pltpu.SMEM),
            halo,
            spec,
            halo,
            pl.BlockSpec(potential.shape, lambda i: (0, 0)),
        ]
        + [spec] * last,
        out_specs=out_spec,
        out_shape=out_shape,
        scratch_shapes=[
            pltpu.VMEM((planes * 3, ROWS, columns), jnp.float32),
            pltpu.VMEM((planes + 4, ROWS, columns), jnp.float32),
            pltpu.VMEM((planes + 4, ROWS, columns), jnp.float32),
        ],
        compiler_params=pltpu.CompilerParams(vmem_limit_bytes=32 * 1024 * 1024),
        cost_estimate=pl.CostEstimate(flops=80000 * count * columns, bytes_accessed=own.size * 16, transcendentals=0),
    )(inside, below, own, above, potential, *([first] if last else []))


def z_order():
    one = np.zeros((NZ, NZ), np.float32)
    for z in range(NZ):
        one[z % ZI * ZB + z // ZI, z] = 1.0
    return jnp.asarray(np.kron(np.eye(GROUPS, dtype=np.float32), one), jnp.bfloat16)


def rotate_kernel(weights, cells, order, out):
    for k in range(cells.shape[1] // ROW_BLOCK):
        at = pl.ds(k * ROW_BLOCK, ROW_BLOCK)
        summed = jnp.dot(weights[...], cells[:, at], preferred_element_type=jnp.float32).astype(jnp.bfloat16)
        out[:, at] = jnp.dot(summed, order[...], preferred_element_type=jnp.float32).astype(jnp.bfloat16)


def rotate(weights, cells):
    return pl.pallas_call(
        rotate_kernel,
        out_shape=jax.ShapeDtypeStruct((weights.shape[0], cells.shape[1]), jnp.bfloat16),
        compiler_params=pltpu.CompilerParams(vmem_limit_bytes=32 * 1024 * 1024),
        cost_estimate=pl.CostEstimate(
            flops=4 * weights.size * cells.shape[1], bytes_accessed=4 * cells.size, transcendentals=0
        ),
    )(weights, cells, z_order())


def body(orbitals, potential, rotation):
    count, planes, columns = orbitals.shape
    domains = lax.axis_size("space")
    members = lax.axis_size("band")
    up = [(i, i + 1) for i in range(domains - 1)]
    down = [(i + 1, i) for i in range(domains - 1)]

    def around(to_above, to_below):
        return lax.ppermute(to_above, "space", up), lax.ppermute(to_below, "space", down)

    at = lax.axis_index("space")
    inside = jnp.stack([at > 0, at < domains - 1]).astype(jnp.float32)

    zeroth, *halo = to_runs(orbitals.transpose(1, 0, 2))
    below, above = around(*halo)

    runs = potential.reshape(planes, GROUPS, RUNS, ZB, ZI).transpose(0, 2, 4, 1, 3).reshape(planes, columns)
    potential_below = lax.ppermute(runs[planes - 2 :], "space", up)
    potential_above = lax.ppermute(runs[:2], "space", down)
    field = jnp.concatenate([potential_below, runs, potential_above], axis=0)

    second, *halo = two_steps(inside, below, zeroth, above, field)
    below, above = around(*halo)
    filtered = two_steps(inside, below, second, above, field, first=zeroth).astype(jnp.bfloat16)
    gathered = lax.all_to_all(filtered, "band", 0, 0)
    width = columns // GROUPS
    summed = rotate(rotation.T, gathered.reshape(members * count, width))
    back = lax.all_to_all(summed.reshape(members, count, width), "band", 0, 0)
    back = back.reshape(planes, GROUPS, count, width).transpose(2, 0, 1, 3)
    return back.reshape(count, planes, columns).astype(jnp.float32)


def solution(mesh):
    return jax.shard_map(
        body,
        mesh=mesh,
        in_specs=(P("band", "space", None), P("space", None), P()),
        out_specs=P("band", "space", None),
        check_vma=False,
    )
```

time: 142 us -> 145 us (1.021)
  blocking collectives: 53.8 us -> 26.5 us
  local copies, waits for them, and re-layouts: 6.4 us -> 23.7 us
  waiting for transfers between devices: 34.4 us -> 42.5 us
  starting transfers between devices: 23.4 us -> 29.7 us
    all_to_all x1 -> x0, blocking collectives: 27.4 us -> none  [body(): gathered.append(lax.all_to_all(filtered, 'band', 0, 0))]
    all_to_all x0 -> x1, waiting for transfers between devices: none -> 17.8 us  [body(): gathered = lax.all_to_all(filtered, 'band', 0, 0)]
    ppermute x6, waiting for transfers between devices: 34.4 us -> 24.7 us  [the longest x2 12.8 us: around(): lax.ppermute(to_above, 'space', up)]
    all_to_all x0 -> x1, starting transfers between devices: none -> 8.45 us  [body(): gathered = lax.all_to_all(filtered, 'band', 0, 0)]
    slice x1 -> x5, local copies, waits for them, and re-layouts: 0.04 us -> 8.4 us  [the longest x3 6.19 us: body(): potential_below = lax.ppermute(runs[planes - 2:], 'space', up)]
    reshape x2, local copies, waits for them, and re-layouts: 0.81 us -> 4.99 us  [body(): potential.reshape(planes, GROUPS, RUNS, ZB, ZI).transpose(0, 2, 4, 1, 3)]
    unnamed x7 -> x14, local copies, waits for them, and re-layouts: 2.11 us -> 5.01 us
    transpose x0 -> x1, local copies, waits for them, and re-layouts: none -> 2.71 us  [body(): potential.reshape(planes, GROUPS, RUNS, ZB, ZI).transpose(0, 2, 4, 1, 3)]
  transfers between devices with their start and end apart: 6 -> 7, of which waited for: 3 -> 4; matrix products, arithmetic and copies ran while one was open for 0% -> 11% of each run, Pallas kernels for 0% -> 0%
where the time goes in v3:
time: 145 us
  waiting for transfers between devices  42.5 us (29%)
  starting transfers between devices  29.7 us (20%)
  blocking collectives  26.5 us (18%)
  local copies, waits for them, and re-layouts  23.7 us (16%)
  Pallas kernels  20.9 us (14%)
    all_to_all x1, blocking collectives, body(): back = lax.all_to_all(summed.reshape(members, count, width), 'band', 0, 0)  26.5 us
    all_to_all x1, waiting for transfers between devices, body(): gathered = lax.all_to_all(filtered, 'band', 0, 0)  17.8 us
    pallas_call x2, Pallas kernels, two_steps(): pl.pallas_call(functools.partial(two_steps_kernel, last), grid=(count //...  15.4 us
    ppermute x2, waiting for transfers between devices, around(): lax.ppermute(to_above, 'space', up)  12.8 us
    all_to_all x1, starting transfers between devices, body(): gathered = lax.all_to_all(filtered, 'band', 0, 0)  8.45 us
    ppermute x2, starting transfers between devices, around(): lax.ppermute(to_above, 'space', up)  8.21 us
    ppermute x2, waiting for transfers between devices, around(): lax.ppermute(to_below, 'space', down)  8.01 us
    ppermute x1, starting transfers between devices, body(): potential_below = lax.ppermute(runs[planes - 2:], 'space', up)  7.26 us
  transfers between devices with their start and end apart: 7, of which 4 were waited for; matrix products, arithmetic and copies ran while one was open for 11% of the time, Pallas kernels for 0%

profile of v3, /device:TPU:25, one launch (start us, length us, event | category | flops | bytes accessed | tf_op | source)
XLA Modules:
  0.0 144.5 jit_solution(13058085295746562197)
XLA Ops:
  0.0 0.0 copy-start.1
  0.0 2.1 %copy.19 = f32[24,4,4608]{2,0,1:T(8,128)S(1)} copy(f32[24,4,4608]{2,1,0:T(4,128)} %param.5) | data formatting | bytes 3538944 | tf_op args[0]
  2.1 0.0 copy-done.1
  2.1 0.0 copy-start.5
  2.1 4.1 %shard_map.55 = (f32[4,24,4608]{2,1,0:T(8,128)S(1)}, bf16[3,48,4608]{2,1,0:T(8,128)(2,1)}, bf16[3,48,4608]{2,1,0:T(8,128)(2,1)S(1)}) custom-call(f32[4,24,4608]{2,1,0:T(8,128)S(1)} %bitcast.14, bf16[384,384]{1,0:T(8,128)(2,1)S(1)} %copy-done.1), custom_call_target="tpu_custom_call" | custom-call | flops 4423680000 | bytes 3538944 | tf_op jit(solution)/shard_map/pallas_call | solution.py:123
  6.2 0.0 copy-start.2
  6.2 1.2 copy-done.2
  7.4 4.9 %collective-permute-start = (bf16[3,48,4608]{2,1,0:T(8,128)(2,1)}, bf16[3,48,4608]{2,1,0:T(8,128)(2,1)S(1)}, u32[]{:S(2)}, u32[]{:S(2)}) collective-permute-start(bf16[3,48,4608]{2,1,0:T(8,128)(2,1)} %get-tuple-element.11), channel_id=1, source_target_pairs={{0,16},{16,32},{32,48},{48,64},{64,80},{80,96},{96,112},{112,128},... | collective-permute-start | bytes 3981320 | tf_op jit(solution)/shard_map/ppermute | solution.py:306
  12.3 1.9 %collective-permute-start.1 = (bf16[3,48,4608]{2,1,0:T(8,128)(2,1)S(1)}, bf16[3,48,4608]{2,1,0:T(8,128)(2,1)}, u32[]{:S(2)}, u32[]{:S(2)}) collective-permute-start(bf16[3,48,4608]{2,1,0:T(8,128)(2,1)S(1)} %get-tuple-element.13), channel_id=1, source_target_pairs={{16,0},{32,16},{48,32},{64,48},{80,64},{96,80},{112,96},{128,112},... | collective-permute-start | bytes 3981320 | tf_op jit(solution)/shard_map/ppermute | solution.py:306
  14.2 0.0 copy-done.5
  14.2 4.8 %reshape.20 = f32[4,4,12,32,3]{4,3,2,1,0:T(8,128)} reshape(f32[4,4608]{1,0:T(4,128)S(1)} %copy-done.5) | data formatting | bytes 147456 | tf_op jit(solution)/shard_map/reshape | solution.py:314
  19.0 4.0 %fusion = (f32[2,12,3,4,32]{2,4,1,3,0:T(8,128)}, f32[2,12,3,4,32]{2,4,1,3,0:T(8,128)}) fusion(f32[4,12,3,4,32]{2,4,1,3,0:T(8,128)} %bitcast.18), kind=kLoop, calls=%fused_computation.4 | loop fusion | bytes 147456 | tf_op jit(solution)/shard_map/slice | solution.py:315
  23.0 2.0 %copy.12 = f32[2,12,3,4,32]{4,3,2,1,0:T(4,128)S(1)} copy(f32[2,12,3,4,32]{2,4,1,3,0:T(8,128)} %get-tuple-element.17) | data formatting | bytes 73728 | tf_op jit(solution)/shard_map/slice | solution.py:315
  25.0 0.2 slice.13
  25.2 7.3 %collective-permute-start.2 = (f32[2,4608]{1,0:T(2,128)S(1)}, f32[2,4608]{1,0:T(2,128)S(1)}, u32[]{:S(2)}, u32[]{:S(2)}) collective-permute-start(f32[2,4608]{1,0:T(2,128)S(1)} %slice.13), channel_id=1, source_target_pairs={{0,16},{16,32},{32,48},{48,64},{64,80},{80,96},{96,112},{112,128},... | collective-permute-start | bytes 110600 | tf_op jit(solution)/shard_map/ppermute | solution.py:315
  32.5 2.0 %copy.14 = f32[2,12,3,4,32]{4,3,2,1,0:T(4,128)S(1)} copy(f32[2,12,3,4,32]{2,4,1,3,0:T(8,128)} %get-tuple-element.18) | data formatting | bytes 73728 | tf_op jit(solution)/shard_map/slice | solution.py:316
  34.5 0.2 slice.15
  34.7 1.9 %collective-permute-start.3 = (f32[2,4608]{1,0:T(2,128)S(1)}, f32[2,4608]{1,0:T(2,128)S(1)}, u32[]{:S(2)}, u32[]{:S(2)}) collective-permute-start(f32[2,4608]{1,0:T(2,128)S(1)} %slice.15), channel_id=1, source_target_pairs={{16,0},{32,16},{48,32},{64,48},{80,64},{96,80},{112,96},{128,112},... | collective-permute-start | bytes 110600 | tf_op jit(solution)/shard_map/ppermute | solution.py:316
  36.6 0.1 add_convert_fusion.inside
  36.7 2.7 %copy.13 = f32[4,12,3,4,32]{4,3,2,1,0:T(4,128)S(1)} copy(f32[4,12,3,4,32]{2,4,1,3,0:T(8,128)} %bitcast.19) | data formatting | bytes 147456 | tf_op jit(solution)/shard_map/transpose | solution.py:314
  39.4 0.2 reshape.21
  39.6 0.0 collective-permute-done.2
  39.6 3.9 %collective-permute-done.3 = f32[2,4608]{1,0:T(2,128)S(1)} collective-permute-done((f32[2,4608]{1,0:T(2,128)S(1)}, f32[2,4608]{1,0:T(2,128)S(1)}, u32[]{:S(2)}, u32[]{:S(2)}) %collective-permute-start.3) | collective-permute-done | bytes 36896 | tf_op jit(solution)/shard_map/ppermute | solution.py:316
  43.6 0.1 pad_maximum_fusion.potential
  43.6 0.0 collective-permute-done.below
  43.6 0.0 collective-permute-done.1.above
  43.6 0.0 copy-start.3
  43.7 1.5 %copy-done.3 = f32[4,24,4608]{2,1,0:T(8,128)S(1)} copy-done((f32[4,24,4608]{2,1,0:T(8,128)S(1)}, f32[4,24,4608]{2,1,0:T(8,128)}, u32[]{:S(2)}) %copy-start.3) | copy-done | bytes 1769496
  45.1 7.0 %shard_map.56 = (f32[4,24,4608]{2,1,0:T(8,128)S(1)}, bf16[3,48,4608]{2,1,0:T(8,128)(2,1)S(1)}, bf16[3,48,4608]{2,1,0:T(8,128)(2,1)S(1)}) custom-call(f32[2]{0:T(128)S(1)} %add_convert_fusion.inside, bf16[3,48,4608]{2,1,0:T(8,128)(2,1)S(1)} %collective-permute-done.below, f32[4,24,4608]{2,1,0:T(8,128)S(1)} %copy-done.3, ...), custom_call_target="tpu_custom_call" | custom-call | flops 8847360000 | bytes 7077888 | tf_op jit(solution)/shard_map/pallas_call | solution.py:250
  52.2 3.4 %collective-permute-start.4 = (bf16[3,48,4608]{2,1,0:T(8,128)(2,1)S(1)}, bf16[3,48,4608]{2,1,0:T(8,128)(2,1)S(1)}, u32[]{:S(2)}, u32[]{:S(2)}) collective-permute-start(bf16[3,48,4608]{2,1,0:T(8,128)(2,1)S(1)} %get-tuple-element.14), channel_id=1, source_target_pairs={{0,16},{16,32},{32,48},{48,64},{64,80},{80,96},{96,112},{112,128},... | collective-permute-start | bytes 3981320 | tf_op jit(solution)/shard_map/ppermute | solution.py:306
  55.5 1.9 %collective-permute-start.5 = (bf16[3,48,4608]{2,1,0:T(8,128)(2,1)S(1)}, bf16[3,48,4608]{2,1,0:T(8,128)(2,1)S(1)}, u32[]{:S(2)}, u32[]{:S(2)}) collective-permute-start(bf16[3,48,4608]{2,1,0:T(8,128)(2,1)S(1)} %get-tuple-element.16), channel_id=1, source_target_pairs={{16,0},{32,16},{48,32},{64,48},{80,64},{96,80},{112,96},{128,112},... | collective-permute-start | bytes 3981320 | tf_op jit(solution)/shard_map/ppermute | solution.py:306
  57.5 12.8 %collective-permute-done.4.below = bf16[3,48,4608]{2,1,0:T(8,128)(2,1)S(1)} collective-permute-done((bf16[3,48,4608]{2,1,0:T(8,128)(2,1)S(1)}, bf16[3,48,4608]{2,1,0:T(8,128)(2,1)S(1)}, u32[]{:S(2)}, u32[]{:S(2)}) %collective-permute-start.4) | collective-permute-done | bytes 1327136 | tf_op jit(solution)/shard_map/ppermute | solution.py:306
  70.2 8.0 %collective-permute-done.5.above = bf16[3,48,4608]{2,1,0:T(8,128)(2,1)S(1)} collective-permute-done((bf16[3,48,4608]{2,1,0:T(8,128)(2,1)S(1)}, bf16[3,48,4608]{2,1,0:T(8,128)(2,1)S(1)}, u32[]{:S(2)}, u32[]{:S(2)}) %collective-permute-start.5) | collective-permute-done | bytes 1327136 | tf_op jit(solution)/shard_map/ppermute | solution.py:306
  78.2 8.3 %shard_map.57 = f32[16,24,1152]{2,1,0:T(8,128)S(1)} custom-call(f32[2]{0:T(128)S(1)} %add_convert_fusion.inside, bf16[3,48,4608]{2,1,0:T(8,128)(2,1)S(1)} %collective-permute-done.4.below, f32[4,24,4608]{2,1,0:T(8,128)S(1)} %get-tuple-element.15.own, bf16[3,48,4608]{2,1,0:T(8,128)(2,1)S(1)} %collective-permute-done.5.above, ...), custom_call_target="tpu_custom_call" | custom-call | flops 8847360000 | bytes 7077888 | tf_op jit(solution)/shard_map/pallas_call | solution.py:250
  86.6 0.0 copy-start.4
  86.6 1.0 convert_element_type.19
  87.6 0.0 copy-start
  87.6 8.5 %all-to-all-start = ((bf16[16,24,1152]{2,1,0:T(8,128)(2,1)}), bf16[16,24,1152]{2,1,0:T(8,128)(2,1)S(1)}, u32[]{:S(2)}, u32[]{:S(2)}) async-start(bf16[16,24,1152]{2,1,0:T(8,128)(2,1)} %convert_element_type.19), calls=%async_computation | async-start | bytes 1769472 | tf_op jit(solution)/shard_map/all_to_all | solution.py:322
  96.1 0.0 copy-done.4
  96.1 0.2 copy.10
  96.3 17.8 %all-to-all-done = bf16[16,24,1152]{2,1,0:T(8,128)(2,1)S(1)} async-done(((bf16[16,24,1152]{2,1,0:T(8,128)(2,1)}), bf16[16,24,1152]{2,1,0:T(8,128)(2,1)S(1)}, u32[]{:S(2)}, u32[]{:S(2)}) %all-to-all-start) | async-done | bytes 884768 | tf_op jit(solution)/shard_map/all_to_all | solution.py:322
  114.1 0.0 copy-done
  114.1 1.4 shard_map.58
  115.5 26.5 %all_to_all.10 = bf16[16,24,1152]{2,1,0:T(8,128)(2,1)S(1)} all-to-all(bf16[16,24,1152]{2,1,0:T(8,128)(2,1)S(1)} %bitcast.16), channel_id=1, replica_groups=mesh['space'=16,'band'=16] {'band'}, dimensions={0} | all-to-all | bytes 1769472 | tf_op jit(solution)/shard_map/all_to_all | solution.py:325
  142.0 0.3 copy.18
  142.3 2.2 %reshape.24 = f32[24,4,4608]{2,1,0:T(4,128)} reshape(f32[24,4,4,1152]{3,2,1,0:T(4,128)S(1)} %bitcast.20) | data formatting | bytes 3538944 | tf_op jit(solution)/shard_map/convert_element_type | solution.py:327
Async XLA Ops:
  0.0 2.1 %copy-start.1 = (bf16[384,384]{1,0:T(8,128)(2,1)S(1)}, bf16[384,384]{1,0:T(8,128)(2,1)}, u32[]{:S(2)}) copy-start(bf16[384,384]{1,0:T(8,128)(2,1)} %constant.14.order) | copy-start | bytes 884740
  2.1 12.1 %copy-start.5 = (f32[4,4608]{1,0:T(4,128)S(1)}, f32[4,4608]{1,0:T(4,128)}, u32[]{:S(2)}) copy-start(f32[4,4608]{1,0:T(4,128)} %param.6) | copy-start | bytes 221188
  6.2 1.2 copy-start.2
  7.4 36.2 %collective-permute-start = (bf16[3,48,4608]{2,1,0:T(8,128)(2,1)}, bf16[3,48,4608]{2,1,0:T(8,128)(2,1)S(1)}, u32[]{:S(2)}, u32[]{:S(2)}) collective-permute-start(bf16[3,48,4608]{2,1,0:T(8,128)(2,1)} %get-tuple-element.11), channel_id=1, source_target_pairs={{0,16},{16,32},{32,48},{48,64},{64,80},{80,96},{96,112},{112,128},... | collective-permute-start | bytes 3981320 | tf_op jit(solution)/shard_map/ppermute | solution.py:306
  12.3 31.3 %collective-permute-start.1 = (bf16[3,48,4608]{2,1,0:T(8,128)(2,1)S(1)}, bf16[3,48,4608]{2,1,0:T(8,128)(2,1)}, u32[]{:S(2)}, u32[]{:S(2)}) collective-permute-start(bf16[3,48,4608]{2,1,0:T(8,128)(2,1)S(1)} %get-tuple-element.13), channel_id=1, source_target_pairs={{16,0},{32,16},{48,32},{64,48},{80,64},{96,80},{112,96},{128,112},... | collective-permute-start | bytes 3981320 | tf_op jit(solution)/shard_map/ppermute | solution.py:306
  25.2 14.4 %collective-permute-start.2 = (f32[2,4608]{1,0:T(2,128)S(1)}, f32[2,4608]{1,0:T(2,128)S(1)}, u32[]{:S(2)}, u32[]{:S(2)}) collective-permute-start(f32[2,4608]{1,0:T(2,128)S(1)} %slice.13), channel_id=1, source_target_pairs={{0,16},{16,32},{32,48},{48,64},{64,80},{80,96},{96,112},{112,128},... | collective-permute-start | bytes 110600 | tf_op jit(solution)/shard_map/ppermute | solution.py:315
  34.7 8.9 %collective-permute-start.3 = (f32[2,4608]{1,0:T(2,128)S(1)}, f32[2,4608]{1,0:T(2,128)S(1)}, u32[]{:S(2)}, u32[]{:S(2)}) collective-permute-start(f32[2,4608]{1,0:T(2,128)S(1)} %slice.15), channel_id=1, source_target_pairs={{16,0},{32,16},{48,32},{64,48},{80,64},{96,80},{112,96},{128,112},... | collective-permute-start | bytes 110600 | tf_op jit(solution)/shard_map/ppermute | solution.py:316
  43.6 1.5 %copy-start.3 = (f32[4,24,4608]{2,1,0:T(8,128)S(1)}, f32[4,24,4608]{2,1,0:T(8,128)}, u32[]{:S(2)}) copy-start(f32[4,24,4608]{2,1,0:T(8,128)} %copy-done.2) | copy-start | bytes 5308420
  52.2 18.1 %collective-permute-start.4 = (bf16[3,48,4608]{2,1,0:T(8,128)(2,1)S(1)}, bf16[3,48,4608]{2,1,0:T(8,128)(2,1)S(1)}, u32[]{:S(2)}, u32[]{:S(2)}) collective-permute-start(bf16[3,48,4608]{2,1,0:T(8,128)(2,1)S(1)} %get-tuple-element.14), channel_id=1, source_target_pairs={{0,16},{16,32},{32,48},{48,64},{64,80},{80,96},{96,112},{112,128},... | collective-permute-start | bytes 3981320 | tf_op jit(solution)/shard_map/ppermute | solution.py:306
  55.5 22.7 %collective-permute-start.5 = (bf16[3,48,4608]{2,1,0:T(8,128)(2,1)S(1)}, bf16[3,48,4608]{2,1,0:T(8,128)(2,1)S(1)}, u32[]{:S(2)}, u32[]{:S(2)}) collective-permute-start(bf16[3,48,4608]{2,1,0:T(8,128)(2,1)S(1)} %get-tuple-element.16), channel_id=1, source_target_pairs={{16,0},{32,16},{48,32},{64,48},{80,64},{96,80},{112,96},{128,112},... | collective-permute-start | bytes 3981320 | tf_op jit(solution)/shard_map/ppermute | solution.py:306
  86.6 9.5 %copy-start.4 = (bf16[384,384]{1,0:T(8,128)(2,1)S(1)}, bf16[384,384]{1,0:T(8,128)(2,1)}, u32[]{:S(2)}) copy-start(bf16[384,384]{1,0:T(8,128)(2,1)} %param.7) | copy-start | bytes 884740
  87.6 26.5 %copy-start = (bf16[384,384]{1,0:T(8,128)(2,1)S(1)}, bf16[384,384]{1,0:T(8,128)(2,1)}, u32[]{:S(2)}) copy-start(bf16[384,384]{1,0:T(8,128)(2,1)} %constant.11.clone.order) | copy-start | bytes 884740
  87.6 26.5 %all-to-all-start = ((bf16[16,24,1152]{2,1,0:T(8,128)(2,1)}), bf16[16,24,1152]{2,1,0:T(8,128)(2,1)S(1)}, u32[]{:S(2)}, u32[]{:S(2)}) async-start(bf16[16,24,1152]{2,1,0:T(8,128)(2,1)} %convert_element_type.19), calls=%async_computation | async-start | bytes 1769472 | tf_op jit(solution)/shard_map/all_to_all | solution.py:322

commit v4 on v3

v4 whole, which is shorter than its diff:
```python
import functools

import jax
import jax.numpy as jnp
import numpy as np
from jax import lax
from jax.experimental import pallas as pl
from jax.experimental.pallas import tpu as pltpu
from jax.sharding import PartitionSpec as P

NY = 48
NZ = 96
LANE = 128
ROWS = 8
GROUPS = 4
RUNS = NY // GROUPS
ZI = 3
ZB = NZ // ZI
PIECES = RUNS * ZI
ROW_BLOCK = GROUPS * NZ
VMEM_LIMIT = 18 * 1024 * 1024
CHUNKS = (16, 8)

CENTER = 4.75
HALF_WIDTH = 3.75
NEAR = -2.0 / 3.0 / HALF_WIDTH
FAR = 1.0 / 24.0 / HALF_WIDTH


def lanes_of(rows):
    return lax.broadcasted_iota(jnp.int32, (rows, LANE), 1)


def piece(j):
    return pl.ds(j * LANE, LANE)


def split_groups(four, odd, upper):
    half = {}
    for i in (0, 2):
        half[i] = jnp.where(odd, pltpu.roll(four[i + 1], ZB, 1), four[i])
        half[i + 1] = jnp.where(odd, four[i + 1], pltpu.roll(four[i], LANE - ZB, 1))
    done = {}
    for i in (0, 1):
        done[i] = jnp.where(upper, pltpu.roll(half[i + 2], 2 * ZB, 1), half[i])
        done[i + 2] = jnp.where(upper, half[i + 2], pltpu.roll(half[i], 2 * ZB, 1))
    return done


def rounded(x):
    return x.astype(jnp.bfloat16).astype(jnp.float32)


def pack_halo(planes, odd, to_mate, to_other):
    base = pl.program_id(0) * 3
    for to, upward in ((to_mate, 1 - odd), (to_other, odd)):
        near, next_near, far, farthest = [jnp.where(upward == 1, 3 - k, k) for k in range(4)]
        for j in range(PIECES):
            for i, p in enumerate((near, next_near)):
                x = planes[p, :, piece(j)]
                to[base + i, :, piece(j)] = jnp.concatenate([x, x - rounded(x)], axis=0).astype(jnp.bfloat16)
            both = jnp.concatenate([planes[far, :, piece(j)], planes[farthest, :, piece(j)]], axis=0)
            to[base + 2, :, piece(j)] = both.astype(jnp.bfloat16)


def unpack_halo(halo, below, field):
    base = pl.program_id(0) * 3
    near, next_near, far, farthest = [jnp.where(below == 1, 3 - k, 8 + k) for k in range(4)]
    columns = field.shape[2]
    for at in range(0, columns, ROW_BLOCK):
        lanes = pl.ds(at, ROW_BLOCK)
        for i, p in enumerate((near, next_near)):
            both = halo[base + i, :, lanes].astype(jnp.float32)
            field[p, :, lanes] = both[:ROWS] + both[ROWS:]
        both = halo[base + 2, :, lanes].astype(jnp.float32)
        field[far, :, lanes] = both[:ROWS]
        field[farthest, :, lanes] = both[ROWS:]


def halo_shape(count, columns, extra=0):
    return jax.ShapeDtypeStruct((count // ROWS * 3 + extra, 2 * ROWS, columns), jnp.bfloat16)


def whole_spec(shape):
    return pl.BlockSpec(shape, lambda i: (0,) * len(shape))


def split_terms(x, terms, at):
    first = rounded(x)
    second = rounded(x - first)
    terms[0, at] = first.astype(jnp.bfloat16)
    terms[1, at] = second.astype(jnp.bfloat16)
    terms[2, at] = (x - first - second).astype(jnp.bfloat16)


def reordered(terms, order):
    parts = [jnp.dot(terms[i], order[...], preferred_element_type=jnp.float32) for i in range(3)]
    return parts[0] + (parts[1] + parts[2])


def potential_to_runs(cells, odd, order, out, to_mate, to_other, gathered, terms):
    planes, columns = cells.shape
    blocks = columns // ROW_BLOCK
    at_row = lax.broadcasted_iota(jnp.int32, (ROWS, LANE), 0)
    for k in range(blocks):
        x = cells[:, pl.ds(k * ROW_BLOCK, ROW_BLOCK)]
        gathered[pl.ds(k * ROWS, ROWS), :] = jnp.concatenate([x, jnp.zeros_like(x)], axis=0)
    split_terms(gathered[...], terms, pl.ds(0, blocks * ROWS))
    gathered[...] = reordered(terms, order)
    group = lanes_of(ROWS) // ZB
    per_group = blocks // GROUPS
    for m in range(PIECES // GROUPS):
        four = [gathered[pl.ds((a * per_group + m // ZI) * ROWS, ROWS), piece(m % ZI)] for a in range(GROUPS)]
        done = split_groups(four, group % 2 == 1, group >= 2)
        for i in range(GROUPS):
            x = done[i]
            j = GROUPS * m + i
            out[:, piece(j)] = x[:planes]
            for to, upward in ((to_mate, 1 - odd), (to_other, odd)):
                near = jnp.where(upward == 1, x[planes - 1 : planes], x[0:1])
                next_near = jnp.where(upward == 1, x[planes - 2 : planes - 1], x[1:2])
                rows = [near, near - rounded(near), next_near, next_near - rounded(next_near)]
                total = jnp.zeros((ROWS, LANE), jnp.float32)
                for r, row in enumerate(rows):
                    total = jnp.where(at_row == r, row, total)
                total = jnp.concatenate([total, jnp.zeros_like(total)], axis=0)
                to[to.shape[0] - 1, :, piece(j)] = total.astype(jnp.bfloat16)


def to_runs_kernel(extra, place, cells, *rest):
    if extra:
        potential, out, to_mate, to_other, runs, order, terms, turned, gathered, few_terms = rest
    else:
        out, to_mate, to_other, order, terms, turned = rest
    planes, rows, columns = out.shape
    blocks = columns // ROW_BLOCK

    @pl.when(pl.program_id(0) == 0)
    def _():
        to = lax.broadcasted_iota(jnp.int32, order.shape, 1)
        source = to // NZ * NZ + to % ZB * ZI + to % NZ // ZB
        order[...] = jnp.where(lax.broadcasted_iota(jnp.int32, order.shape, 0) == source, 1.0, 0.0).astype(jnp.bfloat16)
        if extra:
            potential_to_runs(potential, place[2], order, runs, to_mate, to_other, gathered, few_terms)

    for k in range(blocks):
        x = cells[:, :, pl.ds(k * ROW_BLOCK, ROW_BLOCK)].reshape(rows * planes, ROW_BLOCK)
        split_terms(x, terms, pl.ds(k * rows * planes, rows * planes))
    whole = reordered(terms, order)
    for zi in range(ZI):
        turned[zi] = whole[:, zi * LANE : (zi + 1) * LANE]

    group = lanes_of(rows) // ZB
    odd = group % 2 == 1
    upper = group >= 2
    per_group = blocks // GROUPS
    for m in range(PIECES // GROUPS):
        for p in range(planes):
            four = []
            for a in range(GROUPS):
                k = a * per_group + m // ZI
                four.append(turned[m % ZI, pl.ds(k * rows * planes + p, rows, stride=planes), :])
            done = split_groups(four, odd, upper)
            for i in range(GROUPS):
                out[p, :, piece(GROUPS * m + i)] = done[i]
    pack_halo(out, place[2], to_mate, to_other)


def to_runs(place, cells, start, count, potential=None):
    _, planes, columns = cells.shape
    extra = potential is not None
    halo = halo_shape(count, columns, int(extra))
    blocks = columns // ROW_BLOCK
    total = planes * ROWS * blocks
    scratch = [
        pltpu.VMEM((ROW_BLOCK, ROW_BLOCK), jnp.bfloat16),
        pltpu.VMEM((3, total, ROW_BLOCK), jnp.bfloat16),
        pltpu.VMEM((ZI, total, LANE), jnp.float32),
    ]
    if extra:
        scratch.append(pltpu.VMEM((blocks * ROWS, ROW_BLOCK), jnp.float32))
        scratch.append(pltpu.VMEM((3, blocks * ROWS, ROW_BLOCK), jnp.bfloat16))
    return pl.pallas_call(
        functools.partial(to_runs_kernel, extra),
        grid=(count // ROWS,),
        in_specs=[
            pl.BlockSpec(memory_space=pltpu.SMEM),
            pl.BlockSpec((ROWS, planes, columns), lambda i: (start // ROWS + i, 0, 0)),
        ]
        + [whole_spec((planes, columns))] * extra,
        out_specs=[pl.BlockSpec((planes, ROWS, columns), lambda i: (0, i, 0))]
        + [whole_spec(halo.shape)] * 2
        + [whole_spec((planes, columns))] * extra,
        out_shape=[pltpu.HBM((planes, count, columns), cells.dtype), halo, halo]
        + [jax.ShapeDtypeStruct((planes, columns), jnp.float32)] * extra,
        scratch_shapes=scratch,
        compiler_params=pltpu.CompilerParams(vmem_limit_bytes=VMEM_LIMIT),
        cost_estimate=pl.CostEstimate(flops=1, bytes_accessed=1, transcendentals=0),
    )(place, cells, *([potential] if extra else []))


def stencil_row(src, plane, masks, emit):
    a_last, a_first, zb_last, zb_first = masks
    centers, turned = {}, {}

    def center(b, zi):
        if (b, zi) not in centers:
            centers[b, zi] = src[plane + 2, :, piece(ZI * b + zi)]
        return centers[b, zi]

    def turn(b, zi, by, mask):
        if (b, zi, by) not in turned:
            turned[b, zi, by] = jnp.where(mask, 0.0, pltpu.roll(center(b, zi), by, 1))
        return turned[b, zi, by]

    def at_y(b, zi):
        if b < 0:
            return turn(b + RUNS, zi, ZB, a_first)
        if b >= RUNS:
            return turn(b - RUNS, zi, LANE - ZB, a_last)
        return center(b, zi)

    def at_z(b, zi):
        if zi < 0:
            return turn(b, zi + ZI, 1, zb_first)
        if zi >= ZI:
            return turn(b, zi - ZI, LANE - 1, zb_last)
        return center(b, zi)

    def at_x(j, k):
        return src[plane + 2 + k, :, piece(j)]

    for b in range(RUNS):
        for zi in range(ZI):
            j = ZI * b + zi
            near, far = [
                (at_x(j, -k) + at_x(j, k)) + (at_y(b - k, zi) + at_y(b + k, zi)) + (at_z(b, zi - k) + at_z(b, zi + k))
                for k in (1, 2)
            ]
            emit(j, center(b, zi), near, far)


def potential_field_kernel(place, from_mate, own, from_other, out):
    planes = own.shape[0]

    def scale(x):
        return (x + (HALF_WIDTH - CENTER)) / HALF_WIDTH

    out[2 : planes + 2] = scale(own[...])
    mate, other = [halo[0].astype(jnp.float32) for halo in (from_mate, from_other)]
    mate_below = place[2] == 1
    below = jnp.where(mate_below, mate, other)
    above = jnp.where(mate_below, other, mate)
    out[1:2] = scale(below[0:1] + below[1:2])
    out[0:1] = scale(below[2:3] + below[3:4])
    out[planes + 2 : planes + 3] = scale(above[0:1] + above[1:2])
    out[planes + 3 : planes + 4] = scale(above[2:3] + above[3:4])


def potential_field(place, halo, own):
    planes, columns = own.shape
    specs = [pl.BlockSpec((1,) + x.shape[1:], lambda i, n=x.shape[0]: (n - 1, 0, 0)) for x in halo]
    return pl.pallas_call(
        potential_field_kernel,
        grid=(1,),
        in_specs=[pl.BlockSpec(memory_space=pltpu.SMEM), specs[0], whole_spec(own.shape), specs[1]],
        out_specs=whole_spec((planes + 4, columns)),
        out_shape=jax.ShapeDtypeStruct((planes + 4, columns), jnp.float32),
        compiler_params=pltpu.CompilerParams(vmem_limit_bytes=VMEM_LIMIT),
    )(place, halo[0], own, halo[1])


def two_steps_kernel(last, count_done, *refs):
    done = refs[:count_done]
    place, from_mate, own, from_other, potential, *rest = refs[count_done:]
    if last:
        first, out, field, inner, diag, held_all = rest
    else:
        out, to_mate, to_other, field, inner, diag = rest
    planes, rows, columns = own.shape

    @pl.when(pl.program_id(0) == 0)
    def _():
        for p in range(planes + 4):
            diag[p] = jnp.broadcast_to(potential[p : p + 1, :], (rows, columns))

    unpack_halo(from_mate, place[2], field)
    field[planes : 2 * planes] = own[...]
    unpack_halo(from_other, 1 - place[2], field)

    lane = lanes_of(rows)
    masks = (lane >= LANE - ZB, lane < ZB, lane % ZB == ZB - 1, lane % ZB == 0)
    odd = lane // ZB % 2 == 1
    upper = lane >= 2 * ZB

    def first_stage(p, _):
        here = jnp.where(p < 2, place[0], jnp.where(p >= planes + 2, place[1], 1)).astype(jnp.float32)
        near_by = here * NEAR
        far_by = here * FAR

        def emit(j, center, near, far):
            inner[p, :, piece(j)] = diag[p, :, piece(j)] * center + near_by * near + far_by * far

        stencil_row(field, p + planes - 4, masks, emit)
        return 0

    lax.fori_loop(0, planes + 4, first_stage, 0)

    own_rows = pl.ds(pl.multiple_of(pl.program_id(0) * rows, rows), rows)

    def second_stage(p, _):
        held = []

        def emit(j, center, near, far):
            total = diag[p + 2, :, piece(j)] * center + NEAR * near + FAR * far
            total = 2.0 * total - field[p + planes, :, piece(j)]
            if not last:
                out[p, :, piece(j)] = total
                return
            held.append(2.0 * total - first[p, :, piece(j)])
            if len(held) == GROUPS:
                done = split_groups(held, odd, upper)
                for a in range(GROUPS):
                    held_all[GROUPS * p + a, own_rows, piece(j // GROUPS)] = done[a]
                held.clear()

        stencil_row(inner, p, masks, emit)
        return 0

    lax.fori_loop(0, planes, second_stage, 0)
    if not last:
        pack_halo(out, place[2], to_mate, to_other)
        return

    @pl.when(pl.program_id(0) == pl.num_programs(0) - 1)
    def _():
        def one_part(i, _):
            both = [x[i].astype(jnp.float32) for x in done] + [held_all[i]]
            out[i] = jnp.concatenate(both, axis=0).astype(jnp.bfloat16)
            return 0

        lax.fori_loop(0, out.shape[0], one_part, 0)


def two_steps(place, halo, own, potential, first=None, done=()):
    planes, count, columns = own.shape
    last = first is not None
    spec = pl.BlockSpec((planes, ROWS, columns), lambda i: (0, i, 0))
    near = halo_shape(count, columns)
    out_shape = [jax.ShapeDtypeStruct(own.shape, own.dtype), near, near]
    out_spec = [spec, whole_spec(near.shape), whole_spec(near.shape)]
    scratch = [
        pltpu.VMEM((planes * 3, ROWS, columns), jnp.float32),
        pltpu.VMEM((planes + 4, ROWS, columns), jnp.float32),
        pltpu.VMEM((planes + 4, ROWS, columns), jnp.float32),
    ]
    if last:
        shape = (planes * GROUPS, count, columns // GROUPS)
        scratch.append(pltpu.VMEM(shape, jnp.float32))
        shape = (planes * GROUPS, count + sum(x.shape[1] for x in done), columns // GROUPS)
        out_shape = jax.ShapeDtypeStruct(shape, jnp.bfloat16)
        out_spec = pl.BlockSpec(shape, lambda i: (0, 0, 0))
    return pl.pallas_call(
        functools.partial(two_steps_kernel, last, len(done)),
        grid=(count // ROWS,),
        in_specs=[whole_spec(x.shape) for x in done]
        + [pl.BlockSpec(memory_space=pltpu.SMEM)]
        + [whole_spec(halo[0].shape), spec, whole_spec(halo[1].shape), whole_spec(potential.shape)]
        + [spec] * last,
        out_specs=out_spec,
        out_shape=out_shape,
        scratch_shapes=scratch,
        compiler_params=pltpu.CompilerParams(vmem_limit_bytes=VMEM_LIMIT),
        cost_estimate=pl.CostEstimate(flops=1, bytes_accessed=1, transcendentals=0),
    )(*done, place, halo[0], own, halo[1], potential, *([first] if last else []))


def z_order():
    one = np.zeros((NZ, NZ), np.float32)
    for z in range(NZ):
        one[z % ZI * ZB + z // ZI, z] = 1.0
    return jnp.asarray(np.kron(np.eye(GROUPS, dtype=np.float32), one), jnp.bfloat16)


def rotate_kernel(weights, cells, order, out):
    for k in range(cells.shape[1] // ROW_BLOCK):
        at = pl.ds(k * ROW_BLOCK, ROW_BLOCK)
        summed = jnp.dot(weights[...], cells[:, at], preferred_element_type=jnp.float32).astype(jnp.bfloat16)
        out[:, at] = jnp.dot(summed, order[...], preferred_element_type=jnp.float32).astype(jnp.bfloat16)


def rotate(weights, cells):
    return pl.pallas_call(
        rotate_kernel,
        out_shape=jax.ShapeDtypeStruct((weights.shape[0], cells.shape[1]), jnp.bfloat16),
        compiler_params=pltpu.CompilerParams(vmem_limit_bytes=VMEM_LIMIT),
        cost_estimate=pl.CostEstimate(flops=1, bytes_accessed=1, transcendentals=0),
    )(weights, cells, z_order())


def from_parts_kernel(parts, out, mixed):
    rows, planes, columns = out.shape
    width = parts.shape[2]
    groups = columns // width
    for p in range(planes):
        for a in range(groups):
            x = parts[p * groups + a].astype(jnp.float32)
            for j in range(width // LANE):
                for o in range(0, rows, ROWS):
                    at = pl.ds(o * planes + p, ROWS, stride=planes)
                    mixed[a * (width // LANE) + j, at, :] = x[o : o + ROWS, j * LANE : (j + 1) * LANE]
    for j in range(columns // LANE):
        out[:, :, piece(j)] = mixed[j].reshape(rows, planes, LANE)


def from_parts(parts, planes):
    n, count, width = parts.shape
    columns = n // planes * width
    return pl.pallas_call(
        from_parts_kernel,
        grid=(1,),
        in_specs=[pl.BlockSpec(parts.shape, lambda i: (0, 0, 0))],
        out_specs=pl.BlockSpec((count, planes, columns), lambda i: (0, 0, 0)),
        out_shape=jax.ShapeDtypeStruct((count, planes, columns), jnp.float32),
        scratch_shapes=[pltpu.VMEM((columns // LANE, count * planes, LANE), jnp.float32)],
        compiler_params=pltpu.CompilerParams(vmem_limit_bytes=VMEM_LIMIT),
        cost_estimate=pl.CostEstimate(flops=1, bytes_accessed=1, transcendentals=0),
    )(parts)


def body(orbitals, potential, rotation):
    count, planes, columns = orbitals.shape
    domains = lax.axis_size("space")
    members = lax.axis_size("band")
    mates = [(i, i ^ 1) for i in range(domains)]
    others = [(i, i + 1) for i in range(1, domains - 1, 2)]
    others = others + [(j, i) for i, j in others]

    def around(to_mate, to_other):
        other = lax.ppermute(to_other, "space", others)
        return lax.ppermute(to_mate, "space", mates), other

    at = lax.axis_index("space")
    place = jnp.stack([at > 0, at < domains - 1, at % 2]).astype(jnp.int32)

    orbitals = pltpu.with_memory_space_constraint(orbitals, pltpu.HBM)
    starts = [sum(CHUNKS[:i]) for i in range(len(CHUNKS))]
    zeroth, halos = [], []
    for i, (start, chunk) in enumerate(zip(starts, CHUNKS)):
        fields, *halo = to_runs(place, orbitals, start, chunk, potential if i == 0 else None)
        if i == 0:
            field = halo.pop()
        zeroth.append(fields)
        halos.append(around(*halo))

    second, next_halos = [], []
    fields_0, waited = lax.optimization_barrier((zeroth[0], halos[1][0]))
    halos[1] = (waited, halos[1][1])
    field = potential_field(place, halos[0], field)
    fields, *halo = two_steps(place, halos[0], fields_0, field)
    second.append(fields)
    next_halos.append(around(*halo))
    fields_1 = zeroth[1]
    fields, *halo = two_steps(place, halos[1], fields_1, field)
    second.append(fields)
    next_halos.append(around(*halo))
    filtered = ()
    for fields, halo, first in zip(second, next_halos, zeroth):
        filtered = (two_steps(place, halo, fields, field, first, filtered),)
    filtered, = filtered
    gathered = lax.all_to_all(filtered, "band", 0, 0)
    width = columns // GROUPS
    summed = rotate(rotation.T, gathered.reshape(members * count, width))
    back = lax.all_to_all(summed.reshape(members, count, width), "band", 0, 0)
    return from_parts(back, planes)


def solution(mesh):
    return jax.shard_map(
        body,
        mesh=mesh,
        in_specs=(P("band", "space", None), P("space", None), P()),
        out_specs=P("band", "space", None),
        check_vma=False,
    )
```

time: 145 us -> 123 us (0.85)
  local copies, waits for them, and re-layouts: 23.7 us -> 1.12 us
  Pallas kernels: 20.9 us -> 29.6 us
  waiting for transfers between devices: 42.5 us -> 34.1 us
  blocking collectives: 26.5 us -> 28.4 us
    ppermute x6 -> x8, waiting for transfers between devices: 24.7 us -> 13.2 us  [the longest x4 13.2 us: around(): other = lax.ppermute(to_other, 'space', others)]
    pallas_call x3 -> x8, Pallas kernels: 19.5 us -> 28.2 us  [the longest x4 17.2 us: two_steps(): pl.pallas_call(functools.partial(two_steps_kernel, last, len(done)), grid...]
    slice x5 -> x0, local copies, waits for them, and re-layouts: 8.4 us -> none  [the longest x3 6.19 us: body(): potential_below = lax.ppermute(runs[planes - 2:], 'space', up)]
    reshape x2 -> x0, local copies, waits for them, and re-layouts: 4.99 us -> none  [body(): potential.reshape(planes, GROUPS, RUNS, ZB, ZI).transpose(0, 2, 4, 1, 3)]
    unnamed x14 -> x11, local copies, waits for them, and re-layouts: 5.01 us -> 1.12 us
    all_to_all x1, waiting for transfers between devices: 17.8 us -> 20.9 us  [body(): gathered = lax.all_to_all(filtered, 'band', 0, 0)]
    transpose x1 -> x0, local copies, waits for them, and re-layouts: 2.71 us -> none  [body(): potential.reshape(planes, GROUPS, RUNS, ZB, ZI).transpose(0, 2, 4, 1, 3)]
    convert_element_type x2 -> x0, local copies, waits for them, and re-layouts: 2.56 us -> none  [body(): return back.reshape(count, planes, columns).astype(jnp.float32)]
  transfers between devices with their start and end apart: 7 -> 9, of which waited for: 4 -> 3; matrix products, arithmetic and copies ran while one was open for 11% -> 0% of each run, Pallas kernels for 0% -> 14%
where the time goes in v4:
time: 123 us; the launch traced here: 122 us
  waiting for transfers between devices  34.1 us (28%)
  Pallas kernels  29.6 us (24%)
  starting transfers between devices  28.7 us (23%)
  blocking collectives  28.4 us (23%)
    all_to_all x1, blocking collectives, body(): back = lax.all_to_all(summed.reshape(members, count, width), 'band', 0, 0)  28.4 us
    all_to_all x1, waiting for transfers between devices, body(): gathered = lax.all_to_all(filtered, 'band', 0, 0)  20.9 us
    ppermute x4, starting transfers between devices, around(): other = lax.ppermute(to_other, 'space', others)  18.5 us
    pallas_call x4, Pallas kernels, two_steps(): pl.pallas_call(functools.partial(two_steps_kernel, last, len(done)), grid...  17.2 us
    ppermute x4, waiting for transfers between devices, around(): other = lax.ppermute(to_other, 'space', others)  13.2 us
    all_to_all x1, starting transfers between devices, body(): gathered = lax.all_to_all(filtered, 'band', 0, 0)  9.34 us
    pallas_call x2, Pallas kernels, to_runs(): pl.pallas_call(functools.partial(to_runs_kernel, extra), grid=(count // R...  8.57 us
  transfers between devices with their start and end apart: 9, of which 3 were waited for; matrix products, arithmetic and copies ran while one was open for 0% of the time, Pallas kernels for 14%

profile of v4, /device:TPU:25, one launch (start us, length us, event | category | flops | bytes accessed | tf_op | source)
XLA Modules:
  0.0 122.1 jit_solution(6731343105420786152)
XLA Ops:
  0.0 0.1 pad_add_fusion.place.refs_0_.refs_1_
  0.1 0.0 copy-start.3
  0.1 0.9 copy-done.3
  1.0 5.3 %shard_map.46 = (f32[4,16,4608]{2,1,0:T(8,128)}, bf16[7,16,4608]{2,1,0:T(8,128)(2,1)S(1)}, bf16[7,16,4608]{2,1,0:T(8,128)(2,1)S(1)}, f32[4,4608]{1,0:T(4,128)S(1)}) custom-call(s32[3]{0:T(128)S(1)} %pad_add_fusion.place.refs_0_.refs_1_, f32[24,4,4608]{2,1,0:T(4,128)} %cells.3, f32[4,4608]{1,0:T(4,128)S(1)} %copy-done.3), custom_call_target="tpu_custom_call" | custom-call | flops 1 | bytes 1 | tf_op jit(solution)/shard_map/pallas_call | solution.py:183
  6.2 0.7 collective-permute-start
  6.9 0.0 copy-start
  6.9 4.3 %collective-permute-start.2 = (bf16[7,16,4608]{2,1,0:T(8,128)(2,1)S(1)}, bf16[7,16,4608]{2,1,0:T(8,128)(2,1)S(1)}, u32[]{:S(2)}, u32[]{:S(2)}) collective-permute-start(bf16[7,16,4608]{2,1,0:T(8,128)(2,1)S(1)} %get-tuple-element.24), channel_id=1, source_target_pairs={{16,32},{48,64},{80,96},{112,128},{144,160},{176,192},{208,224},{3... | collective-permute-start | bytes 3096584 | tf_op jit(solution)/shard_map/ppermute | solution.py:440
  11.3 3.3 %shard_map.47 = (f32[4,8,4608]{2,1,0:T(8,128)}, bf16[3,16,4608]{2,1,0:T(8,128)(2,1)S(1)}, bf16[3,16,4608]{2,1,0:T(8,128)(2,1)S(1)}) custom-call(s32[3]{0:T(128)S(1)} %pad_add_fusion.place.refs_0_.refs_1_, f32[24,4,4608]{2,1,0:T(4,128)} %cells.3), custom_call_target="tpu_custom_call" | custom-call | flops 1 | bytes 1 | tf_op jit(solution)/shard_map/pallas_call | solution.py:183
  14.6 0.0 collective-permute-start.1
  14.6 5.0 %collective-permute-start.5 = (bf16[3,16,4608]{2,1,0:T(8,128)(2,1)S(1)}, bf16[3,16,4608]{2,1,0:T(8,128)(2,1)S(1)}, u32[]{:S(2)}, u32[]{:S(2)}) collective-permute-start(bf16[3,16,4608]{2,1,0:T(8,128)(2,1)S(1)} %get-tuple-element.31), channel_id=1, source_target_pairs={{16,32},{48,64},{80,96},{112,128},{144,160},{176,192},{208,224},{3... | collective-permute-start | bytes 1327112 | tf_op jit(solution)/shard_map/ppermute | solution.py:440
  19.5 0.0 collective-permute-done.1.refs_1_
  19.6 0.0 collective-permute-done.from_mate.refs_1_
  19.6 7.1 %collective-permute-done.2.from_other.refs_3_ = bf16[7,16,4608]{2,1,0:T(8,128)(2,1)S(1)} collective-permute-done((bf16[7,16,4608]{2,1,0:T(8,128)(2,1)S(1)}, bf16[7,16,4608]{2,1,0:T(8,128)(2,1)S(1)}, u32[]{:S(2)}, u32[]{:S(2)}) %collective-permute-start.2) | collective-permute-done | bytes 1032224 | tf_op jit(solution)/shard_map/ppermute | solution.py:440
  26.6 0.6 shard_map.48.refs_4_.refs_5_
  27.3 0.0 copy-done
  27.3 0.0 copy-start.1
  27.3 4.7 %shard_map.49 = (f32[4,16,4608]{2,1,0:T(8,128)S(1)}, bf16[6,16,4608]{2,1,0:T(8,128)(2,1)S(1)}, bf16[6,16,4608]{2,1,0:T(8,128)(2,1)S(1)}) custom-call(s32[3]{0:T(128)S(1)} %pad_add_fusion.place.refs_0_.refs_1_, bf16[7,16,4608]{2,1,0:T(8,128)(2,1)S(1)} %collective-permute-done.from_mate.refs_1_, f32[4,16,4608]{2,1,0:T(8,128)S(1)} %copy-done, ...), custom_call_target="tpu_custom_call" | custom-call | flops 1 | bytes 1 | tf_op jit(solution)/shard_map/pallas_call | solution.py:363
  32.0 0.1 collective-permute-start.3
  32.1 4.2 %collective-permute-start.4 = (bf16[6,16,4608]{2,1,0:T(8,128)(2,1)S(1)}, bf16[6,16,4608]{2,1,0:T(8,128)(2,1)S(1)}, u32[]{:S(2)}, u32[]{:S(2)}) collective-permute-start(bf16[6,16,4608]{2,1,0:T(8,128)(2,1)S(1)} %get-tuple-element.28), channel_id=1, source_target_pairs={{16,32},{48,64},{80,96},{112,128},{144,160},{176,192},{208,224},{3... | collective-permute-start | bytes 2654216 | tf_op jit(solution)/shard_map/ppermute | solution.py:440
  36.3 0.0 collective-permute-done.5.refs_3_
  36.3 0.0 copy-done.1
  36.3 2.5 %shard_map.51 = (f32[4,8,4608]{2,1,0:T(8,128)S(1)}, bf16[3,16,4608]{2,1,0:T(8,128)(2,1)S(1)}, bf16[3,16,4608]{2,1,0:T(8,128)(2,1)S(1)}) custom-call(s32[3]{0:T(128)S(1)} %pad_add_fusion.place.refs_0_.refs_1_, bf16[3,16,4608]{2,1,0:T(8,128)(2,1)S(1)} %collective-permute-done.1.refs_1_, f32[4,8,4608]{2,1,0:T(8,128)S(1)} %copy-done.1, ...), custom_call_target="tpu_custom_call" | custom-call | flops 1 | bytes 1 | tf_op jit(solution)/shard_map/pallas_call | solution.py:363
  38.8 0.1 collective-permute-start.6
  38.9 5.0 %collective-permute-start.7 = (bf16[3,16,4608]{2,1,0:T(8,128)(2,1)S(1)}, bf16[3,16,4608]{2,1,0:T(8,128)(2,1)S(1)}, u32[]{:S(2)}, u32[]{:S(2)}) collective-permute-start(bf16[3,16,4608]{2,1,0:T(8,128)(2,1)S(1)} %get-tuple-element.34), channel_id=1, source_target_pairs={{16,32},{48,64},{80,96},{112,128},{144,160},{176,192},{208,224},{3... | collective-permute-start | bytes 1327112 | tf_op jit(solution)/shard_map/ppermute | solution.py:440
  43.9 0.0 collective-permute-done.3.refs_1_
  43.9 6.1 %collective-permute-done.4.refs_3_ = bf16[6,16,4608]{2,1,0:T(8,128)(2,1)S(1)} collective-permute-done((bf16[6,16,4608]{2,1,0:T(8,128)(2,1)S(1)}, bf16[6,16,4608]{2,1,0:T(8,128)(2,1)S(1)}, u32[]{:S(2)}, u32[]{:S(2)}) %collective-permute-start.4) | collective-permute-done | bytes 884768 | tf_op jit(solution)/shard_map/ppermute | solution.py:440
  50.0 5.8 %shard_map.50.refs_0_ = bf16[16,16,1152]{2,1,0:T(8,128)(2,1)S(1)} custom-call(s32[3]{0:T(128)S(1)} %pad_add_fusion.place.refs_0_.refs_1_, bf16[6,16,4608]{2,1,0:T(8,128)(2,1)S(1)} %collective-permute-done.3.refs_1_, f32[4,16,4608]{2,1,0:T(8,128)S(1)} %get-tuple-element.27.refs_2_, bf16[6,16,4608]{2,1,0:T(8,128)(2,1)S(1)} %collective-permute-done.4.refs_3_, ...), custom_call_target="tpu_custom_call" | custom-call | flops 1 | bytes 1 | tf_op jit(solution)/shard_map/pallas_call | solution.py:363
  55.9 0.0 collective-permute-done.6.refs_2_
  55.9 0.0 collective-permute-done.7.refs_4_
  55.9 4.2 %shard_map.52 = bf16[16,24,1152]{2,1,0:T(8,128)(2,1)} custom-call(bf16[16,16,1152]{2,1,0:T(8,128)(2,1)S(1)} %shard_map.50.refs_0_, s32[3]{0:T(128)S(1)} %pad_add_fusion.place.refs_0_.refs_1_, bf16[3,16,4608]{2,1,0:T(8,128)(2,1)S(1)} %collective-permute-done.6.refs_2_, f32[4,8,4608]{2,1,0:T(8,128)S(1)} %get-tuple-element.33.refs_3_, ...), custom_call_target="tpu_custom_call" | custom-call | flops 1 | bytes 1 | tf_op jit(solution)/shard_map/pallas_call | solution.py:363
  60.1 0.0 copy-start.4
  60.1 0.0 copy-start.2
  60.1 9.3 %all-to-all-start = ((bf16[16,24,1152]{2,1,0:T(8,128)(2,1)}), bf16[16,24,1152]{2,1,0:T(8,128)(2,1)S(1)}, u32[]{:S(2)}, u32[]{:S(2)}) async-start(bf16[16,24,1152]{2,1,0:T(8,128)(2,1)} %shard_map.52), calls=%async_computation | async-start | bytes 1769472 | tf_op jit(solution)/shard_map/all_to_all | solution.py:471
  69.4 0.0 copy-done.4
  69.4 0.2 copy.5
  69.6 20.9 %all-to-all-done = bf16[16,24,1152]{2,1,0:T(8,128)(2,1)S(1)} async-done(((bf16[16,24,1152]{2,1,0:T(8,128)(2,1)}), bf16[16,24,1152]{2,1,0:T(8,128)(2,1)S(1)}, u32[]{:S(2)}, u32[]{:S(2)}) %all-to-all-start) | async-done | bytes 884768 | tf_op jit(solution)/shard_map/all_to_all | solution.py:471
  90.6 0.0 copy-done.2
  90.6 1.4 %shard_map.53 = bf16[384,1152]{1,0:T(8,128)(2,1)S(1)} custom-call(bf16[384,384]{1,0:T(8,128)(2,1)S(1)} %bitcast.8, bf16[384,1152]{1,0:T(8,128)(2,1)S(1)} %bitcast.6, bf16[384,384]{1,0:T(8,128)(2,1)S(1)} %copy-done.2), custom_call_target="tpu_custom_call" | custom-call | flops 1 | bytes 1 | tf_op jit(solution)/shard_map/pallas_call | solution.py:393
  92.0 28.4 %all_to_all.10.parts = bf16[16,24,1152]{2,1,0:T(8,128)(2,1)S(1)} all-to-all(bf16[16,24,1152]{2,1,0:T(8,128)(2,1)S(1)} %bitcast.7), channel_id=1, replica_groups=mesh['space'=16,'band'=16] {'band'}, dimensions={0} | all-to-all | bytes 1769472 | tf_op jit(solution)/shard_map/all_to_all | solution.py:474
  120.4 1.7 %shard_map.54 = f32[24,4,4608]{2,1,0:T(4,128)} custom-call(bf16[16,24,1152]{2,1,0:T(8,128)(2,1)S(1)} %all_to_all.10.parts), custom_call_target="tpu_custom_call" | custom-call | flops 1 | bytes 1 | tf_op jit(solution)/shard_map/pallas_call | solution.py:419
Async XLA Ops:
  0.1 0.9 copy-start.3
  6.2 13.3 %collective-permute-start = (bf16[7,16,4608]{2,1,0:T(8,128)(2,1)S(1)}, bf16[7,16,4608]{2,1,0:T(8,128)(2,1)S(1)}, u32[]{:S(2)}, u32[]{:S(2)}) collective-permute-start(bf16[7,16,4608]{2,1,0:T(8,128)(2,1)S(1)} %get-tuple-element.20), channel_id=1, source_target_pairs={{0,16},{16,0},{32,48},{48,32},{64,80},{80,64},{96,112},{112,96},{1... | collective-permute-start | bytes 3096584 | tf_op jit(solution)/shard_map/ppermute | solution.py:441
  6.9 20.3 %copy-start = (f32[4,16,4608]{2,1,0:T(8,128)S(1)}, f32[4,16,4608]{2,1,0:T(8,128)}, u32[]{:S(2)}) copy-start(f32[4,16,4608]{2,1,0:T(8,128)} %get-tuple-element.23.refs_2_.refs_5_) | copy-start | bytes 3538948
  6.9 19.7 %collective-permute-start.2 = (bf16[7,16,4608]{2,1,0:T(8,128)(2,1)S(1)}, bf16[7,16,4608]{2,1,0:T(8,128)(2,1)S(1)}, u32[]{:S(2)}, u32[]{:S(2)}) collective-permute-start(bf16[7,16,4608]{2,1,0:T(8,128)(2,1)S(1)} %get-tuple-element.24), channel_id=1, source_target_pairs={{16,32},{48,64},{80,96},{112,128},{144,160},{176,192},{208,224},{3... | collective-permute-start | bytes 3096584 | tf_op jit(solution)/shard_map/ppermute | solution.py:440
  14.6 5.0 %collective-permute-start.1 = (bf16[3,16,4608]{2,1,0:T(8,128)(2,1)S(1)}, bf16[3,16,4608]{2,1,0:T(8,128)(2,1)S(1)}, u32[]{:S(2)}, u32[]{:S(2)}) collective-permute-start(bf16[3,16,4608]{2,1,0:T(8,128)(2,1)S(1)} %get-tuple-element.22), channel_id=1, source_target_pairs={{0,16},{16,0},{32,48},{48,32},{64,80},{80,64},{96,112},{112,96},{1... | collective-permute-start | bytes 1327112 | tf_op jit(solution)/shard_map/ppermute | solution.py:441
  14.6 21.7 %collective-permute-start.5 = (bf16[3,16,4608]{2,1,0:T(8,128)(2,1)S(1)}, bf16[3,16,4608]{2,1,0:T(8,128)(2,1)S(1)}, u32[]{:S(2)}, u32[]{:S(2)}) collective-permute-start(bf16[3,16,4608]{2,1,0:T(8,128)(2,1)S(1)} %get-tuple-element.31), channel_id=1, source_target_pairs={{16,32},{48,64},{80,96},{112,128},{144,160},{176,192},{208,224},{3... | collective-permute-start | bytes 1327112 | tf_op jit(solution)/shard_map/ppermute | solution.py:440
  27.3 9.0 %copy-start.1 = (f32[4,8,4608]{2,1,0:T(8,128)S(1)}, f32[4,8,4608]{2,1,0:T(8,128)}, u32[]{:S(2)}) copy-start(f32[4,8,4608]{2,1,0:T(8,128)} %get-tuple-element.30.refs_2_.refs_6_) | copy-start | bytes 1769476
  32.0 12.0 %collective-permute-start.3 = (bf16[6,16,4608]{2,1,0:T(8,128)(2,1)S(1)}, bf16[6,16,4608]{2,1,0:T(8,128)(2,1)S(1)}, u32[]{:S(2)}, u32[]{:S(2)}) collective-permute-start(bf16[6,16,4608]{2,1,0:T(8,128)(2,1)S(1)} %get-tuple-element.26), channel_id=1, source_target_pairs={{0,16},{16,0},{32,48},{48,32},{64,80},{80,64},{96,112},{112,96},{1... | collective-permute-start | bytes 2654216 | tf_op jit(solution)/shard_map/ppermute | solution.py:441
  32.1 18.0 %collective-permute-start.4 = (bf16[6,16,4608]{2,1,0:T(8,128)(2,1)S(1)}, bf16[6,16,4608]{2,1,0:T(8,128)(2,1)S(1)}, u32[]{:S(2)}, u32[]{:S(2)}) collective-permute-start(bf16[6,16,4608]{2,1,0:T(8,128)(2,1)S(1)} %get-tuple-element.28), channel_id=1, source_target_pairs={{16,32},{48,64},{80,96},{112,128},{144,160},{176,192},{208,224},{3... | collective-permute-start | bytes 2654216 | tf_op jit(solution)/shard_map/ppermute | solution.py:440
  38.8 17.1 %collective-permute-start.6 = (bf16[3,16,4608]{2,1,0:T(8,128)(2,1)S(1)}, bf16[3,16,4608]{2,1,0:T(8,128)(2,1)S(1)}, u32[]{:S(2)}, u32[]{:S(2)}) collective-permute-start(bf16[3,16,4608]{2,1,0:T(8,128)(2,1)S(1)} %get-tuple-element.32), channel_id=1, source_target_pairs={{0,16},{16,0},{32,48},{48,32},{64,80},{80,64},{96,112},{112,96},{1... | collective-permute-start | bytes 1327112 | tf_op jit(solution)/shard_map/ppermute | solution.py:441
  38.9 17.0 %collective-permute-start.7 = (bf16[3,16,4608]{2,1,0:T(8,128)(2,1)S(1)}, bf16[3,16,4608]{2,1,0:T(8,128)(2,1)S(1)}, u32[]{:S(2)}, u32[]{:S(2)}) collective-permute-start(bf16[3,16,4608]{2,1,0:T(8,128)(2,1)S(1)} %get-tuple-element.34), channel_id=1, source_target_pairs={{16,32},{48,64},{80,96},{112,128},{144,160},{176,192},{208,224},{3... | collective-permute-start | bytes 1327112 | tf_op jit(solution)/shard_map/ppermute | solution.py:440
  60.1 9.4 %copy-start.4 = (bf16[384,384]{1,0:T(8,128)(2,1)S(1)}, bf16[384,384]{1,0:T(8,128)(2,1)}, u32[]{:S(2)}) copy-start(bf16[384,384]{1,0:T(8,128)(2,1)} %param.6) | copy-start | bytes 884740
  60.1 30.5 %copy-start.2 = (bf16[384,384]{1,0:T(8,128)(2,1)S(1)}, bf16[384,384]{1,0:T(8,128)(2,1)}, u32[]{:S(2)}) copy-start(bf16[384,384]{1,0:T(8,128)(2,1)} %constant.23.clone.order) | copy-start | bytes 884740
  60.1 30.5 %all-to-all-start = ((bf16[16,24,1152]{2,1,0:T(8,128)(2,1)}), bf16[16,24,1152]{2,1,0:T(8,128)(2,1)S(1)}, u32[]{:S(2)}, u32[]{:S(2)}) async-start(bf16[16,24,1152]{2,1,0:T(8,128)(2,1)} %shard_map.52), calls=%async_computation | async-start | bytes 1769472 | tf_op jit(solution)/shard_map/all_to_all | solution.py:471

commit v5 on v4

--- a/solution.py
+++ b/solution.py
@@ -242,10 +242,7 @@
 
 def potential_field_kernel(place, from_mate, own, from_other, out):
     planes = own.shape[0]
-
-    def scale(x):
-        return (x + (HALF_WIDTH - CENTER)) / HALF_WIDTH
-
+    scale = scaled_potential
     out[2 : planes + 2] = scale(own[...])
     mate, other = [halo[0].astype(jnp.float32) for halo in (from_mate, from_other)]
     mate_below = place[2] == 1
@@ -270,9 +267,59 @@
     )(place, halo[0], own, halo[1])
 
 
+def scaled_potential(x):
+    return (x + (HALF_WIDTH - CENTER)) / HALF_WIDTH
+
+
+def shift_masks(rows):
+    lane = lanes_of(rows)
+    return lane >= LANE - ZB, lane < ZB, lane % ZB == ZB - 1, lane % ZB == 0
+
+
+def own_part_kernel(potential, own, out, field, diag):
+    planes, rows, columns = own.shape
+
+    @pl.when(pl.program_id(0) == 0)
+    def _():
+        for p in (0, 1, planes + 2, planes + 3):
+            field[p] = jnp.zeros((rows, columns), jnp.float32)
+        for p in range(planes):
+            diag[p] = jnp.broadcast_to(scaled_potential(potential[p : p + 1, :]), (rows, columns))
+
+    field[2 : planes + 2] = own[...]
+    masks = shift_masks(rows)
+
+    def one_plane(p, _):
+        def emit(j, center, near, far):
+            out[p, :, piece(j)] = diag[p, :, piece(j)] * center + NEAR * near + FAR * far
+
+        stencil_row(field, p, masks, emit)
+        return 0
+
+    lax.fori_loop(0, planes, one_plane, 0)
+
+
+def own_part(potential, own):
+    planes, count, columns = own.shape
+    spec = pl.BlockSpec((planes, ROWS, columns), lambda i: (0, i, 0))
+    return pl.pallas_call(
+        own_part_kernel,
+        grid=(count // ROWS,),
+        in_specs=[whole_spec(potential.shape), spec],
+        out_specs=spec,
+        out_shape=jax.ShapeDtypeStruct(own.shape, own.dtype),
+        scratch_shapes=[
+            pltpu.VMEM((planes + 4, ROWS, columns), jnp.float32),
+            pltpu.VMEM((planes, ROWS, columns), jnp.float32),
+        ],
+        compiler_params=pltpu.CompilerParams(vmem_limit_bytes=VMEM_LIMIT),
+        cost_estimate=pl.CostEstimate(flops=1, bytes_accessed=1, transcendentals=0),
+    )(potential, own)
+
+
 def two_steps_kernel(last, count_done, *refs):
     done = refs[:count_done]
-    place, from_mate, own, from_other, potential, *rest = refs[count_done:]
+    place, from_mate, own, from_other, potential, partial, *rest = refs[count_done:]
     if last:
         first, out, field, inner, diag, held_all = rest
     else:
@@ -288,13 +335,14 @@
     field[planes : 2 * planes] = own[...]
     unpack_halo(from_other, 1 - place[2], field)
 
-    lane = lanes_of(rows)
-    masks = (lane >= LANE - ZB, lane < ZB, lane % ZB == ZB - 1, lane % ZB == 0)
-    odd = lane // ZB % 2 == 1
-    upper = lane >= 2 * ZB
-
-    def first_stage(p, _):
-        here = jnp.where(p < 2, place[0], jnp.where(p >= planes + 2, place[1], 1)).astype(jnp.float32)
+    masks = shift_masks(rows)
+    group = lanes_of(rows) // ZB
+    odd = group % 2 == 1
+    upper = group >= 2
+
+    def first_stage(q, _):
+        p = q + jnp.where(q >= 2, planes, 0)
+        here = jnp.where(q < 2, place[0], place[1]).astype(jnp.float32)
         near_by = here * NEAR
         far_by = here * FAR
 
@@ -304,7 +352,16 @@
         stencil_row(field, p + planes - 4, masks, emit)
         return 0
 
-    lax.fori_loop(0, planes + 4, first_stage, 0)
+    lax.fori_loop(0, 4, first_stage, 0)
+    top = 2 * planes
+    for at in range(0, columns, ROW_BLOCK):
+        lanes = pl.ds(at, ROW_BLOCK)
+        below = field[planes - 1, :, lanes]
+        above = field[top, :, lanes]
+        inner[2, :, lanes] = partial[0, :, lanes] + (NEAR * below + FAR * field[planes - 2, :, lanes])
+        inner[3, :, lanes] = partial[1, :, lanes] + FAR * below
+        inner[planes, :, lanes] = partial[planes - 2, :, lanes] + FAR * above
+        inner[planes + 1, :, lanes] = partial[planes - 1, :, lanes] + (NEAR * above + FAR * field[top + 1, :, lanes])
 
     own_rows = pl.ds(pl.multiple_of(pl.program_id(0) * rows, rows), rows)
 
@@ -342,7 +399,7 @@
         lax.fori_loop(0, out.shape[0], one_part, 0)
 
 
-def two_steps(place, halo, own, potential, first=None, done=()):
+def two_steps(place, halo, own, potential, partial, first=None, done=()):
     planes, count, columns = own.shape
     last = first is not None
     spec = pl.BlockSpec((planes, ROWS, columns), lambda i: (0, i, 0))
@@ -365,14 +422,14 @@
         grid=(count // ROWS,),
         in_specs=[whole_spec(x.shape) for x in done]
         + [pl.BlockSpec(memory_space=pltpu.SMEM)]
-        + [whole_spec(halo[0].shape), spec, whole_spec(halo[1].shape), whole_spec(potential.shape)]
+        + [whole_spec(halo[0].shape), spec, whole_spec(halo[1].shape), whole_spec(potential.shape), spec]
         + [spec] * last,
         out_specs=out_spec,
         out_shape=out_shape,
         scratch_shapes=scratch,
         compiler_params=pltpu.CompilerParams(vmem_limit_bytes=VMEM_LIMIT),
         cost_estimate=pl.CostEstimate(flops=1, bytes_accessed=1, transcendentals=0),
-    )(*done, place, halo[0], own, halo[1], potential, *([first] if last else []))
+    )(*done, place, halo[0], own, halo[1], potential, partial, *([first] if last else []))
 
 
 def z_order():
@@ -444,6 +501,7 @@
     place = jnp.stack([at > 0, at < domains - 1, at % 2]).astype(jnp.int32)
 
     orbitals = pltpu.with_memory_space_constraint(orbitals, pltpu.HBM)
+    potential = pltpu.with_memory_space_constraint(potential, pltpu.HBM)
     starts = [sum(CHUNKS[:i]) for i in range(len(CHUNKS))]
     zeroth, halos = [], []
     for i, (start, chunk) in enumerate(zip(starts, CHUNKS)):
@@ -453,20 +511,20 @@
         zeroth.append(fields)
         halos.append(around(*halo))
 
-    second, next_halos = [], []
+    runs = field
+    partials = [own_part(runs, x) for x in zeroth]
     fields_0, waited = lax.optimization_barrier((zeroth[0], halos[1][0]))
     halos[1] = (waited, halos[1][1])
-    field = potential_field(place, halos[0], field)
-    fields, *halo = two_steps(place, halos[0], fields_0, field)
-    second.append(fields)
-    next_halos.append(around(*halo))
-    fields_1 = zeroth[1]
-    fields, *halo = two_steps(place, halos[1], fields_1, field)
-    second.append(fields)
-    next_halos.append(around(*halo))
+    field = potential_field(place, halos[0], runs)
+    second, next_halos = [], []
+    for halo, fields, partial in zip(halos, (fields_0, zeroth[1]), partials):
+        fields, *halo = two_steps(place, halo, fields, field, partial)
+        second.append(fields)
+        next_halos.append(around(*halo))
+    partials = [own_part(runs, x) for x in second]
     filtered = ()
-    for fields, halo, first in zip(second, next_halos, zeroth):
-        filtered = (two_steps(place, halo, fields, field, first, filtered),)
+    for fields, halo, partial, first in zip(second, next_halos, partials, zeroth):
+        filtered = (two_steps(place, halo, fields, field, partial, first, filtered),)
     filtered, = filtered
     gathered = lax.all_to_all(filtered, "band", 0, 0)
     width = columns // GROUPS

time: 123 us -> 119 us (0.967)
  waiting for transfers between devices: 34.1 us -> 30.2 us
  Pallas kernels: 29.6 us -> 31.2 us
    pallas_call x0 -> x4, Pallas kernels: none -> 4.25 us  [own_part(): pl.pallas_call(own_part_kernel, grid=(count // ROWS,), in_specs=[whole_sp...]
    ppermute x4, waiting for transfers between devices: 13.2 us -> 9.32 us  [around(): other = lax.ppermute(to_other, 'space', others)]
    pallas_call x4, Pallas kernels: 17.2 us -> 14.5 us  [two_steps(): pl.pallas_call(functools.partial(two_steps_kernel, last, len(done)), grid...]
  transfers between devices with their start and end apart: 9 -> 9, of which waited for: 3 -> 3; matrix products, arithmetic and copies ran while one was open for 0% -> 0% of each run, Pallas kernels for 14% -> 16%
where the time goes in v5:
time: 119 us
  Pallas kernels  31.2 us (26%)
  waiting for transfers between devices  30.2 us (25%)
  starting transfers between devices  28.6 us (24%)
  blocking collectives  28.4 us (24%)
    all_to_all x1, blocking collectives, body(): back = lax.all_to_all(summed.reshape(members, count, width), 'band', 0, 0)  28.4 us
    all_to_all x1, waiting for transfers between devices, body(): gathered = lax.all_to_all(filtered, 'band', 0, 0)  20.9 us
    ppermute x4, starting transfers between devices, around(): other = lax.ppermute(to_other, 'space', others)  18.3 us
    pallas_call x4, Pallas kernels, two_steps(): pl.pallas_call(functools.partial(two_steps_kernel, last, len(done)), grid...  14.5 us
    all_to_all x1, starting transfers between devices, body(): gathered = lax.all_to_all(filtered, 'band', 0, 0)  9.35 us
    ppermute x4, waiting for transfers between devices, around(): other = lax.ppermute(to_other, 'space', others)  9.32 us
    pallas_call x2, Pallas kernels, to_runs(): pl.pallas_call(functools.partial(to_runs_kernel, extra), grid=(count // R...  8.57 us
    pallas_call x4, Pallas kernels, own_part(): pl.pallas_call(own_part_kernel, grid=(count // ROWS,), in_specs=[whole_sp...  4.25 us
  transfers between devices with their start and end apart: 9, of which 3 were waited for; matrix products, arithmetic and copies ran while one was open for 0% of the time, Pallas kernels for 16%

profile of v5, /device:TPU:25, one launch (start us, length us, event | category | flops | bytes accessed | tf_op | source)
XLA Modules:
  0.0 118.9 jit_solution(9869409256853235874)
XLA Ops:
  0.0 0.1 pad_add_fusion.place.refs_0_.refs_1_
  0.1 5.3 %shard_map.46 = (f32[4,16,4608]{2,1,0:T(8,128)}, bf16[7,16,4608]{2,1,0:T(8,128)(2,1)S(1)}, bf16[7,16,4608]{2,1,0:T(8,128)(2,1)S(1)}, f32[4,4608]{1,0:T(4,128)S(1)}) custom-call(s32[3]{0:T(128)S(1)} %pad_add_fusion.place.refs_0_.refs_1_, f32[24,4,4608]{2,1,0:T(4,128)} %cells.3, f32[4,4608]{1,0:T(4,128)} %rest_0_.1), custom_call_target="tpu_custom_call" | custom-call | flops 1 | bytes 1 | tf_op jit(solution)/shard_map/pallas_call | solution.py:183
  5.4 0.0 copy-start
  5.4 0.7 collective-permute-start
  6.0 4.3 %collective-permute-start.2 = (bf16[7,16,4608]{2,1,0:T(8,128)(2,1)S(1)}, bf16[7,16,4608]{2,1,0:T(8,128)(2,1)S(1)}, u32[]{:S(2)}, u32[]{:S(2)}) collective-permute-start(bf16[7,16,4608]{2,1,0:T(8,128)(2,1)S(1)} %get-tuple-element.24), channel_id=1, source_target_pairs={{16,32},{48,64},{80,96},{112,128},{144,160},{176,192},{208,224},{3... | collective-permute-start | bytes 3096584 | tf_op jit(solution)/shard_map/ppermute | solution.py:497
  10.4 3.3 %shard_map.47 = (f32[4,8,4608]{2,1,0:T(8,128)}, bf16[3,16,4608]{2,1,0:T(8,128)(2,1)S(1)}, bf16[3,16,4608]{2,1,0:T(8,128)(2,1)S(1)}) custom-call(s32[3]{0:T(128)S(1)} %pad_add_fusion.place.refs_0_.refs_1_, f32[24,4,4608]{2,1,0:T(4,128)} %cells.3), custom_call_target="tpu_custom_call" | custom-call | flops 1 | bytes 1 | tf_op jit(solution)/shard_map/pallas_call | solution.py:183
  13.7 0.0 collective-permute-start.1
  13.7 4.8 %collective-permute-start.5 = (bf16[3,16,4608]{2,1,0:T(8,128)(2,1)S(1)}, bf16[3,16,4608]{2,1,0:T(8,128)(2,1)S(1)}, u32[]{:S(2)}, u32[]{:S(2)}) collective-permute-start(bf16[3,16,4608]{2,1,0:T(8,128)(2,1)S(1)} %get-tuple-element.31), channel_id=1, source_target_pairs={{16,32},{48,64},{80,96},{112,128},{144,160},{176,192},{208,224},{3... | collective-permute-start | bytes 1327112 | tf_op jit(solution)/shard_map/ppermute | solution.py:497
  18.5 0.0 copy-done
  18.5 1.5 %shard_map.49.refs_5_ = f32[4,16,4608]{2,1,0:T(8,128)S(1)} custom-call(f32[4,4608]{1,0:T(4,128)S(1)} %get-tuple-element.25.own.potential, f32[4,16,4608]{2,1,0:T(8,128)S(1)} %copy-done), custom_call_target="tpu_custom_call" | custom-call | flops 1 | bytes 1 | tf_op jit(solution)/shard_map/pallas_call | solution.py:305
  20.0 0.0 collective-permute-done.1.refs_1_
  20.0 0.0 collective-permute-done.from_mate.refs_1_
  20.0 5.6 %collective-permute-done.2.from_other.refs_3_ = bf16[7,16,4608]{2,1,0:T(8,128)(2,1)S(1)} collective-permute-done((bf16[7,16,4608]{2,1,0:T(8,128)(2,1)S(1)}, bf16[7,16,4608]{2,1,0:T(8,128)(2,1)S(1)}, u32[]{:S(2)}, u32[]{:S(2)}) %collective-permute-start.2) | collective-permute-done | bytes 1032224 | tf_op jit(solution)/shard_map/ppermute | solution.py:497
  25.6 0.6 shard_map.48.refs_4_.refs_5_
  26.2 0.0 copy-start.1
  26.2 3.8 %shard_map.50 = (f32[4,16,4608]{2,1,0:T(8,128)S(1)}, bf16[6,16,4608]{2,1,0:T(8,128)(2,1)S(1)}, bf16[6,16,4608]{2,1,0:T(8,128)(2,1)S(1)}) custom-call(s32[3]{0:T(128)S(1)} %pad_add_fusion.place.refs_0_.refs_1_, bf16[7,16,4608]{2,1,0:T(8,128)(2,1)S(1)} %collective-permute-done.from_mate.refs_1_, f32[4,16,4608]{2,1,0:T(8,128)S(1)} %copy-done, ...), custom_call_target="tpu_custom_call" | custom-call | flops 1 | bytes 1 | tf_op jit(solution)/shard_map/pallas_call | solution.py:420
  30.0 0.1 collective-permute-start.3
  30.1 4.3 %collective-permute-start.4 = (bf16[6,16,4608]{2,1,0:T(8,128)(2,1)S(1)}, bf16[6,16,4608]{2,1,0:T(8,128)(2,1)S(1)}, u32[]{:S(2)}, u32[]{:S(2)}) collective-permute-start(bf16[6,16,4608]{2,1,0:T(8,128)(2,1)S(1)} %get-tuple-element.28), channel_id=1, source_target_pairs={{16,32},{48,64},{80,96},{112,128},{144,160},{176,192},{208,224},{3... | collective-permute-start | bytes 2654216 | tf_op jit(solution)/shard_map/ppermute | solution.py:497
  34.5 0.0 copy-done.1
  34.5 0.7 shard_map.53.refs_5_
  35.2 0.0 collective-permute-done.5.refs_3_
  35.2 2.1 %shard_map.54 = (f32[4,8,4608]{2,1,0:T(8,128)S(1)}, bf16[3,16,4608]{2,1,0:T(8,128)(2,1)S(1)}, bf16[3,16,4608]{2,1,0:T(8,128)(2,1)S(1)}) custom-call(s32[3]{0:T(128)S(1)} %pad_add_fusion.place.refs_0_.refs_1_, bf16[3,16,4608]{2,1,0:T(8,128)(2,1)S(1)} %collective-permute-done.1.refs_1_, f32[4,8,4608]{2,1,0:T(8,128)S(1)} %copy-done.1, ...), custom_call_target="tpu_custom_call" | custom-call | flops 1 | bytes 1 | tf_op jit(solution)/shard_map/pallas_call | solution.py:420
  37.3 0.1 collective-permute-start.6
  37.4 4.8 %collective-permute-start.7 = (bf16[3,16,4608]{2,1,0:T(8,128)(2,1)S(1)}, bf16[3,16,4608]{2,1,0:T(8,128)(2,1)S(1)}, u32[]{:S(2)}, u32[]{:S(2)}) collective-permute-start(bf16[3,16,4608]{2,1,0:T(8,128)(2,1)S(1)} %get-tuple-element.34), channel_id=1, source_target_pairs={{16,32},{48,64},{80,96},{112,128},{144,160},{176,192},{208,224},{3... | collective-permute-start | bytes 1327112 | tf_op jit(solution)/shard_map/ppermute | solution.py:497
  42.2 1.5 %shard_map.51.refs_5_ = f32[4,16,4608]{2,1,0:T(8,128)S(1)} custom-call(f32[4,4608]{1,0:T(4,128)S(1)} %get-tuple-element.25.own.potential, f32[4,16,4608]{2,1,0:T(8,128)S(1)} %get-tuple-element.27.own.refs_2_), custom_call_target="tpu_custom_call" | custom-call | flops 1 | bytes 1 | tf_op jit(solution)/shard_map/pallas_call | solution.py:305
  43.7 0.7 shard_map.55.refs_6_
  44.3 0.0 collective-permute-done.3.refs_1_
  44.4 3.7 %collective-permute-done.4.refs_3_ = bf16[6,16,4608]{2,1,0:T(8,128)(2,1)S(1)} collective-permute-done((bf16[6,16,4608]{2,1,0:T(8,128)(2,1)S(1)}, bf16[6,16,4608]{2,1,0:T(8,128)(2,1)S(1)}, u32[]{:S(2)}, u32[]{:S(2)}) %collective-permute-start.4) | collective-permute-done | bytes 884768 | tf_op jit(solution)/shard_map/ppermute | solution.py:497
  48.1 5.0 %shard_map.52.refs_0_ = bf16[16,16,1152]{2,1,0:T(8,128)(2,1)S(1)} custom-call(s32[3]{0:T(128)S(1)} %pad_add_fusion.place.refs_0_.refs_1_, bf16[6,16,4608]{2,1,0:T(8,128)(2,1)S(1)} %collective-permute-done.3.refs_1_, f32[4,16,4608]{2,1,0:T(8,128)S(1)} %get-tuple-element.27.own.refs_2_, bf16[6,16,4608]{2,1,0:T(8,128)(2,1)S(1)} %collective-permute-done.4.refs_3_, ...), custom_call_target="tpu_custom_call" | custom-call | flops 1 | bytes 1 | tf_op jit(solution)/shard_map/pallas_call | solution.py:420
  53.1 0.0 collective-permute-done.6.refs_2_
  53.1 0.0 collective-permute-done.7.refs_4_
  53.1 3.7 %shard_map.56 = bf16[16,24,1152]{2,1,0:T(8,128)(2,1)} custom-call(bf16[16,16,1152]{2,1,0:T(8,128)(2,1)S(1)} %shard_map.52.refs_0_, s32[3]{0:T(128)S(1)} %pad_add_fusion.place.refs_0_.refs_1_, bf16[3,16,4608]{2,1,0:T(8,128)(2,1)S(1)} %collective-permute-done.6.refs_2_, f32[4,8,4608]{2,1,0:T(8,128)S(1)} %get-tuple-element.33.own.refs_3_, ...), custom_call_target="tpu_custom_call" | custom-call | flops 1 | bytes 1 | tf_op jit(solution)/shard_map/pallas_call | solution.py:420
  56.8 0.0 copy-start.3
  56.8 0.0 copy-start.2
  56.8 9.4 %all-to-all-start = ((bf16[16,24,1152]{2,1,0:T(8,128)(2,1)}), bf16[16,24,1152]{2,1,0:T(8,128)(2,1)S(1)}, u32[]{:S(2)}, u32[]{:S(2)}) async-start(bf16[16,24,1152]{2,1,0:T(8,128)(2,1)} %shard_map.56), calls=%async_computation | async-start | bytes 1769472 | tf_op jit(solution)/shard_map/all_to_all | solution.py:529
  66.2 0.0 copy-done.3
  66.2 0.2 copy.5
  66.4 20.9 %all-to-all-done = bf16[16,24,1152]{2,1,0:T(8,128)(2,1)S(1)} async-done(((bf16[16,24,1152]{2,1,0:T(8,128)(2,1)}), bf16[16,24,1152]{2,1,0:T(8,128)(2,1)S(1)}, u32[]{:S(2)}, u32[]{:S(2)}) %all-to-all-start) | async-done | bytes 884768 | tf_op jit(solution)/shard_map/all_to_all | solution.py:529
  87.3 0.0 copy-done.2
  87.3 1.4 %shard_map.57 = bf16[384,1152]{1,0:T(8,128)(2,1)S(1)} custom-call(bf16[384,384]{1,0:T(8,128)(2,1)S(1)} %bitcast.8, bf16[384,1152]{1,0:T(8,128)(2,1)S(1)} %bitcast.6, bf16[384,384]{1,0:T(8,128)(2,1)S(1)} %copy-done.2), custom_call_target="tpu_custom_call" | custom-call | flops 1 | bytes 1 | tf_op jit(solution)/shard_map/pallas_call | solution.py:450
  88.8 28.4 %all_to_all.10.parts = bf16[16,24,1152]{2,1,0:T(8,128)(2,1)S(1)} all-to-all(bf16[16,24,1152]{2,1,0:T(8,128)(2,1)S(1)} %bitcast.7), channel_id=1, replica_groups=mesh['space'=16,'band'=16] {'band'}, dimensions={0} | all-to-all | bytes 1769472 | tf_op jit(solution)/shard_map/all_to_all | solution.py:532
  117.1 1.7 %shard_map.58 = f32[24,4,4608]{2,1,0:T(4,128)} custom-call(bf16[16,24,1152]{2,1,0:T(8,128)(2,1)S(1)} %all_to_all.10.parts), custom_call_target="tpu_custom_call" | custom-call | flops 1 | bytes 1 | tf_op jit(solution)/shard_map/pallas_call | solution.py:476
Async XLA Ops:
  5.4 13.2 %copy-start = (f32[4,16,4608]{2,1,0:T(8,128)S(1)}, f32[4,16,4608]{2,1,0:T(8,128)}, u32[]{:S(2)}) copy-start(f32[4,16,4608]{2,1,0:T(8,128)} %get-tuple-element.23.own.refs_2_.refs_6_) | copy-start | bytes 3538948
  5.4 14.7 %collective-permute-start = (bf16[7,16,4608]{2,1,0:T(8,128)(2,1)S(1)}, bf16[7,16,4608]{2,1,0:T(8,128)(2,1)S(1)}, u32[]{:S(2)}, u32[]{:S(2)}) collective-permute-start(bf16[7,16,4608]{2,1,0:T(8,128)(2,1)S(1)} %get-tuple-element.20), channel_id=1, source_target_pairs={{0,16},{16,0},{32,48},{48,32},{64,80},{80,64},{96,112},{112,96},{1... | collective-permute-start | bytes 3096584 | tf_op jit(solution)/shard_map/ppermute | solution.py:498
  6.0 19.5 %collective-permute-start.2 = (bf16[7,16,4608]{2,1,0:T(8,128)(2,1)S(1)}, bf16[7,16,4608]{2,1,0:T(8,128)(2,1)S(1)}, u32[]{:S(2)}, u32[]{:S(2)}) collective-permute-start(bf16[7,16,4608]{2,1,0:T(8,128)(2,1)S(1)} %get-tuple-element.24), channel_id=1, source_target_pairs={{16,32},{48,64},{80,96},{112,128},{144,160},{176,192},{208,224},{3... | collective-permute-start | bytes 3096584 | tf_op jit(solution)/shard_map/ppermute | solution.py:497
  13.7 6.3 %collective-permute-start.1 = (bf16[3,16,4608]{2,1,0:T(8,128)(2,1)S(1)}, bf16[3,16,4608]{2,1,0:T(8,128)(2,1)S(1)}, u32[]{:S(2)}, u32[]{:S(2)}) collective-permute-start(bf16[3,16,4608]{2,1,0:T(8,128)(2,1)S(1)} %get-tuple-element.22), channel_id=1, source_target_pairs={{0,16},{16,0},{32,48},{48,32},{64,80},{80,64},{96,112},{112,96},{1... | collective-permute-start | bytes 1327112 | tf_op jit(solution)/shard_map/ppermute | solution.py:498
  13.7 21.5 %collective-permute-start.5 = (bf16[3,16,4608]{2,1,0:T(8,128)(2,1)S(1)}, bf16[3,16,4608]{2,1,0:T(8,128)(2,1)S(1)}, u32[]{:S(2)}, u32[]{:S(2)}) collective-permute-start(bf16[3,16,4608]{2,1,0:T(8,128)(2,1)S(1)} %get-tuple-element.31), channel_id=1, source_target_pairs={{16,32},{48,64},{80,96},{112,128},{144,160},{176,192},{208,224},{3... | collective-permute-start | bytes 1327112 | tf_op jit(solution)/shard_map/ppermute | solution.py:497
  26.2 8.3 %copy-start.1 = (f32[4,8,4608]{2,1,0:T(8,128)S(1)}, f32[4,8,4608]{2,1,0:T(8,128)}, u32[]{:S(2)}) copy-start(f32[4,8,4608]{2,1,0:T(8,128)} %get-tuple-element.30.own.refs_2_.refs_7_) | copy-start | bytes 1769476
  30.0 14.3 %collective-permute-start.3 = (bf16[6,16,4608]{2,1,0:T(8,128)(2,1)S(1)}, bf16[6,16,4608]{2,1,0:T(8,128)(2,1)S(1)}, u32[]{:S(2)}, u32[]{:S(2)}) collective-permute-start(bf16[6,16,4608]{2,1,0:T(8,128)(2,1)S(1)} %get-tuple-element.26), channel_id=1, source_target_pairs={{0,16},{16,0},{32,48},{48,32},{64,80},{80,64},{96,112},{112,96},{1... | collective-permute-start | bytes 2654216 | tf_op jit(solution)/shard_map/ppermute | solution.py:498
  30.1 18.0 %collective-permute-start.4 = (bf16[6,16,4608]{2,1,0:T(8,128)(2,1)S(1)}, bf16[6,16,4608]{2,1,0:T(8,128)(2,1)S(1)}, u32[]{:S(2)}, u32[]{:S(2)}) collective-permute-start(bf16[6,16,4608]{2,1,0:T(8,128)(2,1)S(1)} %get-tuple-element.28), channel_id=1, source_target_pairs={{16,32},{48,64},{80,96},{112,128},{144,160},{176,192},{208,224},{3... | collective-permute-start | bytes 2654216 | tf_op jit(solution)/shard_map/ppermute | solution.py:497
  37.3 15.8 %collective-permute-start.6 = (bf16[3,16,4608]{2,1,0:T(8,128)(2,1)S(1)}, bf16[3,16,4608]{2,1,0:T(8,128)(2,1)S(1)}, u32[]{:S(2)}, u32[]{:S(2)}) collective-permute-start(bf16[3,16,4608]{2,1,0:T(8,128)(2,1)S(1)} %get-tuple-element.32), channel_id=1, source_target_pairs={{0,16},{16,0},{32,48},{48,32},{64,80},{80,64},{96,112},{112,96},{1... | collective-permute-start | bytes 1327112 | tf_op jit(solution)/shard_map/ppermute | solution.py:498
  37.4 15.7 %collective-permute-start.7 = (bf16[3,16,4608]{2,1,0:T(8,128)(2,1)S(1)}, bf16[3,16,4608]{2,1,0:T(8,128)(2,1)S(1)}, u32[]{:S(2)}, u32[]{:S(2)}) collective-permute-start(bf16[3,16,4608]{2,1,0:T(8,128)(2,1)S(1)} %get-tuple-element.34), channel_id=1, source_target_pairs={{16,32},{48,64},{80,96},{112,128},{144,160},{176,192},{208,224},{3... | collective-permute-start | bytes 1327112 | tf_op jit(solution)/shard_map/ppermute | solution.py:497
  56.8 9.4 %copy-start.3 = (bf16[384,384]{1,0:T(8,128)(2,1)S(1)}, bf16[384,384]{1,0:T(8,128)(2,1)}, u32[]{:S(2)}) copy-start(bf16[384,384]{1,0:T(8,128)(2,1)} %param.6) | copy-start | bytes 884740
  56.8 30.5 %copy-start.2 = (bf16[384,384]{1,0:T(8,128)(2,1)S(1)}, bf16[384,384]{1,0:T(8,128)(2,1)}, u32[]{:S(2)}) copy-start(bf16[384,384]{1,0:T(8,128)(2,1)} %constant.23.clone.order) | copy-start | bytes 884740
  56.8 30.5 %all-to-all-start = ((bf16[16,24,1152]{2,1,0:T(8,128)(2,1)}), bf16[16,24,1152]{2,1,0:T(8,128)(2,1)S(1)}, u32[]{:S(2)}, u32[]{:S(2)}) async-start(bf16[16,24,1152]{2,1,0:T(8,128)(2,1)} %shard_map.56), calls=%async_computation | async-start | bytes 1769472 | tf_op jit(solution)/shard_map/all_to_all | solution.py:529

commit v6 on v5

--- a/solution.py
+++ b/solution.py
@@ -17,6 +17,7 @@
 ZI = 3
 ZB = NZ // ZI
 PIECES = RUNS * ZI
+TERMS = 5
 ROW_BLOCK = GROUPS * NZ
 VMEM_LIMIT = 18 * 1024 * 1024
 CHUNKS = (16, 8)
@@ -52,33 +53,42 @@
 
 
 def pack_halo(planes, odd, to_mate, to_other):
-    base = pl.program_id(0) * 3
+    half = PIECES // 2
+    base = pl.program_id(0) * (TERMS * half * LANE)
+
+    def put(to, term, j, low, high):
+        at = pl.ds(pl.multiple_of(base + (term * half + j) * LANE, LANE), LANE)
+        to[:, at] = jnp.concatenate([low, high], axis=0).astype(jnp.bfloat16)
+
     for to, upward in ((to_mate, 1 - odd), (to_other, odd)):
-        near, next_near, far, farthest = [jnp.where(upward == 1, 3 - k, k) for k in range(4)]
-        for j in range(PIECES):
-            for i, p in enumerate((near, next_near)):
-                x = planes[p, :, piece(j)]
-                to[base + i, :, piece(j)] = jnp.concatenate([x, x - rounded(x)], axis=0).astype(jnp.bfloat16)
-            both = jnp.concatenate([planes[far, :, piece(j)], planes[farthest, :, piece(j)]], axis=0)
-            to[base + 2, :, piece(j)] = both.astype(jnp.bfloat16)
+        order = [jnp.where(upward == 1, 3 - k, k) for k in range(4)]
+        for j in range(half):
+            for k, p in enumerate(order):
+                low, high = planes[p, :, piece(j)], planes[p, :, piece(j + half)]
+                put(to, k + min(k, 1), j, low, high)
+                if k == 0:
+                    put(to, 1, j, low - rounded(low), high - rounded(high))
 
 
 def unpack_halo(halo, below, field):
-    base = pl.program_id(0) * 3
-    near, next_near, far, farthest = [jnp.where(below == 1, 3 - k, 8 + k) for k in range(4)]
-    columns = field.shape[2]
-    for at in range(0, columns, ROW_BLOCK):
-        lanes = pl.ds(at, ROW_BLOCK)
-        for i, p in enumerate((near, next_near)):
-            both = halo[base + i, :, lanes].astype(jnp.float32)
-            field[p, :, lanes] = both[:ROWS] + both[ROWS:]
-        both = halo[base + 2, :, lanes].astype(jnp.float32)
-        field[far, :, lanes] = both[:ROWS]
-        field[farthest, :, lanes] = both[ROWS:]
+    half = PIECES // 2
+    base = pl.program_id(0) * (TERMS * half * LANE)
+    order = [jnp.where(below == 1, 3 - k, 8 + k) for k in range(4)]
+
+    def get(term, j):
+        at = pl.ds(pl.multiple_of(base + (term * half + j) * LANE, LANE), LANE)
+        return halo[:, at].astype(jnp.float32)
+
+    for j in range(half):
+        for k, p in enumerate(order):
+            both = get(0, j) + get(1, j) if k == 0 else get(k + 1, j)
+            field[p, :, piece(j)] = both[:ROWS]
+            field[p, :, piece(j + half)] = both[ROWS:]
 
 
 def halo_shape(count, columns, extra=0):
-    return jax.ShapeDtypeStruct((count // ROWS * 3 + extra, 2 * ROWS, columns), jnp.bfloat16)
+    lanes = count // ROWS * TERMS * columns // 2 + extra * columns // GROUPS
+    return jax.ShapeDtypeStruct((2 * ROWS, lanes), jnp.bfloat16)
 
 
 def whole_spec(shape):
@@ -98,10 +108,9 @@
     return parts[0] + (parts[1] + parts[2])
 
 
-def potential_to_runs(cells, odd, order, out, to_mate, to_other, gathered, terms):
+def potential_to_runs(cells, odd, order, out, to_mate, to_other, gathered, terms, quarters):
     planes, columns = cells.shape
     blocks = columns // ROW_BLOCK
-    at_row = lax.broadcasted_iota(jnp.int32, (ROWS, LANE), 0)
     for k in range(blocks):
         x = cells[:, pl.ds(k * ROW_BLOCK, ROW_BLOCK)]
         gathered[pl.ds(k * ROWS, ROWS), :] = jnp.concatenate([x, jnp.zeros_like(x)], axis=0)
@@ -116,20 +125,21 @@
             x = done[i]
             j = GROUPS * m + i
             out[:, piece(j)] = x[:planes]
-            for to, upward in ((to_mate, 1 - odd), (to_other, odd)):
+            quarter, lanes = j // (PIECES // GROUPS), piece(j % (PIECES // GROUPS))
+            for to, upward in ((0, 1 - odd), (1, odd)):
                 near = jnp.where(upward == 1, x[planes - 1 : planes], x[0:1])
                 next_near = jnp.where(upward == 1, x[planes - 2 : planes - 1], x[1:2])
                 rows = [near, near - rounded(near), next_near, next_near - rounded(next_near)]
-                total = jnp.zeros((ROWS, LANE), jnp.float32)
                 for r, row in enumerate(rows):
-                    total = jnp.where(at_row == r, row, total)
-                total = jnp.concatenate([total, jnp.zeros_like(total)], axis=0)
-                to[to.shape[0] - 1, :, piece(j)] = total.astype(jnp.bfloat16)
+                    quarters[to, GROUPS * r + quarter : GROUPS * r + quarter + 1, lanes] = row
+    width = columns // GROUPS
+    for i, to in enumerate((to_mate, to_other)):
+        to[:, to.shape[1] - width : to.shape[1]] = quarters[i].astype(jnp.bfloat16)
 
 
 def to_runs_kernel(extra, place, cells, *rest):
     if extra:
-        potential, out, to_mate, to_other, runs, order, terms, turned, gathered, few_terms = rest
+        potential, out, to_mate, to_other, runs, order, terms, turned, gathered, few_terms, quarters = rest
     else:
         out, to_mate, to_other, order, terms, turned = rest
     planes, rows, columns = out.shape
@@ -141,7 +151,7 @@
         source = to // NZ * NZ + to % ZB * ZI + to % NZ // ZB
         order[...] = jnp.where(lax.broadcasted_iota(jnp.int32, order.shape, 0) == source, 1.0, 0.0).astype(jnp.bfloat16)
         if extra:
-            potential_to_runs(potential, place[2], order, runs, to_mate, to_other, gathered, few_terms)
+            potential_to_runs(potential, place[2], order, runs, to_mate, to_other, gathered, few_terms, quarters)
 
     for k in range(blocks):
         x = cells[:, :, pl.ds(k * ROW_BLOCK, ROW_BLOCK)].reshape(rows * planes, ROW_BLOCK)
@@ -180,6 +190,7 @@
     if extra:
         scratch.append(pltpu.VMEM((blocks * ROWS, ROW_BLOCK), jnp.float32))
         scratch.append(pltpu.VMEM((3, blocks * ROWS, ROW_BLOCK), jnp.bfloat16))
+        scratch.append(pltpu.VMEM((2, 4 * GROUPS, columns // GROUPS), jnp.float32))
     return pl.pallas_call(
         functools.partial(to_runs_kernel, extra),
         grid=(count // ROWS,),
@@ -244,19 +255,22 @@
     planes = own.shape[0]
     scale = scaled_potential
     out[2 : planes + 2] = scale(own[...])
-    mate, other = [halo[0].astype(jnp.float32) for halo in (from_mate, from_other)]
+    mate, other = [halo[...].astype(jnp.float32) for halo in (from_mate, from_other)]
     mate_below = place[2] == 1
     below = jnp.where(mate_below, mate, other)
     above = jnp.where(mate_below, other, mate)
-    out[1:2] = scale(below[0:1] + below[1:2])
-    out[0:1] = scale(below[2:3] + below[3:4])
-    out[planes + 2 : planes + 3] = scale(above[0:1] + above[1:2])
-    out[planes + 3 : planes + 4] = scale(above[2:3] + above[3:4])
+    width = below.shape[1]
+    rows = ((1, below, 0), (0, below, 2), (planes + 2, above, 0), (planes + 3, above, 2))
+    for p, terms, first in rows:
+        whole = terms[first * GROUPS : (first + 1) * GROUPS] + terms[(first + 1) * GROUPS : (first + 2) * GROUPS]
+        for q in range(GROUPS):
+            out[p : p + 1, q * width : (q + 1) * width] = scale(whole[q : q + 1])
 
 
 def potential_field(place, halo, own):
     planes, columns = own.shape
-    specs = [pl.BlockSpec((1,) + x.shape[1:], lambda i, n=x.shape[0]: (n - 1, 0, 0)) for x in halo]
+    width = columns // GROUPS
+    specs = [pl.BlockSpec((x.shape[0], width), lambda i, n=x.shape[1] // width: (0, n - 1)) for x in halo]
     return pl.pallas_call(
         potential_field_kernel,
         grid=(1,),

time: 119 us -> 115 us (0.966)
  waiting for transfers between devices: 30.2 us -> 25.9 us
    ppermute x4, waiting for transfers between devices: 9.32 us -> 5 us  [around(): other = lax.ppermute(to_other, 'space', others)]
  transfers between devices with their start and end apart: 9 -> 9, of which waited for: 3 -> 3; matrix products, arithmetic and copies ran while one was open for 0% -> 0% of each run, Pallas kernels for 16% -> 17%
where the time goes in v6:
time: 115 us
  Pallas kernels  31.4 us (27%)
  starting transfers between devices  28.6 us (25%)
  blocking collectives  28.4 us (25%)
  waiting for transfers between devices  25.9 us (23%)
    all_to_all x1, blocking collectives, body(): back = lax.all_to_all(summed.reshape(members, count, width), 'band', 0, 0)  28.4 us
    all_to_all x1, waiting for transfers between devices, body(): gathered = lax.all_to_all(filtered, 'band', 0, 0)  20.9 us
    ppermute x4, starting transfers between devices, around(): other = lax.ppermute(to_other, 'space', others)  18.3 us
    pallas_call x4, Pallas kernels, two_steps(): pl.pallas_call(functools.partial(two_steps_kernel, last, len(done)), grid...  14.9 us
    all_to_all x1, starting transfers between devices, body(): gathered = lax.all_to_all(filtered, 'band', 0, 0)  9.35 us
    pallas_call x2, Pallas kernels, to_runs(): pl.pallas_call(functools.partial(to_runs_kernel, extra), grid=(count // R...  8.55 us
    ppermute x4, waiting for transfers between devices, around(): other = lax.ppermute(to_other, 'space', others)  5 us
    pallas_call x4, Pallas kernels, own_part(): pl.pallas_call(own_part_kernel, grid=(count // ROWS,), in_specs=[whole_sp...  4.25 us
  transfers between devices with their start and end apart: 9, of which 3 were waited for; matrix products, arithmetic and copies ran while one was open for 0% of the time, Pallas kernels for 17%

profile of v6, /device:TPU:25, one launch (start us, length us, event | category | flops | bytes accessed | tf_op | source)
XLA Modules:
  0.0 114.8 jit_solution(2790540071660275392)
XLA Ops:
  0.0 0.1 pad_add_fusion.place.refs_0_.refs_1_
  0.1 5.2 %shard_map.46 = (f32[4,16,4608]{2,1,0:T(8,128)}, bf16[16,24192]{1,0:T(8,128)(2,1)S(1)}, bf16[16,24192]{1,0:T(8,128)(2,1)S(1)}, f32[4,4608]{1,0:T(4,128)S(1)}) custom-call(s32[3]{0:T(128)S(1)} %pad_add_fusion.place.refs_0_.refs_1_, f32[24,4,4608]{2,1,0:T(4,128)} %cells.3, f32[4,4608]{1,0:T(4,128)} %rest_0_.1), custom_call_target="tpu_custom_call" | custom-call | flops 1 | bytes 1 | tf_op jit(solution)/shard_map/pallas_call | solution.py:194
  5.3 0.0 copy-start
  5.3 0.7 collective-permute-start
  6.0 4.3 %collective-permute-start.2 = (bf16[16,24192]{1,0:T(8,128)(2,1)S(1)}, bf16[16,24192]{1,0:T(8,128)(2,1)S(1)}, u32[]{:S(2)}, u32[]{:S(2)}) collective-permute-start(bf16[16,24192]{1,0:T(8,128)(2,1)S(1)} %get-tuple-element.24), channel_id=1, source_target_pairs={{16,32},{48,64},{80,96},{112,128},{144,160},{176,192},{208,224},{3... | collective-permute-start | bytes 2322440 | tf_op jit(solution)/shard_map/ppermute | solution.py:511
  10.3 3.3 %shard_map.47 = (f32[4,8,4608]{2,1,0:T(8,128)}, bf16[16,11520]{1,0:T(8,128)(2,1)S(1)}, bf16[16,11520]{1,0:T(8,128)(2,1)S(1)}) custom-call(s32[3]{0:T(128)S(1)} %pad_add_fusion.place.refs_0_.refs_1_, f32[24,4,4608]{2,1,0:T(4,128)} %cells.3), custom_call_target="tpu_custom_call" | custom-call | flops 1 | bytes 1 | tf_op jit(solution)/shard_map/pallas_call | solution.py:194
  13.6 0.0 collective-permute-start.1
  13.6 4.8 %collective-permute-start.5 = (bf16[16,11520]{1,0:T(8,128)(2,1)S(1)}, bf16[16,11520]{1,0:T(8,128)(2,1)S(1)}, u32[]{:S(2)}, u32[]{:S(2)}) collective-permute-start(bf16[16,11520]{1,0:T(8,128)(2,1)S(1)} %get-tuple-element.31), channel_id=1, source_target_pairs={{16,32},{48,64},{80,96},{112,128},{144,160},{176,192},{208,224},{3... | collective-permute-start | bytes 1105928 | tf_op jit(solution)/shard_map/ppermute | solution.py:511
  18.5 0.0 copy-done
  18.5 1.5 %shard_map.49.refs_5_ = f32[4,16,4608]{2,1,0:T(8,128)S(1)} custom-call(f32[4,4608]{1,0:T(4,128)S(1)} %get-tuple-element.25.own.potential, f32[4,16,4608]{2,1,0:T(8,128)S(1)} %copy-done), custom_call_target="tpu_custom_call" | custom-call | flops 1 | bytes 1 | tf_op jit(solution)/shard_map/pallas_call | solution.py:319
  20.0 0.0 collective-permute-done.1.refs_1_
  20.0 0.0 collective-permute-done.from_mate.refs_1_
  20.0 2.8 %collective-permute-done.2.from_other.refs_3_ = bf16[16,24192]{1,0:T(8,128)(2,1)S(1)} collective-permute-done((bf16[16,24192]{1,0:T(8,128)(2,1)S(1)}, bf16[16,24192]{1,0:T(8,128)(2,1)S(1)}, u32[]{:S(2)}, u32[]{:S(2)}) %collective-permute-start.2) | collective-permute-done | bytes 774176 | tf_op jit(solution)/shard_map/ppermute | solution.py:511
  22.8 0.6 shard_map.48.refs_4_.refs_5_
  23.4 0.0 copy-start.1
  23.4 3.9 %shard_map.50 = (f32[4,16,4608]{2,1,0:T(8,128)S(1)}, bf16[16,23040]{1,0:T(8,128)(2,1)S(1)}, bf16[16,23040]{1,0:T(8,128)(2,1)S(1)}) custom-call(s32[3]{0:T(128)S(1)} %pad_add_fusion.place.refs_0_.refs_1_, bf16[16,24192]{1,0:T(8,128)(2,1)S(1)} %collective-permute-done.from_mate.refs_1_, f32[4,16,4608]{2,1,0:T(8,128)S(1)} %copy-done, ...), custom_call_target="tpu_custom_call" | custom-call | flops 1 | bytes 1 | tf_op jit(solution)/shard_map/pallas_call | solution.py:434
  27.3 0.1 collective-permute-start.3
  27.4 4.3 %collective-permute-start.4 = (bf16[16,23040]{1,0:T(8,128)(2,1)S(1)}, bf16[16,23040]{1,0:T(8,128)(2,1)S(1)}, u32[]{:S(2)}, u32[]{:S(2)}) collective-permute-start(bf16[16,23040]{1,0:T(8,128)(2,1)S(1)} %get-tuple-element.28), channel_id=1, source_target_pairs={{16,32},{48,64},{80,96},{112,128},{144,160},{176,192},{208,224},{3... | collective-permute-start | bytes 2211848 | tf_op jit(solution)/shard_map/ppermute | solution.py:511
  31.8 0.0 copy-done.1
  31.8 0.7 shard_map.53.refs_5_
  32.5 0.0 collective-permute-done.5.refs_3_
  32.5 2.1 %shard_map.54 = (f32[4,8,4608]{2,1,0:T(8,128)S(1)}, bf16[16,11520]{1,0:T(8,128)(2,1)S(1)}, bf16[16,11520]{1,0:T(8,128)(2,1)S(1)}) custom-call(s32[3]{0:T(128)S(1)} %pad_add_fusion.place.refs_0_.refs_1_, bf16[16,11520]{1,0:T(8,128)(2,1)S(1)} %collective-permute-done.1.refs_1_, f32[4,8,4608]{2,1,0:T(8,128)S(1)} %copy-done.1, ...), custom_call_target="tpu_custom_call" | custom-call | flops 1 | bytes 1 | tf_op jit(solution)/shard_map/pallas_call | solution.py:434
  34.5 0.1 collective-permute-start.6
  34.6 4.8 %collective-permute-start.7 = (bf16[16,11520]{1,0:T(8,128)(2,1)S(1)}, bf16[16,11520]{1,0:T(8,128)(2,1)S(1)}, u32[]{:S(2)}, u32[]{:S(2)}) collective-permute-start(bf16[16,11520]{1,0:T(8,128)(2,1)S(1)} %get-tuple-element.34), channel_id=1, source_target_pairs={{16,32},{48,64},{80,96},{112,128},{144,160},{176,192},{208,224},{3... | collective-permute-start | bytes 1105928 | tf_op jit(solution)/shard_map/ppermute | solution.py:511
  39.5 1.5 %shard_map.51.refs_5_ = f32[4,16,4608]{2,1,0:T(8,128)S(1)} custom-call(f32[4,4608]{1,0:T(4,128)S(1)} %get-tuple-element.25.own.potential, f32[4,16,4608]{2,1,0:T(8,128)S(1)} %get-tuple-element.27.own.refs_2_), custom_call_target="tpu_custom_call" | custom-call | flops 1 | bytes 1 | tf_op jit(solution)/shard_map/pallas_call | solution.py:319
  41.0 0.7 shard_map.55.refs_6_
  41.6 0.0 collective-permute-done.3.refs_1_
  41.6 2.2 %collective-permute-done.4.refs_3_ = bf16[16,23040]{1,0:T(8,128)(2,1)S(1)} collective-permute-done((bf16[16,23040]{1,0:T(8,128)(2,1)S(1)}, bf16[16,23040]{1,0:T(8,128)(2,1)S(1)}, u32[]{:S(2)}, u32[]{:S(2)}) %collective-permute-start.4) | collective-permute-done | bytes 737312 | tf_op jit(solution)/shard_map/ppermute | solution.py:511
  43.8 5.2 %shard_map.52.refs_0_ = bf16[16,16,1152]{2,1,0:T(8,128)(2,1)S(1)} custom-call(s32[3]{0:T(128)S(1)} %pad_add_fusion.place.refs_0_.refs_1_, bf16[16,23040]{1,0:T(8,128)(2,1)S(1)} %collective-permute-done.3.refs_1_, f32[4,16,4608]{2,1,0:T(8,128)S(1)} %get-tuple-element.27.own.refs_2_, bf16[16,23040]{1,0:T(8,128)(2,1)S(1)} %collective-permute-done.4.refs_3_, ...), custom_call_target="tpu_custom_call" | custom-call | flops 1 | bytes 1 | tf_op jit(solution)/shard_map/pallas_call | solution.py:434
  49.0 0.0 collective-permute-done.6.refs_2_
  49.0 0.0 collective-permute-done.7.refs_4_
  49.0 3.7 %shard_map.56 = bf16[16,24,1152]{2,1,0:T(8,128)(2,1)} custom-call(bf16[16,16,1152]{2,1,0:T(8,128)(2,1)S(1)} %shard_map.52.refs_0_, s32[3]{0:T(128)S(1)} %pad_add_fusion.place.refs_0_.refs_1_, bf16[16,11520]{1,0:T(8,128)(2,1)S(1)} %collective-permute-done.6.refs_2_, f32[4,8,4608]{2,1,0:T(8,128)S(1)} %get-tuple-element.33.own.refs_3_, ...), custom_call_target="tpu_custom_call" | custom-call | flops 1 | bytes 1 | tf_op jit(solution)/shard_map/pallas_call | solution.py:434
  52.7 0.0 copy-start.3
  52.7 0.0 copy-start.2
  52.7 9.4 %all-to-all-start = ((bf16[16,24,1152]{2,1,0:T(8,128)(2,1)}), bf16[16,24,1152]{2,1,0:T(8,128)(2,1)S(1)}, u32[]{:S(2)}, u32[]{:S(2)}) async-start(bf16[16,24,1152]{2,1,0:T(8,128)(2,1)} %shard_map.56), calls=%async_computation | async-start | bytes 1769472 | tf_op jit(solution)/shard_map/all_to_all | solution.py:543
  62.1 0.0 copy-done.3
  62.1 0.2 copy.5
  62.3 20.9 %all-to-all-done = bf16[16,24,1152]{2,1,0:T(8,128)(2,1)S(1)} async-done(((bf16[16,24,1152]{2,1,0:T(8,128)(2,1)}), bf16[16,24,1152]{2,1,0:T(8,128)(2,1)S(1)}, u32[]{:S(2)}, u32[]{:S(2)}) %all-to-all-start) | async-done | bytes 884768 | tf_op jit(solution)/shard_map/all_to_all | solution.py:543
  83.2 0.0 copy-done.2
  83.2 1.4 %shard_map.57 = bf16[384,1152]{1,0:T(8,128)(2,1)S(1)} custom-call(bf16[384,384]{1,0:T(8,128)(2,1)S(1)} %bitcast.8, bf16[384,1152]{1,0:T(8,128)(2,1)S(1)} %bitcast.6, bf16[384,384]{1,0:T(8,128)(2,1)S(1)} %copy-done.2), custom_call_target="tpu_custom_call" | custom-call | flops 1 | bytes 1 | tf_op jit(solution)/shard_map/pallas_call | solution.py:464
  84.7 28.4 %all_to_all.10.parts = bf16[16,24,1152]{2,1,0:T(8,128)(2,1)S(1)} all-to-all(bf16[16,24,1152]{2,1,0:T(8,128)(2,1)S(1)} %bitcast.7), channel_id=1, replica_groups=mesh['space'=16,'band'=16] {'band'}, dimensions={0} | all-to-all | bytes 1769472 | tf_op jit(solution)/shard_map/all_to_all | solution.py:546
  113.1 1.7 %shard_map.58 = f32[24,4,4608]{2,1,0:T(4,128)} custom-call(bf16[16,24,1152]{2,1,0:T(8,128)(2,1)S(1)} %all_to_all.10.parts), custom_call_target="tpu_custom_call" | custom-call | flops 1 | bytes 1 | tf_op jit(solution)/shard_map/pallas_call | solution.py:490
Async XLA Ops:
  5.3 13.2 %copy-start = (f32[4,16,4608]{2,1,0:T(8,128)S(1)}, f32[4,16,4608]{2,1,0:T(8,128)}, u32[]{:S(2)}) copy-start(f32[4,16,4608]{2,1,0:T(8,128)} %get-tuple-element.23.own.refs_2_.refs_6_) | copy-start | bytes 3538948
  5.3 14.7 %collective-permute-start = (bf16[16,24192]{1,0:T(8,128)(2,1)S(1)}, bf16[16,24192]{1,0:T(8,128)(2,1)S(1)}, u32[]{:S(2)}, u32[]{:S(2)}) collective-permute-start(bf16[16,24192]{1,0:T(8,128)(2,1)S(1)} %get-tuple-element.20), channel_id=1, source_target_pairs={{0,16},{16,0},{32,48},{48,32},{64,80},{80,64},{96,112},{112,96},{1... | collective-permute-start | bytes 2322440 | tf_op jit(solution)/shard_map/ppermute | solution.py:512
  6.0 16.8 %collective-permute-start.2 = (bf16[16,24192]{1,0:T(8,128)(2,1)S(1)}, bf16[16,24192]{1,0:T(8,128)(2,1)S(1)}, u32[]{:S(2)}, u32[]{:S(2)}) collective-permute-start(bf16[16,24192]{1,0:T(8,128)(2,1)S(1)} %get-tuple-element.24), channel_id=1, source_target_pairs={{16,32},{48,64},{80,96},{112,128},{144,160},{176,192},{208,224},{3... | collective-permute-start | bytes 2322440 | tf_op jit(solution)/shard_map/ppermute | solution.py:511
  13.6 6.3 %collective-permute-start.1 = (bf16[16,11520]{1,0:T(8,128)(2,1)S(1)}, bf16[16,11520]{1,0:T(8,128)(2,1)S(1)}, u32[]{:S(2)}, u32[]{:S(2)}) collective-permute-start(bf16[16,11520]{1,0:T(8,128)(2,1)S(1)} %get-tuple-element.22), channel_id=1, source_target_pairs={{0,16},{16,0},{32,48},{48,32},{64,80},{80,64},{96,112},{112,96},{1... | collective-permute-start | bytes 1105928 | tf_op jit(solution)/shard_map/ppermute | solution.py:512
  13.6 18.8 %collective-permute-start.5 = (bf16[16,11520]{1,0:T(8,128)(2,1)S(1)}, bf16[16,11520]{1,0:T(8,128)(2,1)S(1)}, u32[]{:S(2)}, u32[]{:S(2)}) collective-permute-start(bf16[16,11520]{1,0:T(8,128)(2,1)S(1)} %get-tuple-element.31), channel_id=1, source_target_pairs={{16,32},{48,64},{80,96},{112,128},{144,160},{176,192},{208,224},{3... | collective-permute-start | bytes 1105928 | tf_op jit(solution)/shard_map/ppermute | solution.py:511
  23.4 8.4 %copy-start.1 = (f32[4,8,4608]{2,1,0:T(8,128)S(1)}, f32[4,8,4608]{2,1,0:T(8,128)}, u32[]{:S(2)}) copy-start(f32[4,8,4608]{2,1,0:T(8,128)} %get-tuple-element.30.own.refs_2_.refs_7_) | copy-start | bytes 1769476
  27.3 14.3 %collective-permute-start.3 = (bf16[16,23040]{1,0:T(8,128)(2,1)S(1)}, bf16[16,23040]{1,0:T(8,128)(2,1)S(1)}, u32[]{:S(2)}, u32[]{:S(2)}) collective-permute-start(bf16[16,23040]{1,0:T(8,128)(2,1)S(1)} %get-tuple-element.26), channel_id=1, source_target_pairs={{0,16},{16,0},{32,48},{48,32},{64,80},{80,64},{96,112},{112,96},{1... | collective-permute-start | bytes 2211848 | tf_op jit(solution)/shard_map/ppermute | solution.py:512
  27.4 16.4 %collective-permute-start.4 = (bf16[16,23040]{1,0:T(8,128)(2,1)S(1)}, bf16[16,23040]{1,0:T(8,128)(2,1)S(1)}, u32[]{:S(2)}, u32[]{:S(2)}) collective-permute-start(bf16[16,23040]{1,0:T(8,128)(2,1)S(1)} %get-tuple-element.28), channel_id=1, source_target_pairs={{16,32},{48,64},{80,96},{112,128},{144,160},{176,192},{208,224},{3... | collective-permute-start | bytes 2211848 | tf_op jit(solution)/shard_map/ppermute | solution.py:511
  34.5 14.5 %collective-permute-start.6 = (bf16[16,11520]{1,0:T(8,128)(2,1)S(1)}, bf16[16,11520]{1,0:T(8,128)(2,1)S(1)}, u32[]{:S(2)}, u32[]{:S(2)}) collective-permute-start(bf16[16,11520]{1,0:T(8,128)(2,1)S(1)} %get-tuple-element.32), channel_id=1, source_target_pairs={{0,16},{16,0},{32,48},{48,32},{64,80},{80,64},{96,112},{112,96},{1... | collective-permute-start | bytes 1105928 | tf_op jit(solution)/shard_map/ppermute | solution.py:512
  34.6 14.4 %collective-permute-start.7 = (bf16[16,11520]{1,0:T(8,128)(2,1)S(1)}, bf16[16,11520]{1,0:T(8,128)(2,1)S(1)}, u32[]{:S(2)}, u32[]{:S(2)}) collective-permute-start(bf16[16,11520]{1,0:T(8,128)(2,1)S(1)} %get-tuple-element.34), channel_id=1, source_target_pairs={{16,32},{48,64},{80,96},{112,128},{144,160},{176,192},{208,224},{3... | collective-permute-start | bytes 1105928 | tf_op jit(solution)/shard_map/ppermute | solution.py:511
  52.7 9.4 %copy-start.3 = (bf16[384,384]{1,0:T(8,128)(2,1)S(1)}, bf16[384,384]{1,0:T(8,128)(2,1)}, u32[]{:S(2)}) copy-start(bf16[384,384]{1,0:T(8,128)(2,1)} %param.6) | copy-start | bytes 884740
  52.7 30.5 %copy-start.2 = (bf16[384,384]{1,0:T(8,128)(2,1)S(1)}, bf16[384,384]{1,0:T(8,128)(2,1)}, u32[]{:S(2)}) copy-start(bf16[384,384]{1,0:T(8,128)(2,1)} %constant.23.clone.order) | copy-start | bytes 884740
  52.7 30.5 %all-to-all-start = ((bf16[16,24,1152]{2,1,0:T(8,128)(2,1)}), bf16[16,24,1152]{2,1,0:T(8,128)(2,1)S(1)}, u32[]{:S(2)}, u32[]{:S(2)}) async-start(bf16[16,24,1152]{2,1,0:T(8,128)(2,1)} %shard_map.56), calls=%async_computation | async-start | bytes 1769472 | tf_op jit(solution)/shard_map/all_to_all | solution.py:543

commit v7 on v6

--- a/solution.py
+++ b/solution.py
@@ -19,7 +19,7 @@
 PIECES = RUNS * ZI
 TERMS = 5
 ROW_BLOCK = GROUPS * NZ
-VMEM_LIMIT = 18 * 1024 * 1024
+VMEM_LIMIT = 14 * 1024 * 1024
 CHUNKS = (16, 8)
 
 CENTER = 4.75
@@ -267,20 +267,6 @@
             out[p : p + 1, q * width : (q + 1) * width] = scale(whole[q : q + 1])
 
 
-def potential_field(place, halo, own):
-    planes, columns = own.shape
-    width = columns // GROUPS
-    specs = [pl.BlockSpec((x.shape[0], width), lambda i, n=x.shape[1] // width: (0, n - 1)) for x in halo]
-    return pl.pallas_call(
-        potential_field_kernel,
-        grid=(1,),
-        in_specs=[pl.BlockSpec(memory_space=pltpu.SMEM), specs[0], whole_spec(own.shape), specs[1]],
-        out_specs=whole_spec((planes + 4, columns)),
-        out_shape=jax.ShapeDtypeStruct((planes + 4, columns), jnp.float32),
-        compiler_params=pltpu.CompilerParams(vmem_limit_bytes=VMEM_LIMIT),
-    )(place, halo[0], own, halo[1])
-
-
 def scaled_potential(x):
     return (x + (HALF_WIDTH - CENTER)) / HALF_WIDTH
 
@@ -331,9 +317,12 @@
     )(potential, own)
 
 
-def two_steps_kernel(last, count_done, *refs):
+def two_steps_kernel(last, extra, count_done, *refs):
     done = refs[:count_done]
     place, from_mate, own, from_other, potential, partial, *rest = refs[count_done:]
+    if extra:
+        runs, (mate_end, other_end, out, to_mate, to_other, potential, *rest) = potential, rest
+        rest = (out, to_mate, to_other, *rest)
     if last:
         first, out, field, inner, diag, held_all = rest
     else:
@@ -342,6 +331,8 @@
 
     @pl.when(pl.program_id(0) == 0)
     def _():
+        if extra:
+            potential_field_kernel(place, mate_end, runs, other_end, potential)
         for p in range(planes + 4):
             diag[p] = jnp.broadcast_to(potential[p : p + 1, :], (rows, columns))
 
@@ -413,13 +404,20 @@
         lax.fori_loop(0, out.shape[0], one_part, 0)
 
 
-def two_steps(place, halo, own, potential, partial, first=None, done=()):
+def two_steps(place, halo, own, potential, partial, first=None, done=(), extra=False):
     planes, count, columns = own.shape
     last = first is not None
     spec = pl.BlockSpec((planes, ROWS, columns), lambda i: (0, i, 0))
     near = halo_shape(count, columns)
     out_shape = [jax.ShapeDtypeStruct(own.shape, own.dtype), near, near]
     out_spec = [spec, whole_spec(near.shape), whole_spec(near.shape)]
+    ends = []
+    if extra:
+        diagonal = jax.ShapeDtypeStruct((planes + 4, columns), jnp.float32)
+        out_shape.append(diagonal)
+        out_spec.append(whole_spec(diagonal.shape))
+        width = columns // GROUPS
+        ends = [pl.BlockSpec((x.shape[0], width), lambda i, n=x.shape[1] // width: (0, n - 1)) for x in halo]
     scratch = [
         pltpu.VMEM((planes * 3, ROWS, columns), jnp.float32),
         pltpu.VMEM((planes + 4, ROWS, columns), jnp.float32),
@@ -432,18 +430,19 @@
         out_shape = jax.ShapeDtypeStruct(shape, jnp.bfloat16)
         out_spec = pl.BlockSpec(shape, lambda i: (0, 0, 0))
     return pl.pallas_call(
-        functools.partial(two_steps_kernel, last, len(done)),
+        functools.partial(two_steps_kernel, last, extra, len(done)),
         grid=(count // ROWS,),
         in_specs=[whole_spec(x.shape) for x in done]
         + [pl.BlockSpec(memory_space=pltpu.SMEM)]
         + [whole_spec(halo[0].shape), spec, whole_spec(halo[1].shape), whole_spec(potential.shape), spec]
+        + ends
         + [spec] * last,
         out_specs=out_spec,
         out_shape=out_shape,
         scratch_shapes=scratch,
         compiler_params=pltpu.CompilerParams(vmem_limit_bytes=VMEM_LIMIT),
         cost_estimate=pl.CostEstimate(flops=1, bytes_accessed=1, transcendentals=0),
-    )(*done, place, halo[0], own, halo[1], potential, partial, *([first] if last else []))
+    )(*done, place, halo[0], own, halo[1], potential, partial, *(halo if extra else ()), *([first] if last else []))
 
 
 def z_order():
@@ -529,10 +528,12 @@
     partials = [own_part(runs, x) for x in zeroth]
     fields_0, waited = lax.optimization_barrier((zeroth[0], halos[1][0]))
     halos[1] = (waited, halos[1][1])
-    field = potential_field(place, halos[0], runs)
+    field = runs
     second, next_halos = [], []
-    for halo, fields, partial in zip(halos, (fields_0, zeroth[1]), partials):
-        fields, *halo = two_steps(place, halo, fields, field, partial)
+    for i, (halo, fields, partial) in enumerate(zip(halos, (fields_0, zeroth[1]), partials)):
+        fields, *halo = two_steps(place, halo, fields, field, partial, extra=i == 0)
+        if i == 0:
+            field = halo.pop()
         second.append(fields)
         next_halos.append(around(*halo))
     partials = [own_part(runs, x) for x in second]

time: 115 us -> 115 us (level)
    pallas_call x5 -> x4, Pallas kernels: 15.5 us -> 14.9 us  [two_steps(): pl.pallas_call(functools.partial(two_steps_kernel, last, extra, len(done)...]
  transfers between devices with their start and end apart: 9 -> 9, of which waited for: 3 -> 3; matrix products, arithmetic and copies ran while one was open for 0% -> 0% of each run, Pallas kernels for 17% -> 16%
where the time goes in v7:
time: 115 us; the launch traced here: 114 us
  Pallas kernels  30.9 us (27%)
  starting transfers between devices  28.6 us (25%)
  blocking collectives  28.4 us (25%)
  waiting for transfers between devices  25.9 us (23%)
    all_to_all x1, blocking collectives, body(): back = lax.all_to_all(summed.reshape(members, count, width), 'band', 0, 0)  28.4 us
    all_to_all x1, waiting for transfers between devices, body(): gathered = lax.all_to_all(filtered, 'band', 0, 0)  20.9 us
    ppermute x4, starting transfers between devices, around(): other = lax.ppermute(to_other, 'space', others)  18.3 us
    pallas_call x4, Pallas kernels, two_steps(): pl.pallas_call(functools.partial(two_steps_kernel, last, extra, len(done)...  14.9 us
    all_to_all x1, starting transfers between devices, body(): gathered = lax.all_to_all(filtered, 'band', 0, 0)  9.35 us
    pallas_call x2, Pallas kernels, to_runs(): pl.pallas_call(functools.partial(to_runs_kernel, extra), grid=(count // R...  8.55 us
    ppermute x4, waiting for transfers between devices, around(): other = lax.ppermute(to_other, 'space', others)  4.99 us
    pallas_call x4, Pallas kernels, own_part(): pl.pallas_call(own_part_kernel, grid=(count // ROWS,), in_specs=[whole_sp...  4.25 us
  transfers between devices with their start and end apart: 9, of which 3 were waited for; matrix products, arithmetic and copies ran while one was open for 0% of the time, Pallas kernels for 16%

profile of v7, /device:TPU:25, one launch (start us, length us, event | category | flops | bytes accessed | tf_op | source)
XLA Modules:
  0.0 114.2 jit_solution(6935342812123898543)
XLA Ops:
  0.0 0.1 pad_add_fusion.place.refs_0_.refs_1_
  0.1 5.2 %shard_map.46 = (f32[4,16,4608]{2,1,0:T(8,128)}, bf16[16,24192]{1,0:T(8,128)(2,1)S(1)}, bf16[16,24192]{1,0:T(8,128)(2,1)S(1)}, f32[4,4608]{1,0:T(4,128)S(1)}) custom-call(s32[3]{0:T(128)S(1)} %pad_add_fusion.place.refs_0_.refs_1_, f32[24,4,4608]{2,1,0:T(4,128)} %cells.3, f32[4,4608]{1,0:T(4,128)} %rest_0_.1), custom_call_target="tpu_custom_call" | custom-call | flops 1 | bytes 1 | tf_op jit(solution)/shard_map/pallas_call | solution.py:194
  5.3 0.0 copy-start
  5.3 0.7 collective-permute-start
  6.0 4.3 %collective-permute-start.2 = (bf16[16,24192]{1,0:T(8,128)(2,1)S(1)}, bf16[16,24192]{1,0:T(8,128)(2,1)S(1)}, u32[]{:S(2)}, u32[]{:S(2)}) collective-permute-start(bf16[16,24192]{1,0:T(8,128)(2,1)S(1)} %get-tuple-element.25), channel_id=1, source_target_pairs={{16,32},{48,64},{80,96},{112,128},{144,160},{176,192},{208,224},{3... | collective-permute-start | bytes 2322440 | tf_op jit(solution)/shard_map/ppermute | solution.py:510
  10.3 3.3 %shard_map.47 = (f32[4,8,4608]{2,1,0:T(8,128)}, bf16[16,11520]{1,0:T(8,128)(2,1)S(1)}, bf16[16,11520]{1,0:T(8,128)(2,1)S(1)}) custom-call(s32[3]{0:T(128)S(1)} %pad_add_fusion.place.refs_0_.refs_1_, f32[24,4,4608]{2,1,0:T(4,128)} %cells.3), custom_call_target="tpu_custom_call" | custom-call | flops 1 | bytes 1 | tf_op jit(solution)/shard_map/pallas_call | solution.py:194
  13.6 0.0 collective-permute-start.1
  13.6 4.8 %collective-permute-start.5 = (bf16[16,11520]{1,0:T(8,128)(2,1)S(1)}, bf16[16,11520]{1,0:T(8,128)(2,1)S(1)}, u32[]{:S(2)}, u32[]{:S(2)}) collective-permute-start(bf16[16,11520]{1,0:T(8,128)(2,1)S(1)} %get-tuple-element.33), channel_id=1, source_target_pairs={{16,32},{48,64},{80,96},{112,128},{144,160},{176,192},{208,224},{3... | collective-permute-start | bytes 1105928 | tf_op jit(solution)/shard_map/ppermute | solution.py:510
  18.5 0.0 copy-done
  18.5 1.5 %shard_map.48.refs_5_ = f32[4,16,4608]{2,1,0:T(8,128)S(1)} custom-call(f32[4,4608]{1,0:T(4,128)S(1)} %get-tuple-element.26.potential.refs_4_, f32[4,16,4608]{2,1,0:T(8,128)S(1)} %copy-done), custom_call_target="tpu_custom_call" | custom-call | flops 1 | bytes 1 | tf_op jit(solution)/shard_map/pallas_call | solution.py:305
  20.0 0.0 copy-start.1
  20.0 0.0 collective-permute-done.1.refs_1_
  20.0 0.0 collective-permute-done.refs_1_.refs_6_
  20.0 2.8 %collective-permute-done.2.refs_3_.refs_7_ = bf16[16,24192]{1,0:T(8,128)(2,1)S(1)} collective-permute-done((bf16[16,24192]{1,0:T(8,128)(2,1)S(1)}, bf16[16,24192]{1,0:T(8,128)(2,1)S(1)}, u32[]{:S(2)}, u32[]{:S(2)}) %collective-permute-start.2) | collective-permute-done | bytes 774176 | tf_op jit(solution)/shard_map/ppermute | solution.py:510
  22.8 4.0 %shard_map.49 = (f32[4,16,4608]{2,1,0:T(8,128)S(1)}, bf16[16,23040]{1,0:T(8,128)(2,1)S(1)}, bf16[16,23040]{1,0:T(8,128)(2,1)S(1)}, f32[8,4608]{1,0:T(8,128)S(1)}) custom-call(s32[3]{0:T(128)S(1)} %pad_add_fusion.place.refs_0_.refs_1_, bf16[16,24192]{1,0:T(8,128)(2,1)S(1)} %collective-permute-done.refs_1_.refs_6_, f32[4,16,4608]{2,1,0:T(8,128)S(1)} %copy-done, ...), custom_call_target="tpu_custom_call" | custom-call | flops 1 | bytes 1 | tf_op jit(solution)/shard_map/pallas_call | solution.py:432
  26.8 0.1 collective-permute-start.3
  26.9 4.3 %collective-permute-start.4 = (bf16[16,23040]{1,0:T(8,128)(2,1)S(1)}, bf16[16,23040]{1,0:T(8,128)(2,1)S(1)}, u32[]{:S(2)}, u32[]{:S(2)}) collective-permute-start(bf16[16,23040]{1,0:T(8,128)(2,1)S(1)} %get-tuple-element.29), channel_id=1, source_target_pairs={{16,32},{48,64},{80,96},{112,128},{144,160},{176,192},{208,224},{3... | collective-permute-start | bytes 2211848 | tf_op jit(solution)/shard_map/ppermute | solution.py:510
  31.2 0.0 copy-done.1
  31.2 0.7 shard_map.52.refs_5_
  31.9 0.0 collective-permute-done.5.refs_3_
  31.9 2.1 %shard_map.53 = (f32[4,8,4608]{2,1,0:T(8,128)S(1)}, bf16[16,11520]{1,0:T(8,128)(2,1)S(1)}, bf16[16,11520]{1,0:T(8,128)(2,1)S(1)}) custom-call(s32[3]{0:T(128)S(1)} %pad_add_fusion.place.refs_0_.refs_1_, bf16[16,11520]{1,0:T(8,128)(2,1)S(1)} %collective-permute-done.1.refs_1_, f32[4,8,4608]{2,1,0:T(8,128)S(1)} %copy-done.1, ...), custom_call_target="tpu_custom_call" | custom-call | flops 1 | bytes 1 | tf_op jit(solution)/shard_map/pallas_call | solution.py:432
  34.0 0.1 collective-permute-start.6
  34.1 4.8 %collective-permute-start.7 = (bf16[16,11520]{1,0:T(8,128)(2,1)S(1)}, bf16[16,11520]{1,0:T(8,128)(2,1)S(1)}, u32[]{:S(2)}, u32[]{:S(2)}) collective-permute-start(bf16[16,11520]{1,0:T(8,128)(2,1)S(1)} %get-tuple-element.36), channel_id=1, source_target_pairs={{16,32},{48,64},{80,96},{112,128},{144,160},{176,192},{208,224},{3... | collective-permute-start | bytes 1105928 | tf_op jit(solution)/shard_map/ppermute | solution.py:510
  38.9 1.5 %shard_map.50.refs_5_ = f32[4,16,4608]{2,1,0:T(8,128)S(1)} custom-call(f32[4,4608]{1,0:T(4,128)S(1)} %get-tuple-element.26.potential.refs_4_, f32[4,16,4608]{2,1,0:T(8,128)S(1)} %get-tuple-element.28.own.refs_2_), custom_call_target="tpu_custom_call" | custom-call | flops 1 | bytes 1 | tf_op jit(solution)/shard_map/pallas_call | solution.py:305
  40.4 0.7 shard_map.54.refs_6_
  41.1 0.0 collective-permute-done.3.refs_1_
  41.1 2.2 %collective-permute-done.4.refs_3_ = bf16[16,23040]{1,0:T(8,128)(2,1)S(1)} collective-permute-done((bf16[16,23040]{1,0:T(8,128)(2,1)S(1)}, bf16[16,23040]{1,0:T(8,128)(2,1)S(1)}, u32[]{:S(2)}, u32[]{:S(2)}) %collective-permute-start.4) | collective-permute-done | bytes 737312 | tf_op jit(solution)/shard_map/ppermute | solution.py:510
  43.3 5.2 %shard_map.51.refs_0_ = bf16[16,16,1152]{2,1,0:T(8,128)(2,1)S(1)} custom-call(s32[3]{0:T(128)S(1)} %pad_add_fusion.place.refs_0_.refs_1_, bf16[16,23040]{1,0:T(8,128)(2,1)S(1)} %collective-permute-done.3.refs_1_, f32[4,16,4608]{2,1,0:T(8,128)S(1)} %get-tuple-element.28.own.refs_2_, bf16[16,23040]{1,0:T(8,128)(2,1)S(1)} %collective-permute-done.4.refs_3_, ...), custom_call_target="tpu_custom_call" | custom-call | flops 1 | bytes 1 | tf_op jit(solution)/shard_map/pallas_call | solution.py:432
  48.5 0.0 collective-permute-done.6.refs_2_
  48.5 0.0 collective-permute-done.7.refs_4_
  48.5 3.7 %shard_map.55 = bf16[16,24,1152]{2,1,0:T(8,128)(2,1)} custom-call(bf16[16,16,1152]{2,1,0:T(8,128)(2,1)S(1)} %shard_map.51.refs_0_, s32[3]{0:T(128)S(1)} %pad_add_fusion.place.refs_0_.refs_1_, bf16[16,11520]{1,0:T(8,128)(2,1)S(1)} %collective-permute-done.6.refs_2_, f32[4,8,4608]{2,1,0:T(8,128)S(1)} %get-tuple-element.35.own.refs_3_, ...), custom_call_target="tpu_custom_call" | custom-call | flops 1 | bytes 1 | tf_op jit(solution)/shard_map/pallas_call | solution.py:432
  52.2 0.0 copy-start.3
  52.2 0.0 copy-start.2
  52.2 9.4 %all-to-all-start = ((bf16[16,24,1152]{2,1,0:T(8,128)(2,1)}), bf16[16,24,1152]{2,1,0:T(8,128)(2,1)S(1)}, u32[]{:S(2)}, u32[]{:S(2)}) async-start(bf16[16,24,1152]{2,1,0:T(8,128)(2,1)} %shard_map.55), calls=%async_computation | async-start | bytes 1769472 | tf_op jit(solution)/shard_map/all_to_all | solution.py:544
  61.5 0.0 copy-done.3
  61.5 0.2 copy.5
  61.8 20.9 %all-to-all-done = bf16[16,24,1152]{2,1,0:T(8,128)(2,1)S(1)} async-done(((bf16[16,24,1152]{2,1,0:T(8,128)(2,1)}), bf16[16,24,1152]{2,1,0:T(8,128)(2,1)S(1)}, u32[]{:S(2)}, u32[]{:S(2)}) %all-to-all-start) | async-done | bytes 884768 | tf_op jit(solution)/shard_map/all_to_all | solution.py:544
  82.7 0.0 copy-done.2
  82.7 1.4 %shard_map.56 = bf16[384,1152]{1,0:T(8,128)(2,1)S(1)} custom-call(bf16[384,384]{1,0:T(8,128)(2,1)S(1)} %bitcast.8, bf16[384,1152]{1,0:T(8,128)(2,1)S(1)} %bitcast.6, bf16[384,384]{1,0:T(8,128)(2,1)S(1)} %copy-done.2), custom_call_target="tpu_custom_call" | custom-call | flops 1 | bytes 1 | tf_op jit(solution)/shard_map/pallas_call | solution.py:463
  84.1 28.4 %all_to_all.10.parts = bf16[16,24,1152]{2,1,0:T(8,128)(2,1)S(1)} all-to-all(bf16[16,24,1152]{2,1,0:T(8,128)(2,1)S(1)} %bitcast.7), channel_id=1, replica_groups=mesh['space'=16,'band'=16] {'band'}, dimensions={0} | all-to-all | bytes 1769472 | tf_op jit(solution)/shard_map/all_to_all | solution.py:547
  112.5 1.7 %shard_map.57 = f32[24,4,4608]{2,1,0:T(4,128)} custom-call(bf16[16,24,1152]{2,1,0:T(8,128)(2,1)S(1)} %all_to_all.10.parts), custom_call_target="tpu_custom_call" | custom-call | flops 1 | bytes 1 | tf_op jit(solution)/shard_map/pallas_call | solution.py:489
Async XLA Ops:
  5.3 13.2 %copy-start = (f32[4,16,4608]{2,1,0:T(8,128)S(1)}, f32[4,16,4608]{2,1,0:T(8,128)}, u32[]{:S(2)}) copy-start(f32[4,16,4608]{2,1,0:T(8,128)} %get-tuple-element.24.own.refs_2_.refs_6_) | copy-start | bytes 3538948
  5.3 14.7 %collective-permute-start = (bf16[16,24192]{1,0:T(8,128)(2,1)S(1)}, bf16[16,24192]{1,0:T(8,128)(2,1)S(1)}, u32[]{:S(2)}, u32[]{:S(2)}) collective-permute-start(bf16[16,24192]{1,0:T(8,128)(2,1)S(1)} %get-tuple-element.21), channel_id=1, source_target_pairs={{0,16},{16,0},{32,48},{48,32},{64,80},{80,64},{96,112},{112,96},{1... | collective-permute-start | bytes 2322440 | tf_op jit(solution)/shard_map/ppermute | solution.py:511
  6.0 16.8 %collective-permute-start.2 = (bf16[16,24192]{1,0:T(8,128)(2,1)S(1)}, bf16[16,24192]{1,0:T(8,128)(2,1)S(1)}, u32[]{:S(2)}, u32[]{:S(2)}) collective-permute-start(bf16[16,24192]{1,0:T(8,128)(2,1)S(1)} %get-tuple-element.25), channel_id=1, source_target_pairs={{16,32},{48,64},{80,96},{112,128},{144,160},{176,192},{208,224},{3... | collective-permute-start | bytes 2322440 | tf_op jit(solution)/shard_map/ppermute | solution.py:510
  13.6 6.3 %collective-permute-start.1 = (bf16[16,11520]{1,0:T(8,128)(2,1)S(1)}, bf16[16,11520]{1,0:T(8,128)(2,1)S(1)}, u32[]{:S(2)}, u32[]{:S(2)}) collective-permute-start(bf16[16,11520]{1,0:T(8,128)(2,1)S(1)} %get-tuple-element.23), channel_id=1, source_target_pairs={{0,16},{16,0},{32,48},{48,32},{64,80},{80,64},{96,112},{112,96},{1... | collective-permute-start | bytes 1105928 | tf_op jit(solution)/shard_map/ppermute | solution.py:511
  13.6 18.3 %collective-permute-start.5 = (bf16[16,11520]{1,0:T(8,128)(2,1)S(1)}, bf16[16,11520]{1,0:T(8,128)(2,1)S(1)}, u32[]{:S(2)}, u32[]{:S(2)}) collective-permute-start(bf16[16,11520]{1,0:T(8,128)(2,1)S(1)} %get-tuple-element.33), channel_id=1, source_target_pairs={{16,32},{48,64},{80,96},{112,128},{144,160},{176,192},{208,224},{3... | collective-permute-start | bytes 1105928 | tf_op jit(solution)/shard_map/ppermute | solution.py:510
  20.0 11.3 %copy-start.1 = (f32[4,8,4608]{2,1,0:T(8,128)S(1)}, f32[4,8,4608]{2,1,0:T(8,128)}, u32[]{:S(2)}) copy-start(f32[4,8,4608]{2,1,0:T(8,128)} %get-tuple-element.32.own.refs_2_.refs_7_) | copy-start | bytes 1769476
  26.8 14.3 %collective-permute-start.3 = (bf16[16,23040]{1,0:T(8,128)(2,1)S(1)}, bf16[16,23040]{1,0:T(8,128)(2,1)S(1)}, u32[]{:S(2)}, u32[]{:S(2)}) collective-permute-start(bf16[16,23040]{1,0:T(8,128)(2,1)S(1)} %get-tuple-element.27), channel_id=1, source_target_pairs={{0,16},{16,0},{32,48},{48,32},{64,80},{80,64},{96,112},{112,96},{1... | collective-permute-start | bytes 2211848 | tf_op jit(solution)/shard_map/ppermute | solution.py:511
  26.9 16.4 %collective-permute-start.4 = (bf16[16,23040]{1,0:T(8,128)(2,1)S(1)}, bf16[16,23040]{1,0:T(8,128)(2,1)S(1)}, u32[]{:S(2)}, u32[]{:S(2)}) collective-permute-start(bf16[16,23040]{1,0:T(8,128)(2,1)S(1)} %get-tuple-element.29), channel_id=1, source_target_pairs={{16,32},{48,64},{80,96},{112,128},{144,160},{176,192},{208,224},{3... | collective-permute-start | bytes 2211848 | tf_op jit(solution)/shard_map/ppermute | solution.py:510
  34.0 14.5 %collective-permute-start.6 = (bf16[16,11520]{1,0:T(8,128)(2,1)S(1)}, bf16[16,11520]{1,0:T(8,128)(2,1)S(1)}, u32[]{:S(2)}, u32[]{:S(2)}) collective-permute-start(bf16[16,11520]{1,0:T(8,128)(2,1)S(1)} %get-tuple-element.34), channel_id=1, source_target_pairs={{0,16},{16,0},{32,48},{48,32},{64,80},{80,64},{96,112},{112,96},{1... | collective-permute-start | bytes 1105928 | tf_op jit(solution)/shard_map/ppermute | solution.py:511
  34.1 14.4 %collective-permute-start.7 = (bf16[16,11520]{1,0:T(8,128)(2,1)S(1)}, bf16[16,11520]{1,0:T(8,128)(2,1)S(1)}, u32[]{:S(2)}, u32[]{:S(2)}) collective-permute-start(bf16[16,11520]{1,0:T(8,128)(2,1)S(1)} %get-tuple-element.36), channel_id=1, source_target_pairs={{16,32},{48,64},{80,96},{112,128},{144,160},{176,192},{208,224},{3... | collective-permute-start | bytes 1105928 | tf_op jit(solution)/shard_map/ppermute | solution.py:510
  52.2 9.4 %copy-start.3 = (bf16[384,384]{1,0:T(8,128)(2,1)S(1)}, bf16[384,384]{1,0:T(8,128)(2,1)}, u32[]{:S(2)}) copy-start(bf16[384,384]{1,0:T(8,128)(2,1)} %param.6) | copy-start | bytes 884740
  52.2 30.5 %copy-start.2 = (bf16[384,384]{1,0:T(8,128)(2,1)S(1)}, bf16[384,384]{1,0:T(8,128)(2,1)}, u32[]{:S(2)}) copy-start(bf16[384,384]{1,0:T(8,128)(2,1)} %constant.23.clone.order) | copy-start | bytes 884740
  52.2 30.5 %all-to-all-start = ((bf16[16,24,1152]{2,1,0:T(8,128)(2,1)}), bf16[16,24,1152]{2,1,0:T(8,128)(2,1)S(1)}, u32[]{:S(2)}, u32[]{:S(2)}) async-start(bf16[16,24,1152]{2,1,0:T(8,128)(2,1)} %shard_map.55), calls=%async_computation | async-start | bytes 1769472 | tf_op jit(solution)/shard_map/all_to_all | solution.py:544

commit v8 on v7

--- a/solution.py
+++ b/solution.py
@@ -104,8 +104,9 @@
 
 
 def reordered(terms, order):
-    parts = [jnp.dot(terms[i], order[...], preferred_element_type=jnp.float32) for i in range(3)]
-    return parts[0] + (parts[1] + parts[2])
+    _, count, width = terms.shape
+    whole = jnp.dot(terms[...].reshape(3 * count, width), order[...], preferred_element_type=jnp.float32)
+    return whole[:count] + (whole[count : 2 * count] + whole[2 * count :])
 
 
 def potential_to_runs(cells, odd, order, out, to_mate, to_other, gathered, terms, quarters):

time: 115 us -> 114 us (level)
  no operation moved by 1% of the time
where the time goes in v8:
time: 114 us
  Pallas kernels  30.6 us (27%)
  starting transfers between devices  28.5 us (25%)
  blocking collectives  28.4 us (25%)
  waiting for transfers between devices  26 us (23%)
    all_to_all x1, blocking collectives, body(): back = lax.all_to_all(summed.reshape(members, count, width), 'band', 0, 0)  28.4 us
    all_to_all x1, waiting for transfers between devices, body(): gathered = lax.all_to_all(filtered, 'band', 0, 0)  20.9 us
    ppermute x4, starting transfers between devices, around(): other = lax.ppermute(to_other, 'space', others)  18.3 us
    pallas_call x4, Pallas kernels, two_steps(): pl.pallas_call(functools.partial(two_steps_kernel, last, extra, len(done)...  14.9 us
    all_to_all x1, starting transfers between devices, body(): gathered = lax.all_to_all(filtered, 'band', 0, 0)  9.35 us
    pallas_call x2, Pallas kernels, to_runs(): pl.pallas_call(functools.partial(to_runs_kernel, extra), grid=(count // R...  8.23 us
    ppermute x4, waiting for transfers between devices, around(): other = lax.ppermute(to_other, 'space', others)  5.13 us
    pallas_call x4, Pallas kernels, own_part(): pl.pallas_call(own_part_kernel, grid=(count // ROWS,), in_specs=[whole_sp...  4.25 us
  transfers between devices with their start and end apart: 9, of which 3 were waited for; matrix products, arithmetic and copies ran while one was open for 0% of the time, Pallas kernels for 16%

profile of v8, /device:TPU:25, one launch (start us, length us, event | category | flops | bytes accessed | tf_op | source)
XLA Modules:
  0.0 114.1 jit_solution(18029502410491501114)
XLA Ops:
  0.0 0.1 pad_add_fusion.place.refs_0_.refs_1_
  0.1 5.1 %shard_map.46 = (f32[4,16,4608]{2,1,0:T(8,128)}, bf16[16,24192]{1,0:T(8,128)(2,1)S(1)}, bf16[16,24192]{1,0:T(8,128)(2,1)S(1)}, f32[4,4608]{1,0:T(4,128)S(1)}) custom-call(s32[3]{0:T(128)S(1)} %pad_add_fusion.place.refs_0_.refs_1_, f32[24,4,4608]{2,1,0:T(4,128)} %cells.3, f32[4,4608]{1,0:T(4,128)} %rest_0_.1), custom_call_target="tpu_custom_call" | custom-call | flops 1 | bytes 1 | tf_op jit(solution)/shard_map/pallas_call | solution.py:195
  5.1 0.0 copy-start
  5.1 0.7 collective-permute-start
  5.8 4.3 %collective-permute-start.2 = (bf16[16,24192]{1,0:T(8,128)(2,1)S(1)}, bf16[16,24192]{1,0:T(8,128)(2,1)S(1)}, u32[]{:S(2)}, u32[]{:S(2)}) collective-permute-start(bf16[16,24192]{1,0:T(8,128)(2,1)S(1)} %get-tuple-element.25), channel_id=1, source_target_pairs={{16,32},{48,64},{80,96},{112,128},{144,160},{176,192},{208,224},{3... | collective-permute-start | bytes 2322440 | tf_op jit(solution)/shard_map/ppermute | solution.py:511
  10.1 3.2 %shard_map.47 = (f32[4,8,4608]{2,1,0:T(8,128)}, bf16[16,11520]{1,0:T(8,128)(2,1)S(1)}, bf16[16,11520]{1,0:T(8,128)(2,1)S(1)}) custom-call(s32[3]{0:T(128)S(1)} %pad_add_fusion.place.refs_0_.refs_1_, f32[24,4,4608]{2,1,0:T(4,128)} %cells.3), custom_call_target="tpu_custom_call" | custom-call | flops 1 | bytes 1 | tf_op jit(solution)/shard_map/pallas_call | solution.py:195
  13.3 0.0 collective-permute-start.1
  13.3 4.8 %collective-permute-start.5 = (bf16[16,11520]{1,0:T(8,128)(2,1)S(1)}, bf16[16,11520]{1,0:T(8,128)(2,1)S(1)}, u32[]{:S(2)}, u32[]{:S(2)}) collective-permute-start(bf16[16,11520]{1,0:T(8,128)(2,1)S(1)} %get-tuple-element.33), channel_id=1, source_target_pairs={{16,32},{48,64},{80,96},{112,128},{144,160},{176,192},{208,224},{3... | collective-permute-start | bytes 1105928 | tf_op jit(solution)/shard_map/ppermute | solution.py:511
  18.2 0.0 copy-done
  18.2 1.5 %shard_map.48.refs_5_ = f32[4,16,4608]{2,1,0:T(8,128)S(1)} custom-call(f32[4,4608]{1,0:T(4,128)S(1)} %get-tuple-element.26.potential.refs_4_, f32[4,16,4608]{2,1,0:T(8,128)S(1)} %copy-done), custom_call_target="tpu_custom_call" | custom-call | flops 1 | bytes 1 | tf_op jit(solution)/shard_map/pallas_call | solution.py:306
  19.7 0.0 copy-start.1
  19.7 0.0 collective-permute-done.1.refs_1_
  19.7 0.0 collective-permute-done.refs_1_.refs_6_
  19.7 2.9 %collective-permute-done.2.refs_3_.refs_7_ = bf16[16,24192]{1,0:T(8,128)(2,1)S(1)} collective-permute-done((bf16[16,24192]{1,0:T(8,128)(2,1)S(1)}, bf16[16,24192]{1,0:T(8,128)(2,1)S(1)}, u32[]{:S(2)}, u32[]{:S(2)}) %collective-permute-start.2) | collective-permute-done | bytes 774176 | tf_op jit(solution)/shard_map/ppermute | solution.py:511
  22.6 4.0 %shard_map.49 = (f32[4,16,4608]{2,1,0:T(8,128)S(1)}, bf16[16,23040]{1,0:T(8,128)(2,1)S(1)}, bf16[16,23040]{1,0:T(8,128)(2,1)S(1)}, f32[8,4608]{1,0:T(8,128)S(1)}) custom-call(s32[3]{0:T(128)S(1)} %pad_add_fusion.place.refs_0_.refs_1_, bf16[16,24192]{1,0:T(8,128)(2,1)S(1)} %collective-permute-done.refs_1_.refs_6_, f32[4,16,4608]{2,1,0:T(8,128)S(1)} %copy-done, ...), custom_call_target="tpu_custom_call" | custom-call | flops 1 | bytes 1 | tf_op jit(solution)/shard_map/pallas_call | solution.py:433
  26.6 0.1 collective-permute-start.3
  26.7 4.3 %collective-permute-start.4 = (bf16[16,23040]{1,0:T(8,128)(2,1)S(1)}, bf16[16,23040]{1,0:T(8,128)(2,1)S(1)}, u32[]{:S(2)}, u32[]{:S(2)}) collective-permute-start(bf16[16,23040]{1,0:T(8,128)(2,1)S(1)} %get-tuple-element.29), channel_id=1, source_target_pairs={{16,32},{48,64},{80,96},{112,128},{144,160},{176,192},{208,224},{3... | collective-permute-start | bytes 2211848 | tf_op jit(solution)/shard_map/ppermute | solution.py:511
  31.0 0.0 copy-done.1
  31.1 0.7 shard_map.52.refs_5_
  31.7 0.0 collective-permute-done.5.refs_3_
  31.7 2.1 %shard_map.53 = (f32[4,8,4608]{2,1,0:T(8,128)S(1)}, bf16[16,11520]{1,0:T(8,128)(2,1)S(1)}, bf16[16,11520]{1,0:T(8,128)(2,1)S(1)}) custom-call(s32[3]{0:T(128)S(1)} %pad_add_fusion.place.refs_0_.refs_1_, bf16[16,11520]{1,0:T(8,128)(2,1)S(1)} %collective-permute-done.1.refs_1_, f32[4,8,4608]{2,1,0:T(8,128)S(1)} %copy-done.1, ...), custom_call_target="tpu_custom_call" | custom-call | flops 1 | bytes 1 | tf_op jit(solution)/shard_map/pallas_call | solution.py:433
  33.8 0.1 collective-permute-start.6
  33.9 4.8 %collective-permute-start.7 = (bf16[16,11520]{1,0:T(8,128)(2,1)S(1)}, bf16[16,11520]{1,0:T(8,128)(2,1)S(1)}, u32[]{:S(2)}, u32[]{:S(2)}) collective-permute-start(bf16[16,11520]{1,0:T(8,128)(2,1)S(1)} %get-tuple-element.36), channel_id=1, source_target_pairs={{16,32},{48,64},{80,96},{112,128},{144,160},{176,192},{208,224},{3... | collective-permute-start | bytes 1105928 | tf_op jit(solution)/shard_map/ppermute | solution.py:511
  38.7 1.5 %shard_map.50.refs_5_ = f32[4,16,4608]{2,1,0:T(8,128)S(1)} custom-call(f32[4,4608]{1,0:T(4,128)S(1)} %get-tuple-element.26.potential.refs_4_, f32[4,16,4608]{2,1,0:T(8,128)S(1)} %get-tuple-element.28.own.refs_2_), custom_call_target="tpu_custom_call" | custom-call | flops 1 | bytes 1 | tf_op jit(solution)/shard_map/pallas_call | solution.py:306
  40.2 0.7 shard_map.54.refs_6_
  40.9 0.0 collective-permute-done.3.refs_1_
  40.9 2.2 %collective-permute-done.4.refs_3_ = bf16[16,23040]{1,0:T(8,128)(2,1)S(1)} collective-permute-done((bf16[16,23040]{1,0:T(8,128)(2,1)S(1)}, bf16[16,23040]{1,0:T(8,128)(2,1)S(1)}, u32[]{:S(2)}, u32[]{:S(2)}) %collective-permute-start.4) | collective-permute-done | bytes 737312 | tf_op jit(solution)/shard_map/ppermute | solution.py:511
  43.1 5.2 %shard_map.51.refs_0_ = bf16[16,16,1152]{2,1,0:T(8,128)(2,1)S(1)} custom-call(s32[3]{0:T(128)S(1)} %pad_add_fusion.place.refs_0_.refs_1_, bf16[16,23040]{1,0:T(8,128)(2,1)S(1)} %collective-permute-done.3.refs_1_, f32[4,16,4608]{2,1,0:T(8,128)S(1)} %get-tuple-element.28.own.refs_2_, bf16[16,23040]{1,0:T(8,128)(2,1)S(1)} %collective-permute-done.4.refs_3_, ...), custom_call_target="tpu_custom_call" | custom-call | flops 1 | bytes 1 | tf_op jit(solution)/shard_map/pallas_call | solution.py:433
  48.3 0.0 collective-permute-done.6.refs_2_
  48.3 0.0 collective-permute-done.7.refs_4_
  48.3 3.7 %shard_map.55 = bf16[16,24,1152]{2,1,0:T(8,128)(2,1)} custom-call(bf16[16,16,1152]{2,1,0:T(8,128)(2,1)S(1)} %shard_map.51.refs_0_, s32[3]{0:T(128)S(1)} %pad_add_fusion.place.refs_0_.refs_1_, bf16[16,11520]{1,0:T(8,128)(2,1)S(1)} %collective-permute-done.6.refs_2_, f32[4,8,4608]{2,1,0:T(8,128)S(1)} %get-tuple-element.35.own.refs_3_, ...), custom_call_target="tpu_custom_call" | custom-call | flops 1 | bytes 1 | tf_op jit(solution)/shard_map/pallas_call | solution.py:433
  52.0 0.0 copy-start.3
  52.0 0.0 copy-start.2
  52.0 9.4 %all-to-all-start = ((bf16[16,24,1152]{2,1,0:T(8,128)(2,1)}), bf16[16,24,1152]{2,1,0:T(8,128)(2,1)S(1)}, u32[]{:S(2)}, u32[]{:S(2)}) async-start(bf16[16,24,1152]{2,1,0:T(8,128)(2,1)} %shard_map.55), calls=%async_computation | async-start | bytes 1769472 | tf_op jit(solution)/shard_map/all_to_all | solution.py:545
  61.4 0.0 copy-done.3
  61.4 0.2 copy.5
  61.6 20.9 %all-to-all-done = bf16[16,24,1152]{2,1,0:T(8,128)(2,1)S(1)} async-done(((bf16[16,24,1152]{2,1,0:T(8,128)(2,1)}), bf16[16,24,1152]{2,1,0:T(8,128)(2,1)S(1)}, u32[]{:S(2)}, u32[]{:S(2)}) %all-to-all-start) | async-done | bytes 884768 | tf_op jit(solution)/shard_map/all_to_all | solution.py:545
  82.5 0.0 copy-done.2
  82.5 1.4 %shard_map.56 = bf16[384,1152]{1,0:T(8,128)(2,1)S(1)} custom-call(bf16[384,384]{1,0:T(8,128)(2,1)S(1)} %bitcast.8, bf16[384,1152]{1,0:T(8,128)(2,1)S(1)} %bitcast.6, bf16[384,384]{1,0:T(8,128)(2,1)S(1)} %copy-done.2), custom_call_target="tpu_custom_call" | custom-call | flops 1 | bytes 1 | tf_op jit(solution)/shard_map/pallas_call | solution.py:464
  83.9 28.4 %all_to_all.10.parts = bf16[16,24,1152]{2,1,0:T(8,128)(2,1)S(1)} all-to-all(bf16[16,24,1152]{2,1,0:T(8,128)(2,1)S(1)} %bitcast.7), channel_id=1, replica_groups=mesh['space'=16,'band'=16] {'band'}, dimensions={0} | all-to-all | bytes 1769472 | tf_op jit(solution)/shard_map/all_to_all | solution.py:548
  112.3 1.7 %shard_map.57 = f32[24,4,4608]{2,1,0:T(4,128)} custom-call(bf16[16,24,1152]{2,1,0:T(8,128)(2,1)S(1)} %all_to_all.10.parts), custom_call_target="tpu_custom_call" | custom-call | flops 1 | bytes 1 | tf_op jit(solution)/shard_map/pallas_call | solution.py:490
Async XLA Ops:
  5.1 13.0 %copy-start = (f32[4,16,4608]{2,1,0:T(8,128)S(1)}, f32[4,16,4608]{2,1,0:T(8,128)}, u32[]{:S(2)}) copy-start(f32[4,16,4608]{2,1,0:T(8,128)} %get-tuple-element.24.own.refs_2_.refs_6_) | copy-start | bytes 3538948
  5.1 14.5 %collective-permute-start = (bf16[16,24192]{1,0:T(8,128)(2,1)S(1)}, bf16[16,24192]{1,0:T(8,128)(2,1)S(1)}, u32[]{:S(2)}, u32[]{:S(2)}) collective-permute-start(bf16[16,24192]{1,0:T(8,128)(2,1)S(1)} %get-tuple-element.21), channel_id=1, source_target_pairs={{0,16},{16,0},{32,48},{48,32},{64,80},{80,64},{96,112},{112,96},{1... | collective-permute-start | bytes 2322440 | tf_op jit(solution)/shard_map/ppermute | solution.py:512
  5.8 16.8 %collective-permute-start.2 = (bf16[16,24192]{1,0:T(8,128)(2,1)S(1)}, bf16[16,24192]{1,0:T(8,128)(2,1)S(1)}, u32[]{:S(2)}, u32[]{:S(2)}) collective-permute-start(bf16[16,24192]{1,0:T(8,128)(2,1)S(1)} %get-tuple-element.25), channel_id=1, source_target_pairs={{16,32},{48,64},{80,96},{112,128},{144,160},{176,192},{208,224},{3... | collective-permute-start | bytes 2322440 | tf_op jit(solution)/shard_map/ppermute | solution.py:511
  13.3 6.3 %collective-permute-start.1 = (bf16[16,11520]{1,0:T(8,128)(2,1)S(1)}, bf16[16,11520]{1,0:T(8,128)(2,1)S(1)}, u32[]{:S(2)}, u32[]{:S(2)}) collective-permute-start(bf16[16,11520]{1,0:T(8,128)(2,1)S(1)} %get-tuple-element.23), channel_id=1, source_target_pairs={{0,16},{16,0},{32,48},{48,32},{64,80},{80,64},{96,112},{112,96},{1... | collective-permute-start | bytes 1105928 | tf_op jit(solution)/shard_map/ppermute | solution.py:512
  13.3 18.4 %collective-permute-start.5 = (bf16[16,11520]{1,0:T(8,128)(2,1)S(1)}, bf16[16,11520]{1,0:T(8,128)(2,1)S(1)}, u32[]{:S(2)}, u32[]{:S(2)}) collective-permute-start(bf16[16,11520]{1,0:T(8,128)(2,1)S(1)} %get-tuple-element.33), channel_id=1, source_target_pairs={{16,32},{48,64},{80,96},{112,128},{144,160},{176,192},{208,224},{3... | collective-permute-start | bytes 1105928 | tf_op jit(solution)/shard_map/ppermute | solution.py:511
  19.7 11.4 %copy-start.1 = (f32[4,8,4608]{2,1,0:T(8,128)S(1)}, f32[4,8,4608]{2,1,0:T(8,128)}, u32[]{:S(2)}) copy-start(f32[4,8,4608]{2,1,0:T(8,128)} %get-tuple-element.32.own.refs_2_.refs_7_) | copy-start | bytes 1769476
  26.6 14.3 %collective-permute-start.3 = (bf16[16,23040]{1,0:T(8,128)(2,1)S(1)}, bf16[16,23040]{1,0:T(8,128)(2,1)S(1)}, u32[]{:S(2)}, u32[]{:S(2)}) collective-permute-start(bf16[16,23040]{1,0:T(8,128)(2,1)S(1)} %get-tuple-element.27), channel_id=1, source_target_pairs={{0,16},{16,0},{32,48},{48,32},{64,80},{80,64},{96,112},{112,96},{1... | collective-permute-start | bytes 2211848 | tf_op jit(solution)/shard_map/ppermute | solution.py:512
  26.7 16.4 %collective-permute-start.4 = (bf16[16,23040]{1,0:T(8,128)(2,1)S(1)}, bf16[16,23040]{1,0:T(8,128)(2,1)S(1)}, u32[]{:S(2)}, u32[]{:S(2)}) collective-permute-start(bf16[16,23040]{1,0:T(8,128)(2,1)S(1)} %get-tuple-element.29), channel_id=1, source_target_pairs={{16,32},{48,64},{80,96},{112,128},{144,160},{176,192},{208,224},{3... | collective-permute-start | bytes 2211848 | tf_op jit(solution)/shard_map/ppermute | solution.py:511
  33.8 14.5 %collective-permute-start.6 = (bf16[16,11520]{1,0:T(8,128)(2,1)S(1)}, bf16[16,11520]{1,0:T(8,128)(2,1)S(1)}, u32[]{:S(2)}, u32[]{:S(2)}) collective-permute-start(bf16[16,11520]{1,0:T(8,128)(2,1)S(1)} %get-tuple-element.34), channel_id=1, source_target_pairs={{0,16},{16,0},{32,48},{48,32},{64,80},{80,64},{96,112},{112,96},{1... | collective-permute-start | bytes 1105928 | tf_op jit(solution)/shard_map/ppermute | solution.py:512
  33.9 14.4 %collective-permute-start.7 = (bf16[16,11520]{1,0:T(8,128)(2,1)S(1)}, bf16[16,11520]{1,0:T(8,128)(2,1)S(1)}, u32[]{:S(2)}, u32[]{:S(2)}) collective-permute-start(bf16[16,11520]{1,0:T(8,128)(2,1)S(1)} %get-tuple-element.36), channel_id=1, source_target_pairs={{16,32},{48,64},{80,96},{112,128},{144,160},{176,192},{208,224},{3... | collective-permute-start | bytes 1105928 | tf_op jit(solution)/shard_map/ppermute | solution.py:511
  52.0 9.4 %copy-start.3 = (bf16[384,384]{1,0:T(8,128)(2,1)S(1)}, bf16[384,384]{1,0:T(8,128)(2,1)}, u32[]{:S(2)}) copy-start(bf16[384,384]{1,0:T(8,128)(2,1)} %param.6) | copy-start | bytes 884740
  52.0 30.5 %copy-start.2 = (bf16[384,384]{1,0:T(8,128)(2,1)S(1)}, bf16[384,384]{1,0:T(8,128)(2,1)}, u32[]{:S(2)}) copy-start(bf16[384,384]{1,0:T(8,128)(2,1)} %constant.23.clone.order) | copy-start | bytes 884740
  52.0 30.5 %all-to-all-start = ((bf16[16,24,1152]{2,1,0:T(8,128)(2,1)}), bf16[16,24,1152]{2,1,0:T(8,128)(2,1)S(1)}, u32[]{:S(2)}, u32[]{:S(2)}) async-start(bf16[16,24,1152]{2,1,0:T(8,128)(2,1)} %shard_map.55), calls=%async_computation | async-start | bytes 1769472 | tf_op jit(solution)/shard_map/all_to_all | solution.py:545
